TPU v7x, 32 devices: a whole 2x2x4 slice. The times are simulated.
32 devices in a mesh: grp: 2 (over y), band: 4 (over z), tm: 2 (over x), chan: 2 (over core).
Axes of the slice: x: 2, y: 2, z: 4, core: 2. Of those that a mesh axis runs over, the one named last changes fastest.
Arguments:
- tdi_data: float32 [4, 512, 128, 128], P(('grp', 'chan'), 'band', 'tm'), parts along dimension 0, may hold values from -6 to 6
- noise_diag: float32 [4, 512, 128, 128], P(('grp', 'chan'), 'band', 'tm'), parts along dimension 0, may hold values from 0.17 to 11.3
- noise_off: float32 [4, 512, 128, 128], P(('grp', 'chan'), 'band', 'tm'), parts along dimension 0, may hold values from -2.6 to 2.6
- src_blocks: bfloat16 [16384, 2, 128], P(('grp', 'band', 'tm'), 'chan'), parts along dimension 0, may hold values from -3 to 3
- owner_dev: int32 [16384, 1], P(('grp', 'band', 'tm')), parts along dimension 0, may hold values from 0 to 7; in each aligned block of 1024 rows (0 to 1023, 1024 to 2047, ...) at most 256 rows name the same one
- layer_in: int32 [16384], P(('grp', 'band', 'tm')), parts along dimension 0, may hold values from 0 to 127
- seg_in: int32 [16384], P(('grp', 'band', 'tm')), parts along dimension 0, may hold values from 0 to 63
Outputs:
- weighted: float32 [4, 512, 128, 128], P(('grp', 'chan'), 'band', 'tm'), parts along dimension 0
- log_like: float32 [2], P('grp'), parts along dimension 0
- grad_blocks: bfloat16 [16384, 2, 128], P(('grp', 'band', 'tm'), 'chan'), parts along dimension 0
There are 2 independent parts, one for each index of `grp`. A program takes and returns all parts, laid end to end along the dimension named above; each array names one. Nothing has to cross between parts.
Inputs may be any that keep to these rules, and one draw needn't show every extreme that they name: `owner_dev`: of the 1024 rows of one device (aligned blocks of 1024 rows), at most 256 name the same owner, and in every draw some owner is named by exactly 256 rows of one device.
All inputs are finite; a program needn't handle non-finite values.
Results may differ from a plain program's by a relative error of at most 0.0004.
Values may be sent and summed in bfloat16 or wider, within the bound.
No kernel may reach another device: no remote copies, remote signals or barrier semaphores. Data moves between devices by JAX's collectives and lax.ppermute only.
A program may use at most 64 MiB of HBM per device.

v0:
```python
import jax
import jax.numpy as jnp
from jax import lax
from jax.sharding import PartitionSpec as P

C = 2
NF = 512
NT = 16384


def passed_along(value, axis, steps):
    count = lax.axis_size(axis)
    leading, last = (max(0, -steps), min(count, count - steps))
    return lax.ppermute(value, axis, [(source, source + steps) for source in range(leading, last)])


def shards(tdi_data, noise_diag, noise_off, src_blocks, owner_dev, layer_in, seg_in):
    band_count = lax.axis_size("band")
    time_count = lax.axis_size("tm")
    groups = band_count * time_count
    layers_dev = tdi_data.shape[1]
    segs_dev = tdi_data.shape[2]
    bins_dev = tdi_data.shape[3]
    src_count = src_blocks.shape[0]
    slots_per = 2 * src_count // groups
    target = owner_dev[:, 0]
    chosen_rows = (target[:, None] == jnp.arange(groups, dtype=jnp.int32)[None, :]).astype(
        jnp.int32
    )
    slot_rank = jnp.sum((jnp.cumsum(chosen_rows, axis=0) - chosen_rows) * chosen_rows, axis=1)
    position = target * slots_per + slot_rank
    cell_ids = layer_in * segs_dev + seg_in
    outgoing = (
        jnp.zeros((groups * slots_per, bins_dev), jnp.bfloat16)
        .at[position]
        .set(src_blocks[:, 0, :])
    )
    addresses = jnp.zeros((groups * slots_per,), jnp.int32).at[position].set(cell_ids)
    arrived, home_cells = (
        lax.all_to_all(outgoing, ("band", "tm"), split_axis=0, concat_axis=0, tiled=True),
        lax.all_to_all(addresses, ("band", "tm"), split_axis=0, concat_axis=0, tiled=True),
    )
    model_plane = jax.ops.segment_sum(
        arrived.astype(jnp.float32), home_cells, num_segments=layers_dev * segs_dev
    )
    model_plane = model_plane.reshape(1, layers_dev, segs_dev, bins_dev)
    residual = tdi_data - model_plane
    product = noise_off * residual
    lower_rim = passed_along(product[:, -1:], "band", 1)
    upper_rim = passed_along(residual[:, :1], "band", -1)
    upper_full = jnp.concatenate([residual[:, 1:], upper_rim], axis=1)
    lower_full = jnp.concatenate([lower_rim, product[:, :-1]], axis=1)
    weighted = noise_diag * residual + noise_off * upper_full + lower_full
    partial_sum = jnp.sum(residual * weighted)
    summed = lax.psum(partial_sum, ("band", "tm", "chan"))
    log_like = jnp.reshape(-0.5 * summed / (C * NF * NT), (1,))
    flat_plane = weighted.reshape(layers_dev * segs_dev, bins_dev)
    picked = jnp.take(flat_plane, home_cells, axis=0).astype(jnp.bfloat16)
    returned = lax.all_to_all(picked, ("band", "tm"), split_axis=0, concat_axis=0, tiled=True)
    grad_blocks = jnp.take(returned, position, axis=0).reshape(src_count, 1, bins_dev)
    return (weighted, log_like, grad_blocks)


def solution(mesh):
    return jax.shard_map(
        shards,
        mesh=mesh,
        in_specs=(
            P(("grp", "chan"), "band", "tm", None),
            P(("grp", "chan"), "band", "tm", None),
            P(("grp", "chan"), "band", "tm", None),
            P(("grp", "band", "tm"), "chan", None),
            P(("grp", "band", "tm"), None),
            P(("grp", "band", "tm")),
            P(("grp", "band", "tm")),
        ),
        out_specs=(
            P(("grp", "chan"), "band", "tm", None),
            P("grp"),
            P(("grp", "band", "tm"), "chan", None),
        ),
        check_vma=False,
    )
```

profile of v0, /device:TPU:0, one launch (start us, length us, event | category | flops | bytes accessed | tf_op | source)
XLA Modules:
  0.0 131.0 jit_solution(8228546647147961063)
XLA Ops:
  0.6 0.0 copy-start
  0.6 0.7 fusion.11
  1.4 2.3 %reduce-window.6 = s32[8,8,128]{2,1,0:T(8,128)S(1)} reduce-window(s32[8,8,128]{2,1,0:T(8,128)S(1)} %fusion.11, s32[]{:T(128)} %constant.25.clone.1), window={size=1x1x128 pad=0_0x0_0x127_0}, to_apply=%region_0.0 | reduce-window | flops 1040384 | bytes 65540 | tf_op jit(solution)/shard_map/reduce-window
  3.6 0.3 slice_reduce_fusion
  3.9 0.2 reduce-window.9
  4.1 0.1 add_bitcast_fusion
  4.2 0.7 fusion.10
  4.9 0.7 and_reduce_fusion
  5.6 0.7 multiply_add_fusion
  6.3 4.9 %scatter_custom_fusion = s32[2048]{0:T(1024)} fusion(s32[1024]{0:T(1024)S(1)} %bitcast.56, s32[1024]{0:T(1024)S(1)} %multiply_add_fusion, s32[]{:T(128)} %constant.25.clone.1), kind=kCustom, calls=%fused_computation.33 | custom fusion | bytes 8196 | tf_op jit(solution)/shard_map/scatter | solution.py:38
  11.2 7.3 %all-to-all-start = ((s32[8,256,1]{1,2,0:T(1,128)}), s32[8,256,1]{1,2,0:T(1,128)S(1)}, u32[]{:S(2)}, u32[]{:S(2)}) async-start(s32[8,256,1]{1,2,0:T(1,128)} %bitcast.5), calls=%async_computation | async-start | bytes 16384 | tf_op jit(solution)/shard_map/all_to_all | solution.py:41
  18.4 0.0 copy-done
  18.4 4.0 %scatter_custom_fusion.1 = bf16[2048,128]{1,0:T(8,128)(2,1)} fusion(s32[1024]{0:T(1024)S(1)} %bitcast.57, bf16[1024,1,128]{2,0,1:T(8,128)(2,1)S(1)} %copy-done, bf16[]{:T(256)} %constant.29.clone.1), kind=kCustom, calls=%fused_computation.14 | custom fusion | bytes 786434 | tf_op jit(solution)/shard_map/scatter | solution.py:36
  22.4 2.5 %all-to-all-done = s32[8,256,1]{1,2,0:T(1,128)S(1)} async-done(((s32[8,256,1]{1,2,0:T(1,128)}), s32[8,256,1]{1,2,0:T(1,128)S(1)}, u32[]{:S(2)}, u32[]{:S(2)}) %all-to-all-start) | async-done | bytes 8224 | tf_op jit(solution)/shard_map/all_to_all | solution.py:41
  25.0 3.5 %all-to-all-start.1 = ((bf16[8,256,128]{2,1,0:T(8,128)(2,1)}), bf16[8,256,128]{2,1,0:T(8,128)(2,1)S(1)}, u32[]{:S(2)}, u32[]{:S(2)}) async-start(bf16[8,256,128]{2,1,0:T(8,128)(2,1)} %bitcast.8), calls=%async_computation.1 | async-start | bytes 1048576 | tf_op jit(solution)/shard_map/all_to_all | solution.py:40
  28.5 13.9 %all-to-all-done.1 = bf16[8,256,128]{2,1,0:T(8,128)(2,1)S(1)} async-done(((bf16[8,256,128]{2,1,0:T(8,128)(2,1)}), bf16[8,256,128]{2,1,0:T(8,128)(2,1)S(1)}, u32[]{:S(2)}, u32[]{:S(2)}) %all-to-all-start.1) | async-done | bytes 524320 | tf_op jit(solution)/shard_map/all_to_all | solution.py:40
  42.4 14.4 %scatter_custom_fusion.2 = f32[8192,128]{1,0:T(8,128)} fusion(s32[2048]{0:T(1024)S(1)} %bitcast.50, f32[]{:T(128)} %constant.18.clone.1, bf16[2048,128]{1,0:T(8,128)(2,1)S(1)} %bitcast.47), kind=kCustom, calls=%fused_computation.9 | custom fusion | flops 524288 | bytes 4718596 | tf_op jit(solution)/shard_map/scatter-add | solution.py:43
  56.7 6.1 %fusion.15 = (f32[1,128,64,128]{3,2,1,0:T(8,128)S(1)}, f32[1,128,64,128]{3,2,1,0:T(8,128)S(1)}) fusion(f32[1,128,64,128]{3,2,1,0:T(8,128)} %param.9, f32[1,128,64,128]{3,2,1,0:T(8,128)} %param.7, f32[1,128,64,128]{3,2,1,0:T(8,128)} %bitcast.44), kind=kLoop, calls=%fused_computation.36 | loop fusion | flops 2097152 | bytes 20971520 | tf_op jit(solution)/shard_map/mul | solution.py:48
  62.9 1.3 collective-permute-start
  64.2 5.1 %collective-permute-start.1 = (f32[1,1,64,128]{3,2,1,0:T(8,128)S(1)}, f32[1,1,64,128]{3,2,1,0:T(8,128)S(1)}, u32[]{:S(2)}, u32[]{:S(2)}) collective-permute-start(f32[1,1,64,128]{3,2,1,0:T(8,128)S(1)} %slice.31), channel_id=1, source_target_pairs={{0,4},{4,8},{8,12},{1,5},{5,9},{9,13},{2,6},{6,10},{10,14},{3,7},{... | collective-permute-start | bytes 98312 | tf_op jit(solution)/shard_map/ppermute | solution.py:14
  69.4 0.0 copy-start.2
  69.4 0.3 slice.29
  69.7 0.0 copy-start.1
  69.7 0.3 slice.32
  70.0 0.0 collective-permute-done
  70.0 0.9 collective-permute-done.1
  70.9 0.6 copy-done.2
  71.5 1.4 %copy-done.1 = f32[1,128,64,128]{3,2,1,0:T(8,128)S(1)} copy-done((f32[1,128,64,128]{3,2,1,0:T(8,128)S(1)}, f32[1,128,64,128]{3,2,1,0:T(8,128)}, u32[]{:S(2)}) %copy-start.1) | copy-done | bytes 4194328
  72.9 4.9 %multiply_reduce_fusion = (f32[]{:T(128)}, f32[1,128,64,128]{3,2,1,0:T(8,128)}) fusion(f32[1,128,64,128]{3,2,1,0:T(8,128)S(1)} %get-tuple-element.8, f32[1,127,64,128]{3,2,1,0:T(8,128)S(1)} %slice.32, f32[1,1,64,128]{3,2,1,0:T(8,128)S(1)} %collective-permute-done.1, f32[1,128,64,128]{3,2,1,0:T(8,128)S(1)} %copy-done.1, ...), kind=kLoop, calls=%fused_computation.8 | loop fusion | flops 8388607 | bytes 25165828 | tf_op jit(solution)/shard_map/reduce_sum | solution.py:54
  77.8 7.8 %gather_fusion = bf16[2048,128]{1,0:T(8,128)(2,1)S(1)} fusion(f32[8192,128]{1,0:T(8,128)} %bitcast.45, s32[2048]{0:T(1024)S(1)} %broadcast_clamp_fusion), kind=kCustom, calls=%fused_computation | custom fusion | bytes 1056768 | tf_op jit(solution)/shard_map/jit(_take)/gather | solution.py:58
  85.6 1.1 select_convert_fusion
  86.8 3.5 %all-to-all-start.2 = ((bf16[8,256,128]{2,1,0:T(8,128)(2,1)}), bf16[8,256,128]{2,1,0:T(8,128)(2,1)S(1)}, u32[]{:S(2)}, u32[]{:S(2)}) async-start(bf16[8,256,128]{2,1,0:T(8,128)(2,1)} %select_convert_fusion), calls=%async_computation.2 | async-start | bytes 1048576 | tf_op jit(solution)/shard_map/all_to_all | solution.py:59
  90.3 34.9 %psum.7 = f32[]{:T(128)} all-reduce(f32[]{:T(128)} %get-tuple-element.5), channel_id=1, replica_groups=mesh['grp'=2,'band'=4,'tm'=2,'chan'=2] {'band','tm','chan'}, use_global_device_ids=true, to_apply=%region_7.8 | all-reduce | flops 1 | bytes 8 | tf_op jit(solution)/shard_map/psum | solution.py:55
  125.8 0.0 all-to-all-done.2
  125.8 3.2 %gather_fusion.1 = bf16[1024,128]{1,0:T(8,128)(2,1)S(1)} fusion(bf16[2048,128]{1,0:T(8,128)(2,1)S(1)} %bitcast.46, s32[1024]{0:T(1024)S(1)} %broadcast_clamp_fusion.1), kind=kCustom, calls=%fused_computation.1 | custom fusion | bytes 528384 | tf_op jit(solution)/shard_map/jit(_take)/gather | solution.py:60
  129.0 0.9 bitcast_select_fusion
  (6 shorter events, 0.0 us)
Async XLA Ops:
  0.6 17.8 %copy-start = (bf16[1024,1,128]{2,0,1:T(8,128)(2,1)S(1)}, bf16[1024,1,128]{2,0,1:T(8,128)(2,1)}, u32[]{:S(2)}) copy-start(bf16[1024,1,128]{2,0,1:T(8,128)(2,1)} %param.10) | copy-start | bytes 786436
  11.2 13.8 %all-to-all-start = ((s32[8,256,1]{1,2,0:T(1,128)}), s32[8,256,1]{1,2,0:T(1,128)S(1)}, u32[]{:S(2)}, u32[]{:S(2)}) async-start(s32[8,256,1]{1,2,0:T(1,128)} %bitcast.5), calls=%async_computation | async-start | bytes 16384 | tf_op jit(solution)/shard_map/all_to_all | solution.py:41
  25.0 17.4 %all-to-all-start.1 = ((bf16[8,256,128]{2,1,0:T(8,128)(2,1)}), bf16[8,256,128]{2,1,0:T(8,128)(2,1)S(1)}, u32[]{:S(2)}, u32[]{:S(2)}) async-start(bf16[8,256,128]{2,1,0:T(8,128)(2,1)} %bitcast.8), calls=%async_computation.1 | async-start | bytes 1048576 | tf_op jit(solution)/shard_map/all_to_all | solution.py:40
  62.9 7.1 %collective-permute-start = (f32[1,1,64,128]{3,2,1,0:T(8,128)S(1)}, f32[1,1,64,128]{3,2,1,0:T(8,128)S(1)}, u32[]{:S(2)}, u32[]{:S(2)}) collective-permute-start(f32[1,1,64,128]{3,2,1,0:T(8,128)S(1)} %slice.30), channel_id=1, source_target_pairs={{4,0},{8,4},{12,8},{5,1},{9,5},{13,9},{6,2},{10,6},{14,10},{7,3},{... | collective-permute-start | bytes 98312 | tf_op jit(solution)/shard_map/ppermute | solution.py:14
  64.2 6.7 %collective-permute-start.1 = (f32[1,1,64,128]{3,2,1,0:T(8,128)S(1)}, f32[1,1,64,128]{3,2,1,0:T(8,128)S(1)}, u32[]{:S(2)}, u32[]{:S(2)}) collective-permute-start(f32[1,1,64,128]{3,2,1,0:T(8,128)S(1)} %slice.31), channel_id=1, source_target_pairs={{0,4},{4,8},{8,12},{1,5},{5,9},{9,13},{2,6},{6,10},{10,14},{3,7},{... | collective-permute-start | bytes 98312 | tf_op jit(solution)/shard_map/ppermute | solution.py:14
  69.4 2.2 %copy-start.2 = (f32[1,128,64,128]{3,2,1,0:T(8,128)S(1)}, f32[1,128,64,128]{3,2,1,0:T(8,128)}, u32[]{:S(2)}) copy-start(f32[1,128,64,128]{3,2,1,0:T(8,128)} %param.8) | copy-start | bytes 12582916
  69.7 3.2 %copy-start.1 = (f32[1,128,64,128]{3,2,1,0:T(8,128)S(1)}, f32[1,128,64,128]{3,2,1,0:T(8,128)}, u32[]{:S(2)}) copy-start(f32[1,128,64,128]{3,2,1,0:T(8,128)} %param.9) | copy-start | bytes 12582916
  86.8 39.0 %all-to-all-start.2 = ((bf16[8,256,128]{2,1,0:T(8,128)(2,1)}), bf16[8,256,128]{2,1,0:T(8,128)(2,1)S(1)}, u32[]{:S(2)}, u32[]{:S(2)}) async-start(bf16[8,256,128]{2,1,0:T(8,128)(2,1)} %select_convert_fusion), calls=%async_computation.2 | async-start | bytes 1048576 | tf_op jit(solution)/shard_map/all_to_all | solution.py:59
where the time goes:
time: 132 us; the launch traced here: 131 us
  blocking collectives  34.9 us (26%)
  other arithmetic  32.9 us (25%)
  local copies, waits for them, and re-layouts  22.7 us (17%)
  starting transfers between devices  20.7 us (16%)
  waiting for transfers between devices  17.3 us (13%)
  between operations  2.58 us (2%)
    psum x1, blocking collectives, shards(): summed = lax.psum(partial_sum, ('band', 'tm', 'chan'))  34.9 us
    scatter-add x1, other arithmetic, shards(): jax.ops.segment_sum(arrived.astype(jnp.float32), home_cells, num_segments...  14.4 us
    all_to_all x1, waiting for transfers between devices, shards(): lax.all_to_all(outgoing, ('band', 'tm'), split_axis=0, concat_axis=0, til...  13.9 us
    gather x1, local copies, waits for them, and re-layouts, shards(): picked = jnp.take(flat_plane, home_cells, axis=0).astype(jnp.bfloat16)  7.77 us
    all_to_all x1, starting transfers between devices, shards(): lax.all_to_all(addresses, ('band', 'tm'), split_axis=0, concat_axis=0, ti...  7.25 us
    ppermute x2, starting transfers between devices, passed_along(): lax.ppermute(value, axis, [(source, source + steps) for source in range(l...  6.42 us
    mul x1, other arithmetic, shards(): product = noise_off * residual  6.14 us
    reduce_sum x1, other arithmetic, shards(): partial_sum = jnp.sum(residual * weighted)  4.93 us
  transfers between devices with their start and end apart: 5, of which 3 were waited for; matrix products, arithmetic and copies ran while one was open for 4% of the time, Pallas kernels for 0%

commit v1 on v0

v1 whole, which is shorter than its diff:
```python
import functools

import jax
import jax.numpy as jnp
from jax import lax
from jax.experimental import pallas as pl
from jax.experimental.pallas import tpu as pltpu
from jax.sharding import PartitionSpec as P

LANES = 128
TAIL = 16
VMEM = pl.BlockSpec(memory_space=pltpu.VMEM)
HBM = pl.BlockSpec(memory_space=pltpu.HBM)
SMEM = pl.BlockSpec(memory_space=pltpu.SMEM)
F32 = jnp.float32
BF16 = jnp.bfloat16
I32 = jnp.int32


def passed_along(value, axis, steps):
    count = lax.axis_size(axis)
    leading, last = (max(0, -steps), min(count, count - steps))
    return lax.ppermute(value, axis, [(source, source + steps) for source in range(leading, last)])


def all_sum(value, axes):
    for axis in axes:
        count, step = lax.axis_size(axis), 1
        while step < count:
            value = value + lax.ppermute(value, axis, [(i, i ^ step) for i in range(count)])
            step *= 2
    return value


def halves_of(slots):
    return max(1, slots // LANES)


def pack_kernel(
    groups, slots, own_hbm, layer_hbm, seg_hbm, src_hbm, out_ref, pos_ref,
    own_ref, layer_ref, seg_ref, src_ref, sems,
):
    copies = [
        pltpu.make_async_copy(source, target, sems.at[i])
        for i, (source, target) in enumerate(
            ((own_hbm, own_ref), (layer_hbm, layer_ref), (seg_hbm, seg_ref), (src_hbm, src_ref))
        )
    ]
    for copy in copies:
        copy.start()
    copies[0].wait()
    count = own_ref.shape[1]
    own = own_ref[...]
    rows = max(16, groups)
    owned = (lax.broadcasted_iota(I32, (rows, count), 0) == own).astype(F32)
    width = min(count, 256)
    before = (
        lax.broadcasted_iota(I32, (width, width), 0) < lax.broadcasted_iota(I32, (width, width), 1)
    ).astype(F32).astype(BF16)
    carry = jnp.zeros((rows, 1), F32)
    ranks = []
    for start in range(0, count, width):
        part = owned[:, start : start + width]
        earlier = jnp.dot(part.astype(BF16), before, preferred_element_type=F32) + carry
        ranks.append(jnp.sum(part * earlier, axis=0, keepdims=True))
        carry = carry + jnp.sum(part, axis=1, keepdims=True)
    rank = jnp.concatenate(ranks, axis=1).astype(I32)
    pos_ref[...] = own * slots + rank
    tall = max(slots, LANES)
    for copy in copies[1:]:
        copy.wait()
    even = lax.broadcasted_iota(I32, (TAIL, count), 0) % 2 == 0
    names = jnp.where(even, layer_ref[...], seg_ref[...]).astype(F32).astype(BF16)
    slot = lax.broadcasted_iota(I32, (tall, count), 0)
    tail_row = lax.broadcasted_iota(I32, (TAIL, LANES), 0)

    def one(group, carried):
        key = jnp.where(own == group, rank, -1)
        chosen = (slot == key).astype(F32).astype(BF16)
        block = jnp.dot(chosen[:slots], src_ref[...], preferred_element_type=F32)
        cells = lax.dot_general(
            names, chosen, (((1,), (1,)), ((), ())), preferred_element_type=F32
        )
        tail = cells[:, :LANES]
        for half in range(1, halves_of(slots)):
            tail = jnp.where(
                tail_row < 2 * half, tail, cells[:, half * LANES : (half + 1) * LANES]
            )
        out_ref[group, :slots] = block.astype(BF16)
        out_ref[group, slots:] = tail.astype(BF16)
        return carried

    lax.fori_loop(0, groups, one, 0, unroll=groups <= 8)


def cells_of(arrived_ref, group, slots, segs):
    tail = arrived_ref[group, slots:].astype(F32)
    return [
        tail[2 * half : 2 * half + 1] * segs + tail[2 * half + 1 : 2 * half + 2]
        for half in range(halves_of(slots))
    ]


def rim_kernel(slots, layers, arrived_ref, low_ref, high_ref, off_ref, bottom_ref, prod_ref):
    groups = arrived_ref.shape[0]
    segs = low_ref.shape[0]
    line = lax.broadcasted_iota(I32, (2 * segs, LANES), 0)
    wanted = jnp.where(line < segs, line, line + (layers - 2) * segs).astype(F32)
    wide = min(slots, LANES)

    def one(group, total):
        for half, cells in enumerate(cells_of(arrived_ref, group, slots, segs)):
            chosen = (wanted == cells).astype(F32).astype(BF16)
            total = total + jnp.dot(
                chosen[:, :wide],
                arrived_ref[group, half * wide : (half + 1) * wide],
                preferred_element_type=F32,
            )
        return total

    model = lax.fori_loop(
        0, groups, one, jnp.zeros((2 * segs, LANES), F32), unroll=groups <= 8
    )
    bottom_ref[...] = low_ref[...] - model[:segs]
    prod_ref[...] = off_ref[...] * (high_ref[...] - model[segs:])


def scatter_kernel(
    slots, segs, arrived_ref, tdi_hbm, diag_hbm, off_hbm,
    resid_ref, extra_ref, diag_ref, off_ref, cell_ref, blocks, cells, sem, sems,
):
    copies = [
        pltpu.make_async_copy(source, target, sems.at[i])
        for i, (source, target) in enumerate(
            ((tdi_hbm, resid_ref), (diag_hbm, diag_ref), (off_hbm, off_ref))
        )
    ]
    for copy in copies:
        copy.start()
    groups = arrived_ref.shape[0]
    halves = halves_of(slots)
    wide = min(slots, LANES)

    def name(group, carried):
        for half, row in enumerate(cells_of(arrived_ref, group, slots, segs)):
            cell_ref[pl.ds(group * halves + half, 1), :] = row.astype(I32)
        return carried

    lax.fori_loop(0, groups, name, 0, unroll=groups <= 8)
    copy = pltpu.make_async_copy(cell_ref, cells, sem)
    copy.start()

    def widen(group, carried):
        blocks[pl.ds(pl.multiple_of(group * slots, slots), slots), :] = arrived_ref[
            group, :slots
        ].astype(F32)
        return carried

    lax.fori_loop(0, groups, widen, 0, unroll=groups <= 8)
    extra_ref[...] = jnp.zeros_like(extra_ref)
    copy.wait()
    copies[0].wait()

    def scatter(line, carried):
        for slot in range(0, wide, 2):
            for step, plane in enumerate((resid_ref, extra_ref)):
                place = pl.ds(cells[line, slot + step], 1)
                plane[place, :] = plane[place, :] - blocks[
                    pl.ds(line * wide + slot + step, 1), :
                ]
        return carried

    lax.fori_loop(0, groups * halves, scatter, 0)
    for copy in copies[1:]:
        copy.wait()


def weigh_kernel(
    slots, layers, chunk, resid_ref, extra_ref, diag_ref, off_ref, lower_ref, upper_ref, cells,
    weighted_ref, picked_ref, sum_ref, plane, sems,
):
    segs = lower_ref.shape[0]
    steps = layers // chunk
    size = chunk * segs

    def layer_rows(layer):
        return pl.ds(pl.multiple_of(layer * segs, segs), segs)

    def send(step):
        place = pl.ds(pl.multiple_of(step * size, size), size)
        return pltpu.make_async_copy(plane.at[place], weighted_ref.at[place], sems.at[step])

    def weigh(layer, carried):
        here, below, total = carried
        place, above_place = layer_rows(layer), layer_rows(layer + 1)
        above = resid_ref[above_place, :] + extra_ref[above_place, :]
        coupling = off_ref[place, :]
        out = diag_ref[place, :] * here + coupling * above + below
        plane[place, :] = out
        return above, coupling * here, total + here * out

    first, last = layer_rows(0), layer_rows(layers - 1)
    carried = (
        resid_ref[first, :] + extra_ref[first, :],
        lower_ref[...],
        jnp.zeros((segs, LANES), F32),
    )
    for step in range(steps):
        stop = min((step + 1) * chunk, layers - 1)
        carried = lax.fori_loop(step * chunk, stop, weigh, carried)
        if step < steps - 1:
            send(step).start()
    here, below, total = carried
    out = diag_ref[last, :] * here + off_ref[last, :] * upper_ref[...] + below
    plane[last, :] = out
    send(steps - 1).start()
    total = jnp.sum(total + here * out, axis=0, keepdims=True)
    sum_ref[...] = jnp.broadcast_to(jnp.sum(total, axis=1, keepdims=True), (1, LANES))
    wide = min(slots, LANES)

    def gather(line, carried):
        for slot in range(0, wide, 16):
            rows = [plane[pl.ds(cells[line, slot + step], 1), :] for step in range(16)]
            place = pl.ds(pl.multiple_of(line * wide + slot, 16), 16)
            picked_ref[place, :] = jnp.concatenate(rows, axis=0).astype(BF16)
        return carried

    lax.fori_loop(0, cells.shape[0], gather, 0)
    for step in range(steps):
        send(step).wait()


def unpack_kernel(slots, pos_ref, returned_ref, out_ref):
    groups = returned_ref.shape[0]
    count = pos_ref.shape[1]
    wide = min(slots, LANES)
    pos = jnp.transpose(jnp.broadcast_to(pos_ref[...], (LANES, count)).astype(F32))
    lane = lax.broadcasted_iota(I32, (count, LANES), 1).astype(F32)

    def one(group, total):
        for start in range(0, slots, wide):
            base = (group * slots + start) * jnp.float32(1)
            chosen = (pos - base == lane).astype(F32).astype(BF16)
            total = total + jnp.dot(
                chosen[:, :wide],
                returned_ref[group, start : start + wide],
                preferred_element_type=F32,
            )
        return total

    total = lax.fori_loop(0, groups, one, jnp.zeros((count, LANES), F32), unroll=groups <= 8)
    out_ref[...] = total.astype(BF16)


def in_hbm(*arrays):
    return [pltpu.with_memory_space_constraint(array, pltpu.HBM) for array in arrays]


def shape_of(shape, dtype):
    return jax.ShapeDtypeStruct(shape, dtype)


def params(mib):
    return pltpu.CompilerParams(vmem_limit_bytes=mib << 20)


def shards(tdi_data, noise_diag, noise_off, src_blocks, owner_dev, layer_in, seg_in):
    axes = ("band", "tm")
    groups = lax.axis_size("band") * lax.axis_size("tm")
    _, layers, segs, bins = tdi_data.shape
    count = src_blocks.shape[0]
    slots = 2 * count // groups
    block = slots + TAIL
    lines = groups * halves_of(slots)
    cell_count = layers * segs
    tdi = tdi_data.reshape(cell_count, bins)
    diag = noise_diag.reshape(cell_count, bins)
    off = noise_off.reshape(cell_count, bins)
    outgoing, position = pl.pallas_call(
        functools.partial(pack_kernel, groups, slots),
        out_shape=(shape_of((groups, block, bins), BF16), shape_of((1, count), I32)),
        in_specs=[HBM] * 4,
        out_specs=(VMEM, VMEM),
        scratch_shapes=[
            pltpu.VMEM((1, count), I32),
            pltpu.VMEM((1, count), I32),
            pltpu.VMEM((1, count), I32),
            pltpu.VMEM((count, bins), BF16),
            pltpu.SemaphoreType.DMA((4,)),
        ],
        compiler_params=params(48),
    )(
        *in_hbm(
            owner_dev.reshape(1, count),
            layer_in.reshape(1, count),
            seg_in.reshape(1, count),
            src_blocks.reshape(count, bins),
        )
    )
    arrived = lax.all_to_all(outgoing, axes, split_axis=0, concat_axis=0, tiled=True)
    rim = shape_of((segs, bins), F32)
    bottom, product = pl.pallas_call(
        functools.partial(rim_kernel, slots, layers),
        out_shape=(rim, rim),
        in_specs=[VMEM] * 4,
        out_specs=(VMEM, VMEM),
        compiler_params=params(16),
    )(arrived, tdi[:segs], tdi[-segs:], off[-segs:])
    lower_rim = passed_along(product, "band", 1)
    upper_rim = passed_along(bottom, "band", -1)
    plane = shape_of((cell_count, bins), F32)
    resid, extra, diag, off, cells = pl.pallas_call(
        functools.partial(scatter_kernel, slots, segs),
        out_shape=(plane,) * 4 + (shape_of((lines, LANES), I32),),
        in_specs=[VMEM] + [HBM] * 3,
        out_specs=(VMEM,) * 5,
        scratch_shapes=[
            pltpu.VMEM((groups * slots, bins), F32),
            pltpu.SMEM((lines, LANES), I32),
            pltpu.SemaphoreType.DMA,
            pltpu.SemaphoreType.DMA((3,)),
        ],
        compiler_params=params(24),
    )(arrived, *in_hbm(tdi, diag, off))
    chunk = max(1, layers // 8)
    weighted, picked, summed = pl.pallas_call(
        functools.partial(weigh_kernel, slots, layers, chunk),
        out_shape=(plane, shape_of((groups * slots, bins), BF16), shape_of((1, bins), F32)),
        in_specs=[VMEM] * 6 + [SMEM],
        out_specs=(HBM, VMEM, VMEM),
        scratch_shapes=[
            pltpu.VMEM((cell_count, bins), F32),
            pltpu.SemaphoreType.DMA((layers // chunk,)),
        ],
        compiler_params=params(24),
    )(resid, extra, diag, off, lower_rim, upper_rim, cells)
    returned = lax.all_to_all(
        picked.reshape(groups, slots, bins), axes, split_axis=0, concat_axis=0, tiled=True
    )
    summed = all_sum(summed, ("chan", "tm", "band"))
    cells_all = lax.axis_size("chan") * groups * cell_count * bins
    log_like = -0.5 * summed[0, :1] / cells_all
    grads = pl.pallas_call(
        functools.partial(unpack_kernel, slots),
        out_shape=shape_of((count, bins), BF16),
        in_specs=[VMEM, VMEM],
        out_specs=VMEM,
        compiler_params=params(16),
    )(position, returned)
    return (
        weighted.reshape(tdi_data.shape),
        log_like,
        grads.reshape(src_blocks.shape),
    )


def solution(mesh):
    planes = P(("grp", "chan"), "band", "tm", None)
    lists = P(("grp", "band", "tm"))
    return jax.shard_map(
        shards,
        mesh=mesh,
        in_specs=(
            planes,
            planes,
            planes,
            P(("grp", "band", "tm"), "chan", None),
            P(("grp", "band", "tm"), None),
            lists,
            lists,
        ),
        out_specs=(planes, P("grp"), P(("grp", "band", "tm"), "chan", None)),
        check_vma=False,
    )
```

time: 132 us -> 68.8 us (0.52)
  blocking collectives: 34.9 us -> 0 us
  other arithmetic: 32.9 us -> 0.01 us
  local copies, waits for them, and re-layouts: 22.7 us -> 0.8 us
  Pallas kernels: 0 us -> 19.5 us
  waiting for transfers between devices: 17.3 us -> 22.4 us
  starting transfers between devices: 20.7 us -> 23.4 us
    psum x1 -> x0, blocking collectives: 34.9 us -> none  [shards(): summed = lax.psum(partial_sum, ('band', 'tm', 'chan'))]
    pallas_call x0 -> x5, Pallas kernels: none -> 19.5 us  [the longest x1 7.57 us: shards(): pl.pallas_call(functools.partial(scatter_kernel, slots, segs), out_shape=...]
    scatter-add x1 -> x0, other arithmetic: 14.4 us -> none  [shards(): jax.ops.segment_sum(arrived.astype(jnp.float32), home_cells, num_segments...]
    gather x2 -> x0, local copies, waits for them, and re-layouts: 11 us -> none  [the longest x1 7.77 us: shards(): picked = jnp.take(flat_plane, home_cells, axis=0).astype(jnp.bfloat16)]
    scatter x2 -> x0, local copies, waits for them, and re-layouts: 8.86 us -> none  [the longest x1 4.88 us: shards(): jnp.zeros((groups * slots_per,), jnp.int32).at[position].set(cell_ids)]
    ppermute x0 -> x4, waiting for transfers between devices: none -> 8.03 us  [all_sum(): lax.ppermute(value, axis, [(i, i ^ step) for i in range(count)])]
    ppermute x0 -> x4, starting transfers between devices: none -> 6.26 us  [all_sum(): lax.ppermute(value, axis, [(i, i ^ step) for i in range(count)])]
    mul x1 -> x0, other arithmetic: 6.14 us -> none  [shards(): product = noise_off * residual]
  transfers between devices with their start and end apart: 5 -> 8, of which waited for: 3 -> 5; matrix products, arithmetic and copies ran while one was open for 4% -> 1% of each run, Pallas kernels for 0% -> 11%
where the time goes in v1:
time: 68.8 us; the launch traced here: 68.1 us
  starting transfers between devices  23.4 us (34%)
  waiting for transfers between devices  22.4 us (33%)
  Pallas kernels  19.5 us (28%)
  between operations  1.89 us (3%)
  local copies, waits for them, and re-layouts  0.8 us (1%)
    all_to_all x1, waiting for transfers between devices, shards(): lax.all_to_all(outgoing, axes, split_axis=0, concat_axis=0, tiled=True)  14.4 us
    ppermute x4, waiting for transfers between devices, all_sum(): lax.ppermute(value, axis, [(i, i ^ step) for i in range(count)])  8.03 us
    pallas_call x1, Pallas kernels, shards(): pl.pallas_call(functools.partial(scatter_kernel, slots, segs), out_shape=...  7.57 us
    all_to_all x1, starting transfers between devices, shards(): lax.all_to_all(outgoing, axes, split_axis=0, concat_axis=0, tiled=True)  7.27 us
    ppermute x4, starting transfers between devices, all_sum(): lax.ppermute(value, axis, [(i, i ^ step) for i in range(count)])  6.26 us
    all_to_all x1, starting transfers between devices, shards(): lax.all_to_all(picked.reshape(groups, slots, bins), axes, split_axis=0, c...  5.94 us
    pallas_call x1, Pallas kernels, shards(): pl.pallas_call(functools.partial(weigh_kernel, slots, layers, chunk), out...  5.54 us
    pallas_call x1, Pallas kernels, shards(): pl.pallas_call(functools.partial(pack_kernel, groups, slots), out_shape=(...  4.12 us
  transfers between devices with their start and end apart: 8, of which 5 were waited for; matrix products, arithmetic and copies ran while one was open for 1% of the time, Pallas kernels for 11%

profile of v1, /device:TPU:0, one launch (start us, length us, event | category | flops | bytes accessed | tf_op | source)
XLA Modules:
  0.0 68.1 jit_solution(3309876380581850170)
XLA Ops:
  0.6 4.1 %shard_map.94 = (bf16[8,272,128]{2,1,0:T(8,128)(2,1)}, s32[1,1024]{1,0:T(1,128)S(1)}) custom-call(s32[1,1024]{1,0:T(1,128)} %bitcast.23, s32[1,1024]{1,0:T(1,128)} %bitcast.24, s32[1,1024]{1,0:T(1,128)} %bitcast.25, bf16[1024,128]{1,0:T(8,128)(2,1)} %bitcast.22), custom_call_target="tpu_custom_call" | custom-call | tf_op jit(solution)/shard_map/pallas_call | solution.py:279
  4.8 7.3 %all-to-all-start = ((bf16[8,272,128]{2,1,0:T(8,128)(2,1)}), bf16[8,272,128]{2,1,0:T(8,128)(2,1)S(1)}, u32[]{:S(2)}, u32[]{:S(2)}) async-start(bf16[8,272,128]{2,1,0:T(8,128)(2,1)} %get-tuple-element.15), calls=%async_computation | async-start | bytes 1114112 | tf_op jit(solution)/shard_map/all_to_all | solution.py:300
  12.0 0.8 %slice_bitcast_fusion.1 = (f32[64,128]{1,0:T(8,128)S(1)}, f32[64,128]{1,0:T(8,128)S(1)}, f32[64,128]{1,0:T(8,128)S(1)}) fusion(f32[1,128,64,128]{3,2,1,0:T(8,128)} %param.7, f32[1,128,64,128]{3,2,1,0:T(8,128)} %param.9), kind=kLoop, calls=%fused_computation.1 | loop fusion | bytes 196608 | tf_op jit(solution)/shard_map/slice | solution.py:308
  12.8 14.4 %all-to-all-done.arrived_ref = bf16[8,272,128]{2,1,0:T(8,128)(2,1)S(1)} async-done(((bf16[8,272,128]{2,1,0:T(8,128)(2,1)}), bf16[8,272,128]{2,1,0:T(8,128)(2,1)S(1)}, u32[]{:S(2)}, u32[]{:S(2)}) %all-to-all-start) | async-done | bytes 557088 | tf_op jit(solution)/shard_map/all_to_all | solution.py:300
  27.2 0.3 shard_map.96
  27.5 2.6 %collective-permute-start = (f32[64,128]{1,0:T(8,128)S(1)}, f32[64,128]{1,0:T(8,128)S(1)}, u32[]{:S(2)}, u32[]{:S(2)}) collective-permute-start(f32[64,128]{1,0:T(8,128)S(1)} %get-tuple-element.20), channel_id=1, source_target_pairs={{0,4},{4,8},{8,12},{1,5},{5,9},{9,13},{2,6},{6,10},{10,14},{3,7},{... | collective-permute-start | bytes 98312 | tf_op jit(solution)/shard_map/ppermute | solution.py:23
  30.1 1.3 %collective-permute-start.1 = (f32[64,128]{1,0:T(8,128)S(1)}, f32[64,128]{1,0:T(8,128)S(1)}, u32[]{:S(2)}, u32[]{:S(2)}) collective-permute-start(f32[64,128]{1,0:T(8,128)S(1)} %get-tuple-element.21), channel_id=1, source_target_pairs={{4,0},{8,4},{12,8},{5,1},{9,5},{13,9},{6,2},{10,6},{14,10},{7,3},{... | collective-permute-start | bytes 98312 | tf_op jit(solution)/shard_map/ppermute | solution.py:23
  31.4 7.6 %shard_map.95 = (f32[8192,128]{1,0:T(8,128)S(1)}, f32[8192,128]{1,0:T(8,128)S(1)}, f32[8192,128]{1,0:T(8,128)S(1)}, f32[8192,128]{1,0:T(8,128)S(1)}, s32[16,128]{1,0:T(8,128)S(1)}) custom-call(bf16[8,272,128]{2,1,0:T(8,128)(2,1)S(1)} %all-to-all-done.arrived_ref, f32[8192,128]{1,0:T(8,128)} %bitcast.18, f32[8192,128]{1,0:T(8,128)} %bitcast.20, ...), custom_call_target="tpu_custom_call" | custom-call | tf_op jit(solution)/shard_map/pallas_call | solution.py:312
  39.0 0.0 collective-permute-done.lower_ref
  39.0 0.0 collective-permute-done.1.upper_ref
  39.0 5.5 %shard_map.97 = (f32[8192,128]{1,0:T(8,128)}, bf16[2048,128]{1,0:T(8,128)(2,1)}, f32[1,128]{1,0:T(1,128)S(1)}) custom-call(f32[8192,128]{1,0:T(8,128)S(1)} %get-tuple-element.16.resid_ref, f32[8192,128]{1,0:T(8,128)S(1)} %get-tuple-element.17.extra_ref, f32[8192,128]{1,0:T(8,128)S(1)} %get-tuple-element.18.diag_ref, ...), custom_call_target="tpu_custom_call" | custom-call | tf_op jit(solution)/shard_map/pallas_call | solution.py:326
  44.6 5.9 %all-to-all-start.1 = ((bf16[8,256,128]{2,1,0:T(8,128)(2,1)}), bf16[8,256,128]{2,1,0:T(8,128)(2,1)S(1)}, u32[]{:S(2)}, u32[]{:S(2)}) async-start(bf16[8,256,128]{2,1,0:T(8,128)(2,1)} %bitcast.12), calls=%async_computation.1 | async-start | bytes 1048576 | tf_op jit(solution)/shard_map/all_to_all | solution.py:337
  50.5 0.0 collective-permute-start.2
  50.5 1.1 %collective-permute-done.2 = f32[1,128]{1,0:T(1,128)S(1)} collective-permute-done((f32[1,128]{1,0:T(1,128)S(1)}, f32[1,128]{1,0:T(1,128)S(1)}, u32[]{:S(2)}, u32[]{:S(2)}) %collective-permute-start.2) | collective-permute-done | bytes 544 | tf_op jit(solution)/shard_map/ppermute | solution.py:30
  51.7 2.0 %collective-permute-start.3 = (f32[1,128]{1,0:T(1,128)S(1)}, f32[1,128]{1,0:T(1,128)S(1)}, u32[]{:S(2)}, u32[]{:S(2)}) collective-permute-start(f32[1,128]{1,0:T(1,128)S(1)} %add.12), channel_id=1, source_target_pairs={{0,2},{2,0},{1,3},{3,1},{4,6},{6,4},{5,7},{7,5},{8,10},{10,8},{9,1... | collective-permute-start | bytes 1544 | tf_op jit(solution)/shard_map/ppermute | solution.py:30
  53.7 2.7 %collective-permute-done.3 = f32[1,128]{1,0:T(1,128)S(1)} collective-permute-done((f32[1,128]{1,0:T(1,128)S(1)}, f32[1,128]{1,0:T(1,128)S(1)}, u32[]{:S(2)}, u32[]{:S(2)}) %collective-permute-start.3) | collective-permute-done | bytes 544 | tf_op jit(solution)/shard_map/ppermute | solution.py:30
  56.4 0.9 %collective-permute-start.4 = (f32[1,128]{1,0:T(1,128)S(1)}, f32[1,128]{1,0:T(1,128)S(1)}, u32[]{:S(2)}, u32[]{:S(2)}) collective-permute-start(f32[1,128]{1,0:T(1,128)S(1)} %add.13), channel_id=1, source_target_pairs={{0,4},{4,0},{8,12},{12,8},{1,5},{5,1},{9,13},{13,9},{2,6},{6,2},{1... | collective-permute-start | bytes 1544 | tf_op jit(solution)/shard_map/ppermute | solution.py:30
  57.3 2.7 %collective-permute-done.4 = f32[1,128]{1,0:T(1,128)S(1)} collective-permute-done((f32[1,128]{1,0:T(1,128)S(1)}, f32[1,128]{1,0:T(1,128)S(1)}, u32[]{:S(2)}, u32[]{:S(2)}) %collective-permute-start.4) | collective-permute-done | bytes 544 | tf_op jit(solution)/shard_map/ppermute | solution.py:30
  60.0 3.4 %collective-permute-start.5 = (f32[1,128]{1,0:T(1,128)S(1)}, f32[1,128]{1,0:T(1,128)S(1)}, u32[]{:S(2)}, u32[]{:S(2)}) collective-permute-start(f32[1,128]{1,0:T(1,128)S(1)} %add.14), channel_id=1, source_target_pairs={{0,8},{4,12},{8,0},{12,4},{1,9},{5,13},{9,1},{13,5},{2,10},{6,14},... | collective-permute-start | bytes 1544 | tf_op jit(solution)/shard_map/ppermute | solution.py:30
  63.3 1.5 %collective-permute-done.5 = f32[1,128]{1,0:T(1,128)S(1)} collective-permute-done((f32[1,128]{1,0:T(1,128)S(1)}, f32[1,128]{1,0:T(1,128)S(1)}, u32[]{:S(2)}, u32[]{:S(2)}) %collective-permute-start.5) | collective-permute-done | bytes 544 | tf_op jit(solution)/shard_map/ppermute | solution.py:30
  64.9 0.0 all-to-all-done.1.returned_ref
  64.9 2.0 %shard_map.98 = bf16[1024,128]{1,0:T(8,128)(2,1)} custom-call(s32[1,1024]{1,0:T(1,128)S(1)} %get-tuple-element.25.pos_ref, bf16[8,256,128]{2,1,0:T(8,128)(2,1)S(1)} %all-to-all-done.1.returned_ref), custom_call_target="tpu_custom_call" | custom-call | tf_op jit(solution)/shard_map/pallas_call | solution.py:343
  (4 shorter events, 0.0 us)
Async XLA Ops:
  4.8 22.5 %all-to-all-start = ((bf16[8,272,128]{2,1,0:T(8,128)(2,1)}), bf16[8,272,128]{2,1,0:T(8,128)(2,1)S(1)}, u32[]{:S(2)}, u32[]{:S(2)}) async-start(bf16[8,272,128]{2,1,0:T(8,128)(2,1)} %get-tuple-element.15), calls=%async_computation | async-start | bytes 1114112 | tf_op jit(solution)/shard_map/all_to_all | solution.py:300
  27.5 11.5 %collective-permute-start = (f32[64,128]{1,0:T(8,128)S(1)}, f32[64,128]{1,0:T(8,128)S(1)}, u32[]{:S(2)}, u32[]{:S(2)}) collective-permute-start(f32[64,128]{1,0:T(8,128)S(1)} %get-tuple-element.20), channel_id=1, source_target_pairs={{0,4},{4,8},{8,12},{1,5},{5,9},{9,13},{2,6},{6,10},{10,14},{3,7},{... | collective-permute-start | bytes 98312 | tf_op jit(solution)/shard_map/ppermute | solution.py:23
  30.1 8.9 %collective-permute-start.1 = (f32[64,128]{1,0:T(8,128)S(1)}, f32[64,128]{1,0:T(8,128)S(1)}, u32[]{:S(2)}, u32[]{:S(2)}) collective-permute-start(f32[64,128]{1,0:T(8,128)S(1)} %get-tuple-element.21), channel_id=1, source_target_pairs={{4,0},{8,4},{12,8},{5,1},{9,5},{13,9},{6,2},{10,6},{14,10},{7,3},{... | collective-permute-start | bytes 98312 | tf_op jit(solution)/shard_map/ppermute | solution.py:23
  44.6 20.3 %all-to-all-start.1 = ((bf16[8,256,128]{2,1,0:T(8,128)(2,1)}), bf16[8,256,128]{2,1,0:T(8,128)(2,1)S(1)}, u32[]{:S(2)}, u32[]{:S(2)}) async-start(bf16[8,256,128]{2,1,0:T(8,128)(2,1)} %bitcast.12), calls=%async_computation.1 | async-start | bytes 1048576 | tf_op jit(solution)/shard_map/all_to_all | solution.py:337
  50.5 1.1 %collective-permute-start.2 = (f32[1,128]{1,0:T(1,128)S(1)}, f32[1,128]{1,0:T(1,128)S(1)}, u32[]{:S(2)}, u32[]{:S(2)}) collective-permute-start(f32[1,128]{1,0:T(1,128)S(1)} %get-tuple-element.24), channel_id=1, source_target_pairs={{0,1},{1,0},{2,3},{3,2},{4,5},{5,4},{6,7},{7,6},{8,9},{9,8},{10,11... | collective-permute-start | bytes 1544 | tf_op jit(solution)/shard_map/ppermute | solution.py:30
  51.7 4.8 %collective-permute-start.3 = (f32[1,128]{1,0:T(1,128)S(1)}, f32[1,128]{1,0:T(1,128)S(1)}, u32[]{:S(2)}, u32[]{:S(2)}) collective-permute-start(f32[1,128]{1,0:T(1,128)S(1)} %add.12), channel_id=1, source_target_pairs={{0,2},{2,0},{1,3},{3,1},{4,6},{6,4},{5,7},{7,5},{8,10},{10,8},{9,1... | collective-permute-start | bytes 1544 | tf_op jit(solution)/shard_map/ppermute | solution.py:30
  56.4 3.5 %collective-permute-start.4 = (f32[1,128]{1,0:T(1,128)S(1)}, f32[1,128]{1,0:T(1,128)S(1)}, u32[]{:S(2)}, u32[]{:S(2)}) collective-permute-start(f32[1,128]{1,0:T(1,128)S(1)} %add.13), channel_id=1, source_target_pairs={{0,4},{4,0},{8,12},{12,8},{1,5},{5,1},{9,13},{13,9},{2,6},{6,2},{1... | collective-permute-start | bytes 1544 | tf_op jit(solution)/shard_map/ppermute | solution.py:30
  60.0 4.9 %collective-permute-start.5 = (f32[1,128]{1,0:T(1,128)S(1)}, f32[1,128]{1,0:T(1,128)S(1)}, u32[]{:S(2)}, u32[]{:S(2)}) collective-permute-start(f32[1,128]{1,0:T(1,128)S(1)} %add.14), channel_id=1, source_target_pairs={{0,8},{4,12},{8,0},{12,4},{1,9},{5,13},{9,1},{13,5},{2,10},{6,14},... | collective-permute-start | bytes 1544 | tf_op jit(solution)/shard_map/ppermute | solution.py:30

commit v2 on v0

v2 whole, which is shorter than its diff:
```python
import functools

import jax
import jax.numpy as jnp
from jax import lax
from jax.experimental import pallas as pl
from jax.experimental.pallas import tpu as pltpu
from jax.sharding import PartitionSpec as P

LANES = 128
TAIL = 16
AXES = ("band", "tm")
VMEM = pl.BlockSpec(memory_space=pltpu.VMEM)
SMEM = pl.BlockSpec(memory_space=pltpu.SMEM)
HBM = pl.BlockSpec(memory_space=pltpu.HBM)
HBM_BYTES_PER_US = 3_300_000
F32 = jnp.float32
BF16 = jnp.bfloat16
I32 = jnp.int32


def passed_along(value, axis, steps):
    count = lax.axis_size(axis)
    leading, last = (max(0, -steps), min(count, count - steps))
    return lax.ppermute(value, axis, [(source, source + steps) for source in range(leading, last)])


def halves_of(slots):
    return max(1, slots // LANES)


def few(count):
    return count <= 8


def each(refs, firsts, body, carried=0):
    if firsts is None:
        firsts = [sum(ref.shape[0] for ref in refs[:i]) for i in range(len(refs))]
    for ref, first in zip(refs, firsts):
        length = ref.shape[0]
        carried = lax.fori_loop(
            0,
            length,
            lambda i, value, ref=ref, first=first: body(ref, i, first + i, value),
            carried,
            unroll=few(length),
        )
    return carried


def pack_blocks(slots, firsts, pos, names, src_ref, outs):
    count = pos.shape[1]
    slot = lax.broadcasted_iota(I32, (max(slots, LANES), count), 0)
    tail_row = lax.broadcasted_iota(I32, (TAIL, LANES), 0)

    def one(ref, i, block, carried):
        chosen = (slot == pos - block * slots).astype(F32).astype(BF16)
        if slots < LANES:
            chosen = jnp.where(slot < slots, chosen, jnp.zeros_like(chosen))
        rows = jnp.dot(chosen[:slots], src_ref[...], preferred_element_type=F32)
        cells = lax.dot_general(
            names, chosen, (((1,), (1,)), ((), ())), preferred_element_type=F32
        )
        tail = cells[:, :LANES]
        for half in range(1, halves_of(slots)):
            tail = jnp.where(
                tail_row < 2 * half, tail, cells[:, half * LANES : (half + 1) * LANES]
            )
        ref[i, :slots] = rows.astype(BF16)
        ref[i, slots:] = tail.astype(BF16)
        return carried

    each(outs, firsts, one)


def pack_kernel(
    slots, groups, direct, firsts, own_hbm, layer_hbm, seg_hbm, src_hbm,
    pos_ref, names_ref, src_ref, *rest,
):
    outs, (own_ref, layer_ref, seg_ref, sems) = rest[:-4], rest[-4:]
    copies = [
        pltpu.make_async_copy(source, target, sems.at[i])
        for i, (source, target) in enumerate(
            ((own_hbm, own_ref), (layer_hbm, layer_ref), (seg_hbm, seg_ref), (src_hbm, src_ref))
        )
    ]
    for copy in copies:
        copy.start()
    count = own_ref.shape[1]
    width = min(count, 256)
    before = (
        lax.broadcasted_iota(I32, (width, width), 0) < lax.broadcasted_iota(I32, (width, width), 1)
    ).astype(F32).astype(BF16)
    copies[0].wait()
    own = own_ref[...]
    if direct:
        own = own ^ (lax.axis_index("band") * lax.axis_size("tm") + lax.axis_index("tm"))
    rows = max(16, groups)
    owned = (lax.broadcasted_iota(I32, (rows, count), 0) == own).astype(F32)
    carry = jnp.zeros((rows, 1), F32)
    ranks = []
    for start in range(0, count, width):
        part = owned[:, start : start + width]
        earlier = jnp.dot(part.astype(BF16), before, preferred_element_type=F32) + carry
        ranks.append(jnp.sum(part * earlier, axis=0, keepdims=True))
        carry = carry + jnp.sum(part, axis=1, keepdims=True)
    pos = own * slots + jnp.concatenate(ranks, axis=1).astype(I32)
    pos_ref[...] = pos
    for copy in copies[1:]:
        copy.wait()
    even = lax.broadcasted_iota(I32, (TAIL, count), 0) % 2 == 0
    names = jnp.where(even, layer_ref[...], seg_ref[...]).astype(F32).astype(BF16)
    names_ref[...] = names
    pack_blocks(slots, firsts, pos, names, src_ref, outs)


def repack_kernel(slots, firsts, after_ref, pos_ref, names_ref, src_ref, *outs):
    pack_blocks(slots, firsts, pos_ref[...], names_ref[...], src_ref, outs)


def cells_of(ref, i, slots, segs):
    tail = ref[i, slots:].astype(F32)
    return [
        tail[2 * half : 2 * half + 1] * segs + tail[2 * half + 1 : 2 * half + 2]
        for half in range(halves_of(slots))
    ]


def rim_kernel(slots, layers, low_ref, high_ref, off_ref, *rest):
    chunks, (bottom_ref, prod_ref) = rest[:-2], rest[-2:]
    segs = low_ref.shape[0]
    line = lax.broadcasted_iota(I32, (2 * segs, LANES), 0)
    wanted = jnp.where(line < segs, line, line + (layers - 2) * segs).astype(F32)
    wide = min(slots, LANES)

    def one(ref, i, block, total):
        for half, cells in enumerate(cells_of(ref, i, slots, segs)):
            chosen = (wanted == cells).astype(F32).astype(BF16)
            total = total + jnp.dot(
                chosen[:, :wide],
                ref[i, half * wide : (half + 1) * wide],
                preferred_element_type=F32,
            )
        return total

    model = each(chunks, None, one, jnp.zeros((2 * segs, LANES), F32))
    bottom_ref[...] = low_ref[...] - model[:segs]
    prod_ref[...] = off_ref[...] * (high_ref[...] - model[segs:])


def scatter_blocks(slots, segs, chunks, resid_ref, extra_ref, cell_ref, blocks, cells, sem, ready):
    halves = halves_of(slots)
    wide = min(slots, LANES)

    def name(ref, i, block, carried):
        for half, row in enumerate(cells_of(ref, i, slots, segs)):
            cell_ref[pl.ds(block * halves + half, 1), :] = row.astype(I32)
        return carried

    each(chunks, None, name)
    copy = pltpu.make_async_copy(cell_ref, cells, sem)
    copy.start()

    def widen(ref, i, block, carried):
        blocks[pl.ds(pl.multiple_of(block * slots, slots), slots), :] = ref[i, :slots].astype(F32)
        return carried

    each(chunks, None, widen)
    ready()
    copy.wait()

    def scatter(line, carried):
        for slot in range(0, wide, 2):
            for step, plane in enumerate((resid_ref, extra_ref)):
                place = pl.ds(cells[line, slot + step], 1)
                plane[place, :] = plane[place, :] - blocks[
                    pl.ds(line * wide + slot + step, 1), :
                ]
        return carried

    lax.fori_loop(0, cell_ref.shape[0], scatter, 0)


def first_scatter_kernel(slots, segs, tdi_hbm, diag_hbm, off_hbm, *rest):
    chunks, outs, (blocks, cells, sem, sems) = rest[:-12], rest[-12:-4], rest[-4:]
    resid_ref, extra_ref, diag_ref, off_ref, low_ref, high_ref, last_ref, cell_ref = outs
    size = resid_ref.shape[0]
    copies = [
        pltpu.make_async_copy(source, target, sems.at[i])
        for i, (source, target) in enumerate(
            ((tdi_hbm, resid_ref), (diag_hbm, diag_ref), (off_hbm, off_ref))
        )
    ]
    for copy in copies:
        copy.start()

    def ready():
        extra_ref[...] = jnp.zeros_like(extra_ref)
        copies[0].wait()
        low_ref[...] = resid_ref[:segs]
        high_ref[...] = resid_ref[size - segs :]

    scatter_blocks(slots, segs, chunks, resid_ref, extra_ref, cell_ref, blocks, cells, sem, ready)
    for copy in copies[1:]:
        copy.wait()
    last_ref[...] = off_ref[size - segs :]


def scatter_kernel(slots, segs, resid_in, extra_in, *rest):
    chunks, (resid_ref, extra_ref, cell_ref, blocks, cells, sem) = rest[:-6], rest[-6:]
    scatter_blocks(
        slots, segs, chunks, resid_ref, extra_ref, cell_ref, blocks, cells, sem, lambda: None
    )


def weigh_kernel(segs, layers, resid_ref, extra_ref, diag_ref, off_ref, plane_ref, part_ref):
    def layer_rows(layer):
        return pl.ds(pl.multiple_of(layer * segs, segs), segs)

    def weigh(layer, carried):
        here, below, total = carried
        place, above_place = layer_rows(layer), layer_rows(layer + 1)
        above = resid_ref[above_place, :] + extra_ref[above_place, :]
        coupling = off_ref[place, :]
        out = diag_ref[place, :] * here + coupling * above + below
        plane_ref[place, :] = out
        return above, coupling * here, total + here * out

    first, last = layer_rows(0), layer_rows(layers - 1)
    zero = jnp.zeros((segs, LANES), F32)
    here, below, total = lax.fori_loop(
        0, layers - 1, weigh, (resid_ref[first, :] + extra_ref[first, :], zero, zero), unroll=4
    )
    out = diag_ref[last, :] * here + below
    plane_ref[last, :] = out
    part_ref[...] = jnp.sum(total + here * out, axis=0, keepdims=True)


def gather_blocks(slots, plane_ref, cell_refs, outs):
    halves = halves_of(slots)
    wide = min(slots, LANES)

    for cells, out in zip(cell_refs, outs):

        def gather(line, carried, cells=cells, out=out):
            block, half = line // halves, line % halves
            for slot in range(0, wide, 16):
                rows = [plane_ref[pl.ds(cells[line, slot + step], 1), :] for step in range(16)]
                place = pl.ds(pl.multiple_of(half * wide + slot, 16), 16)
                out[block, place, :] = jnp.concatenate(rows, axis=0).astype(BF16)
            return carried

        lax.fori_loop(0, cells.shape[0], gather, 0)


def put_sum(slots, total, outs):
    high = total.astype(BF16).astype(F32)
    middle = (total - high).astype(BF16).astype(F32)
    low = total - high - middle
    row = lax.broadcasted_iota(I32, (TAIL, LANES), 0)
    tail = jnp.where(row == 0, high, jnp.where(row == 1, middle, jnp.where(row == 2, low, 0.0)))

    def one(ref, i, block, carried):
        ref[i, slots:] = tail.astype(BF16)
        return carried

    each(outs, None, one)


def pick_kernel(
    slots, chunks, plane_in, part_ref, lower_ref, upper_ref, off_ref, bottom_ref, prod_ref, *rest
):
    cell_refs = rest[:chunks]
    plane_ref, sum_ref = rest[chunks : chunks + 2]
    outs = rest[chunks + 2 :]
    segs = lower_ref.shape[0]
    first, last = pl.ds(0, segs), pl.ds(plane_ref.shape[0] - segs, segs)
    plane_ref[first, :] = plane_ref[first, :] + lower_ref[...]
    plane_ref[last, :] = plane_ref[last, :] + off_ref[...] * upper_ref[...]
    rims = bottom_ref[...] * lower_ref[...] + prod_ref[...] * upper_ref[...]
    total = jnp.sum(part_ref[...] + jnp.sum(rims, axis=0, keepdims=True), axis=1, keepdims=True)
    total = jnp.broadcast_to(total, (1, LANES))
    sum_ref[...] = total
    put_sum(slots, total, outs)
    gather_blocks(slots, plane_ref, cell_refs, outs)


def repick_kernel(slots, chunks, plane_ref, sum_ref, *rest):
    cell_refs, weighted_ref, outs, sem = rest[:chunks], rest[chunks], rest[chunks + 1 : -1], rest[-1]
    copy = pltpu.make_async_copy(plane_ref, weighted_ref, sem)
    copy.start()
    put_sum(slots, sum_ref[...], outs)
    gather_blocks(slots, plane_ref, cell_refs, outs)
    copy.wait()


def unpacked(slots, firsts, pos, chunks, total):
    lane = lax.broadcasted_iota(I32, pos.shape, 1).astype(F32)
    wide = min(slots, LANES)

    def one(ref, i, block, total):
        for start in range(0, slots, wide):
            base = jnp.asarray(block * slots + start, I32).astype(F32)
            chosen = (pos - base == lane).astype(F32).astype(BF16)
            total = total + jnp.dot(
                chosen[:, :wide], ref[i, start : start + wide], preferred_element_type=F32
            )
        return total

    return each(chunks, firsts, one, total)


def unpack_kernel(slots, firsts, pos_ref, *rest):
    chunks, (places_ref, total_ref) = rest[:-2], rest[-2:]
    count = pos_ref.shape[1]
    pos = jnp.transpose(jnp.broadcast_to(pos_ref[...], (LANES, count)).astype(F32))
    places_ref[...] = pos
    total_ref[...] = unpacked(slots, firsts, pos, chunks, jnp.zeros((count, LANES), F32))


def last_unpack_kernel(slots, firsts, places_ref, total_ref, *rest):
    chunks, out_ref = rest[:-1], rest[-1]
    out_ref[...] = unpacked(slots, firsts, places_ref[...], chunks, total_ref[...]).astype(BF16)


def sum_kernel(slots, after_ref, *rest):
    chunks, out_ref = rest[:-1], rest[-1]

    def one(ref, i, block, total):
        tail = ref[i, slots:].astype(F32)
        return total + tail[0:1] + tail[1:2] + tail[2:3]

    out_ref[...] = each(chunks, None, one, jnp.zeros((1, LANES), F32))


def shape_of(shape, dtype):
    return jax.ShapeDtypeStruct(shape, dtype)


def params(mib):
    return pltpu.CompilerParams(vmem_limit_bytes=mib << 20)


def in_hbm(*arrays):
    return [pltpu.with_memory_space_constraint(array, pltpu.HBM) for array in arrays]


def call(kernel, args, in_specs, out_shape, out_specs, scratch=(), aliases=None, us=1.0):
    return pl.pallas_call(
        kernel,
        out_shape=tuple(out_shape),
        in_specs=list(in_specs),
        out_specs=tuple(out_specs),
        scratch_shapes=list(scratch),
        input_output_aliases=aliases or {},
        compiler_params=params(8),
        cost_estimate=pl.CostEstimate(
            flops=0, bytes_accessed=int(us * HBM_BYTES_PER_US), transcendentals=0
        ),
    )(*args)


def shards(tdi_data, noise_diag, noise_off, src_blocks, owner_dev, layer_in, seg_in):
    groups = lax.axis_size("band") * lax.axis_size("tm")
    _, layers, segs, bins = tdi_data.shape
    count = src_blocks.shape[0]
    slots = 2 * count // groups
    halves = halves_of(slots)
    cell_count = layers * segs
    direct = groups == 8
    if direct:
        sizes, first_out, second_out = [1] * groups, [7, 6, 5, 4, 3, 2, 1, 0], []
        first_back, second_back = [7, 6, 5, 4, 3, 2, 1], [0]
        first_in, second_in = [0, 7, 6], [5, 4, 3, 2, 1]
        early, late = [0, 7, 6, 5, 4, 3], [2, 1]
    else:
        sizes, first_out, second_out = [groups], [0], []
        first_back, second_back = [0], []
        first_in, second_in = [0], []
        early, late = [], [0]
    total = len(sizes)

    def exchanged(number, block):
        if not direct:
            return lax.all_to_all(block, AXES, split_axis=0, concat_axis=0, tiled=True)
        if number == 0:
            return block
        return lax.ppermute(block, AXES, [(i, i ^ number) for i in range(groups)])

    blocks = [shape_of((size, slots + TAIL, bins), BF16) for size in sizes]
    plane = pltpu.VMEM((cell_count, bins), F32)
    rim = shape_of((segs, bins), F32)
    line = shape_of((1, bins), F32)
    tdi = tdi_data.reshape(cell_count, bins)
    diag = noise_diag.reshape(cell_count, bins)
    off = noise_off.reshape(cell_count, bins)

    arrived = [None] * total
    pos, names, src, *packed = call(
        functools.partial(pack_kernel, slots, groups, direct, first_out),
        in_hbm(
            owner_dev.reshape(1, count),
            layer_in.reshape(1, count),
            seg_in.reshape(1, count),
            src_blocks.reshape(count, bins),
        ),
        [HBM] * 4,
        [
            pltpu.VMEM((1, count), I32),
            pltpu.VMEM((TAIL, count), BF16),
            pltpu.VMEM((count, bins), BF16),
        ]
        + [blocks[k] for k in first_out],
        [VMEM] * (3 + len(first_out)),
        [pltpu.VMEM((1, count), I32)] * 3 + [pltpu.SemaphoreType.DMA((4,))],
        us=2.5,
    )
    for k, block in zip(first_out, packed):
        arrived[k] = exchanged(k, block)
    if second_out:
        packed = call(
            functools.partial(repack_kernel, slots, second_out),
            (arrived[first_out[0]], pos, names, src),
            [VMEM] * 4,
            [blocks[k] for k in second_out],
            [VMEM] * len(second_out),
        )
        for k, block in zip(second_out, packed):
            arrived[k] = exchanged(k, block)

    cells = [None] * total

    def scratch_of(step):
        size = sum(sizes[k] for k in step)
        return [
            pltpu.VMEM((size * slots, bins), F32),
            pltpu.SMEM((size * halves, LANES), I32),
            pltpu.SemaphoreType.DMA,
        ]

    def lines_of(step):
        return shape_of((sum(sizes[k] for k in step) * halves, LANES), I32)

    def split_lines(step, joined):
        start = 0
        for k in step:
            stop = start + sizes[k] * halves
            cells[k] = joined[start:stop]
            start = stop

    resid, extra, diag_in, off_in, low, high, off_last, joined = call(
        functools.partial(first_scatter_kernel, slots, segs),
        in_hbm(tdi, diag, off) + [arrived[k] for k in first_in],
        [HBM] * 3 + [VMEM] * len(first_in),
        [plane] * 4 + [rim] * 3 + [lines_of(first_in)],
        [VMEM] * 8,
        scratch_of(first_in) + [pltpu.SemaphoreType.DMA((3,))],
        us=5.0,
    )
    split_lines(first_in, joined)
    bottom, product = call(
        functools.partial(rim_kernel, slots, layers),
        (low, high, off_last, *arrived),
        [VMEM] * (3 + total),
        (rim, rim),
        (VMEM, VMEM),
        us=0.3,
    )
    lower_rim = passed_along(product, "band", 1)
    upper_rim = passed_along(bottom, "band", -1)
    if second_in:
        resid, extra, joined = call(
            functools.partial(scatter_kernel, slots, segs),
            [resid, extra] + [arrived[k] for k in second_in],
            [VMEM] * (2 + len(second_in)),
            [plane] * 2 + [lines_of(second_in)],
            [VMEM] * 3,
            scratch_of(second_in),
            {0: 0, 1: 1},
            us=4.0,
        )
        split_lines(second_in, joined)
    weighed, part = call(
        functools.partial(weigh_kernel, segs, layers),
        (resid, extra, diag_in, off_in),
        [VMEM] * 4,
        (plane, line),
        (VMEM, VMEM),
        us=2.4,
    )
    returned = [None] * total
    weighed, summed, *picked = call(
        functools.partial(pick_kernel, slots, len(first_back)),
        (weighed, part, lower_rim, upper_rim, off_last, bottom, product)
        + tuple(cells[k] for k in first_back),
        [VMEM] * 7 + [SMEM] * len(first_back),
        [plane, line] + [blocks[k] for k in first_back],
        [VMEM] * (2 + len(first_back)),
        aliases={0: 0},
        us=1.7,
    )
    for k, block in zip(first_back, picked):
        returned[k] = exchanged(k, block)
    weighted, *picked = call(
        functools.partial(repick_kernel, slots, len(second_back)),
        (weighed, summed)
        + tuple(cells[k] for k in second_back),
        [VMEM] * 2 + [SMEM] * len(second_back),
        [shape_of((cell_count, bins), F32)] + [blocks[k] for k in second_back],
        [HBM] + [VMEM] * len(second_back),
        [pltpu.SemaphoreType.DMA],
        us=2.0,
    )
    for k, block in zip(second_back, picked):
        returned[k] = exchanged(k, block)

    places, grads = call(
        functools.partial(unpack_kernel, slots, early),
        [pos] + [returned[k] for k in early],
        [VMEM] * (1 + len(early)),
        [pltpu.VMEM((count, LANES), F32)] * 2,
        (VMEM, VMEM),
    )
    (total_sum,) = call(
        functools.partial(sum_kernel, slots),
        [places] + returned,
        [VMEM] * (1 + total),
        (line,),
        (VMEM,),
        us=0.1,
    )
    chan = lax.axis_size("chan")
    other_sum = lax.ppermute(total_sum, "chan", [(i, i ^ 1) for i in range(chan)])
    cells_all = chan * groups * cell_count * bins
    log_like = (total_sum + other_sum)[0, :1] * (-0.5 / cells_all)
    (grads,) = call(
        functools.partial(last_unpack_kernel, slots, late),
        [places, grads] + [returned[k] for k in late],
        [VMEM] * (2 + len(late)),
        (shape_of((count, bins), BF16),),
        (VMEM,),
    )
    return (
        weighted.reshape(tdi_data.shape),
        log_like,
        grads.reshape(src_blocks.shape),
    )


def solution(mesh):
    planes = P(("grp", "chan"), "band", "tm", None)
    lists = P(("grp", "band", "tm"))
    return jax.shard_map(
        shards,
        mesh=mesh,
        in_specs=(
            planes,
            planes,
            planes,
            P(("grp", "band", "tm"), "chan", None),
            P(("grp", "band", "tm"), None),
            lists,
            lists,
        ),
        out_specs=(planes, P("grp"), P(("grp", "band", "tm"), "chan", None)),
        check_vma=False,
    )
```

time: 132 us -> 56.1 us (0.42)
  blocking collectives: 34.9 us -> 0 us
  other arithmetic: 32.9 us -> 0.01 us
  local copies, waits for them, and re-layouts: 22.7 us -> 0.01 us
  Pallas kernels: 0 us -> 21.1 us
  waiting for transfers between devices: 17.3 us -> 0.06 us
  starting transfers between devices: 20.7 us -> 32.4 us
    psum x1 -> x0, blocking collectives: 34.9 us -> none  [shards(): summed = lax.psum(partial_sum, ('band', 'tm', 'chan'))]
    ppermute x0 -> x15, starting transfers between devices: none -> 26.5 us  [the longest x14 26.5 us: exchanged(): return lax.ppermute(block, AXES, [(i, i ^ number) for i in range(groups)])]
    pallas_call x0 -> x10, Pallas kernels: none -> 21.1 us  [call(): pl.pallas_call(kernel, out_shape=tuple(out_shape), in_specs=list(in_specs...]
    all_to_all x3 -> x0, waiting for transfers between devices: 16.4 us -> none  [the longest x1 13.9 us: shards(): lax.all_to_all(outgoing, ('band', 'tm'), split_axis=0, concat_axis=0, til...]
    scatter-add x1 -> x0, other arithmetic: 14.4 us -> none  [shards(): jax.ops.segment_sum(arrived.astype(jnp.float32), home_cells, num_segments...]
    all_to_all x3 -> x0, starting transfers between devices: 14.2 us -> none  [the longest x1 7.25 us: shards(): lax.all_to_all(addresses, ('band', 'tm'), split_axis=0, concat_axis=0, ti...]
    gather x2 -> x0, local copies, waits for them, and re-layouts: 11 us -> none  [the longest x1 7.77 us: shards(): picked = jnp.take(flat_plane, home_cells, axis=0).astype(jnp.bfloat16)]
    scatter x2 -> x0, local copies, waits for them, and re-layouts: 8.86 us -> none  [the longest x1 4.88 us: shards(): jnp.zeros((groups * slots_per,), jnp.int32).at[position].set(cell_ids)]
  transfers between devices with their start and end apart: 5 -> 17, of which waited for: 3 -> 0; matrix products, arithmetic and copies ran while one was open for 4% -> 0% of each run, Pallas kernels for 0% -> 27%
where the time goes in v2:
time: 56.1 us; the launch traced here: 55.6 us
  starting transfers between devices  32.4 us (58%)
  Pallas kernels  21.1 us (38%)
  between operations  1.99 us (4%)
    ppermute x14, starting transfers between devices, exchanged(): return lax.ppermute(block, AXES, [(i, i ^ number) for i in range(groups)])  26.5 us
    pallas_call x10, Pallas kernels, call(): pl.pallas_call(kernel, out_shape=tuple(out_shape), in_specs=list(in_specs...  21.1 us
    ppermute x2, starting transfers between devices, passed_along(): lax.ppermute(value, axis, [(source, source + steps) for source in range(l...  5.87 us
  transfers between devices with their start and end apart: 17, of which 0 were waited for; matrix products, arithmetic and copies ran while one was open for 0% of the time, Pallas kernels for 27%

profile of v2, /device:TPU:0, one launch (start us, length us, event | category | flops | bytes accessed | tf_op | source)
XLA Modules:
  0.0 55.6 jit_solution(16689989442798288925)
XLA Ops:
  0.6 3.3 %shard_map.94 = (s32[1,1024]{1,0:T(1,128)S(1)}, bf16[16,1024]{1,0:T(8,128)(2,1)}, bf16[1024,128]{1,0:T(8,128)(2,1)}, bf16[1,272,128]{2,1,0:T(8,128)(2,1)S(1)}, b...) custom-call(s32[1,1024]{1,0:T(1,128)} %bitcast.16, ...), custom_call_target="tpu_custom_call" | custom-call | bytes 8250000 | tf_op jit(solution)/shard_map/pallas_call | solution.py:349
  4.0 6.0 %collective-permute-start = (bf16[1,272,128]{2,1,0:T(8,128)(2,1)S(1)}, bf16[1,272,128]{2,1,0:T(8,128)(2,1)S(1)}, u32[]{:S(2)}, u32[]{:S(2)}) collective-permute-start(bf16[1,272,128]{2,1,0:T(8,128)(2,1)S(1)} %get-tuple-element.41), channel_id=1, source_target_pairs={{0,14},{2,12},{4,10},{6,8},{8,6},{10,4},{12,2},{14,0},{1,15},{3,13... | collective-permute-start | bytes 208904 | tf_op jit(solution)/shard_map/ppermute | solution.py:388
  10.0 0.2 collective-permute-start.1
  10.2 0.8 %collective-permute-start.2 = (bf16[1,272,128]{2,1,0:T(8,128)(2,1)S(1)}, bf16[1,272,128]{2,1,0:T(8,128)(2,1)S(1)}, u32[]{:S(2)}, u32[]{:S(2)}) collective-permute-start(bf16[1,272,128]{2,1,0:T(8,128)(2,1)S(1)} %get-tuple-element.45), channel_id=1, source_target_pairs={{0,10},{2,8},{4,14},{6,12},{8,2},{10,0},{12,6},{14,4},{1,11},{3,9}... | collective-permute-start | bytes 208904 | tf_op jit(solution)/shard_map/ppermute | solution.py:388
  11.0 2.0 %collective-permute-start.3 = (bf16[1,272,128]{2,1,0:T(8,128)(2,1)S(1)}, bf16[1,272,128]{2,1,0:T(8,128)(2,1)S(1)}, u32[]{:S(2)}, u32[]{:S(2)}) collective-permute-start(bf16[1,272,128]{2,1,0:T(8,128)(2,1)S(1)} %get-tuple-element.46), channel_id=1, source_target_pairs={{0,8},{2,10},{4,12},{6,14},{8,0},{10,2},{12,4},{14,6},{1,9},{3,11}... | collective-permute-start | bytes 208904 | tf_op jit(solution)/shard_map/ppermute | solution.py:388
  13.0 2.3 %collective-permute-start.4 = (bf16[1,272,128]{2,1,0:T(8,128)(2,1)S(1)}, bf16[1,272,128]{2,1,0:T(8,128)(2,1)S(1)}, u32[]{:S(2)}, u32[]{:S(2)}) collective-permute-start(bf16[1,272,128]{2,1,0:T(8,128)(2,1)S(1)} %get-tuple-element.47), channel_id=1, source_target_pairs={{0,6},{2,4},{4,2},{6,0},{8,14},{10,12},{12,10},{14,8},{1,7},{3,5},... | collective-permute-start | bytes 208904 | tf_op jit(solution)/shard_map/ppermute | solution.py:388
  15.3 0.0 collective-permute-done.rest_1_.rest_7_
  15.3 1.4 %collective-permute-start.5 = (bf16[1,272,128]{2,1,0:T(8,128)(2,1)S(1)}, bf16[1,272,128]{2,1,0:T(8,128)(2,1)S(1)}, u32[]{:S(2)}, u32[]{:S(2)}) collective-permute-start(bf16[1,272,128]{2,1,0:T(8,128)(2,1)S(1)} %get-tuple-element.48), channel_id=1, source_target_pairs={{0,4},{2,6},{4,0},{6,2},{8,12},{10,14},{12,8},{14,10},{1,5},{3,7},... | collective-permute-start | bytes 208904 | tf_op jit(solution)/shard_map/ppermute | solution.py:388
  16.7 0.0 collective-permute-done.1.rest_2_.rest_6_
  16.7 0.5 collective-permute-start.6
  17.3 4.7 %shard_map.95 = (f32[8192,128]{1,0:T(8,128)S(1)}, f32[8192,128]{1,0:T(8,128)S(1)}, f32[8192,128]{1,0:T(8,128)S(1)}, f32[8192,128]{1,0:T(8,128)S(1)}, f32[64,128]...) custom-call(f32[8192,128]{1,0:T(8,128)} %bitcast.11, f32[8192,128]{1,0:T(8,128)} %bitcast.12, ...), custom_call_target="tpu_custom_call" | custom-call | bytes 16500000 | tf_op jit(solution)/shard_map/pallas_call | solution.py:349
  22.0 0.0 collective-permute-done.2.rest_0_.rest_5_
  22.0 0.0 collective-permute-done.3.rest_1_.rest_4_
  22.0 0.0 collective-permute-done.4.rest_2_.rest_3_
  22.0 0.0 collective-permute-done.5.rest_3_.rest_2_
  22.0 0.0 collective-permute-done.6.rest_4_.rest_1_
  22.0 0.3 shard_map.98
  22.3 4.6 %collective-permute-start.7 = (f32[64,128]{1,0:T(8,128)S(1)}, f32[64,128]{1,0:T(8,128)S(1)}, u32[]{:S(2)}, u32[]{:S(2)}) collective-permute-start(f32[64,128]{1,0:T(8,128)S(1)} %get-tuple-element.59.prod_ref), channel_id=1, source_target_pairs={{0,4},{4,8},{8,12},{1,5},{5,9},{9,13},{2,6},{6,10},{10,14},{3,7},{... | collective-permute-start | bytes 98312 | tf_op jit(solution)/shard_map/ppermute | solution.py:25
  26.9 1.3 %collective-permute-start.8 = (f32[64,128]{1,0:T(8,128)S(1)}, f32[64,128]{1,0:T(8,128)S(1)}, u32[]{:S(2)}, u32[]{:S(2)}) collective-permute-start(f32[64,128]{1,0:T(8,128)S(1)} %get-tuple-element.60.bottom_ref), channel_id=1, source_target_pairs={{4,0},{8,4},{12,8},{5,1},{9,5},{13,9},{6,2},{10,6},{14,10},{7,3},{... | collective-permute-start | bytes 98312 | tf_op jit(solution)/shard_map/ppermute | solution.py:25
  28.2 4.1 %shard_map.96 = (f32[8192,128]{1,0:T(8,128)S(1)}, f32[8192,128]{1,0:T(8,128)S(1)}, s32[10,128]{1,0:T(8,128)S(1)}) custom-call(f32[8192,128]{1,0:T(8,128)S(1)} %get-tuple-element.43.resid_in, f32[8192,128]{1,0:T(8,128)S(1)} %get-tuple-element.44.extra_in, ...), custom_call_target="tpu_custom_call", output_to_operand_aliasing={{0}: (0, {}), {1}: (1, {})} | custom-call | bytes 13200000 | tf_op jit(solution)/shard_map/pallas_call | solution.py:349
  32.4 1.4 %shard_map.97 = (f32[8192,128]{1,0:T(8,128)S(1)}, f32[1,128]{1,0:T(1,128)S(1)}) custom-call(f32[8192,128]{1,0:T(8,128)S(1)} %get-tuple-element.50.resid_ref, f32[8192,128]{1,0:T(8,128)S(1)} %get-tuple-element.51.extra_ref, f32[8192,128]{1,0:T(8,128)S(1)} %get-tuple-element.52.diag_ref, f32[8192,128]{1,0:T(8,128)S(1)} %get-tuple-element.53.off_ref), custom_call_target="tpu_custom_call" | custom-call | bytes 7920000 | tf_op jit(solution)/shard_map/pallas_call | solution.py:349
  33.8 0.0 collective-permute-done.7.lower_ref
  33.8 0.0 collective-permute-done.8.upper_ref
  33.8 2.5 %shard_map.99 = (f32[8192,128]{1,0:T(8,128)S(1)}, f32[1,128]{1,0:T(1,128)S(1)}, bf16[1,272,128]{2,1,0:T(8,128)(2,1)S(1)}, bf16[1,272,128]{2,1,0:T(8,128)(2,1)S(1...) custom-call(f32[8192,128]{1,0:T(8,128)S(1)} %get-tuple-element.54.pl, ...), custom_call_target="tpu_custom_call", output_to_operand_aliasing={{0}: (0, {})} | custom-call | bytes 5610000 | tf_op jit(solution)/shard_map/pallas_call | solution.py:349
  36.3 5.5 %collective-permute-start.9 = (bf16[1,272,128]{2,1,0:T(8,128)(2,1)S(1)}, bf16[1,272,128]{2,1,0:T(8,128)(2,1)S(1)}, u32[]{:S(2)}, u32[]{:S(2)}) collective-permute-start(bf16[1,272,128]{2,1,0:T(8,128)(2,1)S(1)} %get-tuple-element.68), channel_id=1, source_target_pairs={{0,14},{2,12},{4,10},{6,8},{8,6},{10,4},{12,2},{14,0},{1,15},{3,13... | collective-permute-start | bytes 208904 | tf_op jit(solution)/shard_map/ppermute | solution.py:388
  41.8 0.4 collective-permute-start.10
  42.2 2.3 %collective-permute-start.11 = (bf16[1,272,128]{2,1,0:T(8,128)(2,1)S(1)}, bf16[1,272,128]{2,1,0:T(8,128)(2,1)S(1)}, u32[]{:S(2)}, u32[]{:S(2)}) collective-permute-start(bf16[1,272,128]{2,1,0:T(8,128)(2,1)S(1)} %get-tuple-element.70), channel_id=1, source_target_pairs={{0,10},{2,8},{4,14},{6,12},{8,2},{10,0},{12,6},{14,4},{1,11},{3,9}... | collective-permute-start | bytes 208904 | tf_op jit(solution)/shard_map/ppermute | solution.py:388
  44.5 1.4 %collective-permute-start.12 = (bf16[1,272,128]{2,1,0:T(8,128)(2,1)S(1)}, bf16[1,272,128]{2,1,0:T(8,128)(2,1)S(1)}, u32[]{:S(2)}, u32[]{:S(2)}) collective-permute-start(bf16[1,272,128]{2,1,0:T(8,128)(2,1)S(1)} %get-tuple-element.71), channel_id=1, source_target_pairs={{0,8},{2,10},{4,12},{6,14},{8,0},{10,2},{12,4},{14,6},{1,9},{3,11}... | collective-permute-start | bytes 208904 | tf_op jit(solution)/shard_map/ppermute | solution.py:388
  45.9 1.5 %collective-permute-start.13 = (bf16[1,272,128]{2,1,0:T(8,128)(2,1)S(1)}, bf16[1,272,128]{2,1,0:T(8,128)(2,1)S(1)}, u32[]{:S(2)}, u32[]{:S(2)}) collective-permute-start(bf16[1,272,128]{2,1,0:T(8,128)(2,1)S(1)} %get-tuple-element.72), channel_id=1, source_target_pairs={{0,6},{2,4},{4,2},{6,0},{8,14},{10,12},{12,10},{14,8},{1,7},{3,5},... | collective-permute-start | bytes 208904 | tf_op jit(solution)/shard_map/ppermute | solution.py:388
  47.4 0.0 collective-permute-done.9.rest_1_.rest_7_
  47.4 1.5 %collective-permute-start.14 = (bf16[1,272,128]{2,1,0:T(8,128)(2,1)S(1)}, bf16[1,272,128]{2,1,0:T(8,128)(2,1)S(1)}, u32[]{:S(2)}, u32[]{:S(2)}) collective-permute-start(bf16[1,272,128]{2,1,0:T(8,128)(2,1)S(1)} %get-tuple-element.74), channel_id=1, source_target_pairs={{0,2},{2,0},{4,6},{6,4},{8,10},{10,8},{12,14},{14,12},{1,3},{3,1},... | collective-permute-start | bytes 208904 | tf_op jit(solution)/shard_map/ppermute | solution.py:388
  48.9 0.0 collective-permute-done.10.rest_2_.rest_6_
  48.9 0.6 %collective-permute-start.15 = (bf16[1,272,128]{2,1,0:T(8,128)(2,1)S(1)}, bf16[1,272,128]{2,1,0:T(8,128)(2,1)S(1)}, u32[]{:S(2)}, u32[]{:S(2)}) collective-permute-start(bf16[1,272,128]{2,1,0:T(8,128)(2,1)S(1)} %get-tuple-element.75), channel_id=1, source_target_pairs={{0,4},{2,6},{4,0},{6,2},{8,12},{10,14},{12,8},{14,10},{1,5},{3,7},... | collective-permute-start | bytes 208904 | tf_op jit(solution)/shard_map/ppermute | solution.py:388
  49.5 2.6 %shard_map.100 = (f32[8192,128]{1,0:T(8,128)}, bf16[1,272,128]{2,1,0:T(8,128)(2,1)S(1)}) custom-call(f32[8192,128]{1,0:T(8,128)S(1)} %get-tuple-element.63.plane_ref, f32[1,128]{1,0:T(1,128)S(1)} %get-tuple-element.64.sum_ref, s32[2,128]{1,0:T(2,128)S(1)} %get-tuple-element.87.rest_0_), custom_call_target="tpu_custom_call" | custom-call | bytes 6600000 | tf_op jit(solution)/shard_map/pallas_call | solution.py:349
  52.0 0.0 collective-permute-done.11.rest_3_.rest_5_
  52.1 0.0 collective-permute-done.12.rest_4_
  52.1 0.0 collective-permute-done.13.rest_5_.rest_3_
  52.1 1.1 %shard_map.101 = (f32[1024,128]{1,0:T(8,128)S(1)}, f32[1024,128]{1,0:T(8,128)S(1)}) custom-call(s32[1,1024]{1,0:T(1,128)S(1)} %get-tuple-element.66.pos_ref, bf16[1,272,128]{2,1,0:T(8,128)(2,1)S(1)} %get-tuple-element.67.rest_0_, bf16[1,272,128]{2,1,0:T(8,128)(2,1)S(1)} %collective-permute-done.9.rest_1_.rest_7_, ...), custom_call_target="tpu_custom_call" | custom-call | bytes 3300000 | tf_op jit(solution)/shard_map/pallas_call | solution.py:349
  53.1 0.0 collective-permute-done.14.rest_1_
  53.1 0.0 collective-permute-done.15.rest_2_.rest_0_
  53.2 0.1 collective-permute-start.16
  53.3 1.1 %shard_map.103 = bf16[1024,128]{1,0:T(8,128)(2,1)} custom-call(f32[1024,128]{1,0:T(8,128)S(1)} %get-tuple-element.73.after_ref.places_ref, f32[1024,128]{1,0:T(8,128)S(1)} %get-tuple-element.76.total_ref, bf16[1,272,128]{2,1,0:T(8,128)(2,1)S(1)} %collective-permute-done.15.rest_2_.rest_0_, bf16[1,272,128]{2,1,0:T(8,128)(2,1)S(1)} %collective-permute-done.14.rest_1_), custom_call_target="tpu_custom_call" | custom-call | bytes 3300000 | tf_op jit(solution)/shard_map/pallas_call | solution.py:349
  54.4 0.0 collective-permute-done.16
  (3 shorter events, 0.0 us)
Async XLA Ops:
  4.0 11.3 %collective-permute-start = (bf16[1,272,128]{2,1,0:T(8,128)(2,1)S(1)}, bf16[1,272,128]{2,1,0:T(8,128)(2,1)S(1)}, u32[]{:S(2)}, u32[]{:S(2)}) collective-permute-start(bf16[1,272,128]{2,1,0:T(8,128)(2,1)S(1)} %get-tuple-element.41), channel_id=1, source_target_pairs={{0,14},{2,12},{4,10},{6,8},{8,6},{10,4},{12,2},{14,0},{1,15},{3,13... | collective-permute-start | bytes 208904 | tf_op jit(solution)/shard_map/ppermute | solution.py:388
  10.0 6.7 %collective-permute-start.1 = (bf16[1,272,128]{2,1,0:T(8,128)(2,1)S(1)}, bf16[1,272,128]{2,1,0:T(8,128)(2,1)S(1)}, u32[]{:S(2)}, u32[]{:S(2)}) collective-permute-start(bf16[1,272,128]{2,1,0:T(8,128)(2,1)S(1)} %get-tuple-element.42), channel_id=1, source_target_pairs={{0,12},{2,14},{4,8},{6,10},{8,4},{10,6},{12,0},{14,2},{1,13},{3,15... | collective-permute-start | bytes 208904 | tf_op jit(solution)/shard_map/ppermute | solution.py:388
  10.2 11.8 %collective-permute-start.2 = (bf16[1,272,128]{2,1,0:T(8,128)(2,1)S(1)}, bf16[1,272,128]{2,1,0:T(8,128)(2,1)S(1)}, u32[]{:S(2)}, u32[]{:S(2)}) collective-permute-start(bf16[1,272,128]{2,1,0:T(8,128)(2,1)S(1)} %get-tuple-element.45), channel_id=1, source_target_pairs={{0,10},{2,8},{4,14},{6,12},{8,2},{10,0},{12,6},{14,4},{1,11},{3,9}... | collective-permute-start | bytes 208904 | tf_op jit(solution)/shard_map/ppermute | solution.py:388
  11.0 11.0 %collective-permute-start.3 = (bf16[1,272,128]{2,1,0:T(8,128)(2,1)S(1)}, bf16[1,272,128]{2,1,0:T(8,128)(2,1)S(1)}, u32[]{:S(2)}, u32[]{:S(2)}) collective-permute-start(bf16[1,272,128]{2,1,0:T(8,128)(2,1)S(1)} %get-tuple-element.46), channel_id=1, source_target_pairs={{0,8},{2,10},{4,12},{6,14},{8,0},{10,2},{12,4},{14,6},{1,9},{3,11}... | collective-permute-start | bytes 208904 | tf_op jit(solution)/shard_map/ppermute | solution.py:388
  13.0 9.0 %collective-permute-start.4 = (bf16[1,272,128]{2,1,0:T(8,128)(2,1)S(1)}, bf16[1,272,128]{2,1,0:T(8,128)(2,1)S(1)}, u32[]{:S(2)}, u32[]{:S(2)}) collective-permute-start(bf16[1,272,128]{2,1,0:T(8,128)(2,1)S(1)} %get-tuple-element.47), channel_id=1, source_target_pairs={{0,6},{2,4},{4,2},{6,0},{8,14},{10,12},{12,10},{14,8},{1,7},{3,5},... | collective-permute-start | bytes 208904 | tf_op jit(solution)/shard_map/ppermute | solution.py:388
  15.3 6.7 %collective-permute-start.5 = (bf16[1,272,128]{2,1,0:T(8,128)(2,1)S(1)}, bf16[1,272,128]{2,1,0:T(8,128)(2,1)S(1)}, u32[]{:S(2)}, u32[]{:S(2)}) collective-permute-start(bf16[1,272,128]{2,1,0:T(8,128)(2,1)S(1)} %get-tuple-element.48), channel_id=1, source_target_pairs={{0,4},{2,6},{4,0},{6,2},{8,12},{10,14},{12,8},{14,10},{1,5},{3,7},... | collective-permute-start | bytes 208904 | tf_op jit(solution)/shard_map/ppermute | solution.py:388
  16.7 5.3 %collective-permute-start.6 = (bf16[1,272,128]{2,1,0:T(8,128)(2,1)S(1)}, bf16[1,272,128]{2,1,0:T(8,128)(2,1)S(1)}, u32[]{:S(2)}, u32[]{:S(2)}) collective-permute-start(bf16[1,272,128]{2,1,0:T(8,128)(2,1)S(1)} %get-tuple-element.49), channel_id=1, source_target_pairs={{0,2},{2,0},{4,6},{6,4},{8,10},{10,8},{12,14},{14,12},{1,3},{3,1},... | collective-permute-start | bytes 208904 | tf_op jit(solution)/shard_map/ppermute | solution.py:388
  22.3 11.5 %collective-permute-start.7 = (f32[64,128]{1,0:T(8,128)S(1)}, f32[64,128]{1,0:T(8,128)S(1)}, u32[]{:S(2)}, u32[]{:S(2)}) collective-permute-start(f32[64,128]{1,0:T(8,128)S(1)} %get-tuple-element.59.prod_ref), channel_id=1, source_target_pairs={{0,4},{4,8},{8,12},{1,5},{5,9},{9,13},{2,6},{6,10},{10,14},{3,7},{... | collective-permute-start | bytes 98312 | tf_op jit(solution)/shard_map/ppermute | solution.py:25
  26.9 6.9 %collective-permute-start.8 = (f32[64,128]{1,0:T(8,128)S(1)}, f32[64,128]{1,0:T(8,128)S(1)}, u32[]{:S(2)}, u32[]{:S(2)}) collective-permute-start(f32[64,128]{1,0:T(8,128)S(1)} %get-tuple-element.60.bottom_ref), channel_id=1, source_target_pairs={{4,0},{8,4},{12,8},{5,1},{9,5},{13,9},{6,2},{10,6},{14,10},{7,3},{... | collective-permute-start | bytes 98312 | tf_op jit(solution)/shard_map/ppermute | solution.py:25
  36.3 11.1 %collective-permute-start.9 = (bf16[1,272,128]{2,1,0:T(8,128)(2,1)S(1)}, bf16[1,272,128]{2,1,0:T(8,128)(2,1)S(1)}, u32[]{:S(2)}, u32[]{:S(2)}) collective-permute-start(bf16[1,272,128]{2,1,0:T(8,128)(2,1)S(1)} %get-tuple-element.68), channel_id=1, source_target_pairs={{0,14},{2,12},{4,10},{6,8},{8,6},{10,4},{12,2},{14,0},{1,15},{3,13... | collective-permute-start | bytes 208904 | tf_op jit(solution)/shard_map/ppermute | solution.py:388
  41.8 7.0 %collective-permute-start.10 = (bf16[1,272,128]{2,1,0:T(8,128)(2,1)S(1)}, bf16[1,272,128]{2,1,0:T(8,128)(2,1)S(1)}, u32[]{:S(2)}, u32[]{:S(2)}) collective-permute-start(bf16[1,272,128]{2,1,0:T(8,128)(2,1)S(1)} %get-tuple-element.69), channel_id=1, source_target_pairs={{0,12},{2,14},{4,8},{6,10},{8,4},{10,6},{12,0},{14,2},{1,13},{3,15... | collective-permute-start | bytes 208904 | tf_op jit(solution)/shard_map/ppermute | solution.py:388
  42.2 9.8 %collective-permute-start.11 = (bf16[1,272,128]{2,1,0:T(8,128)(2,1)S(1)}, bf16[1,272,128]{2,1,0:T(8,128)(2,1)S(1)}, u32[]{:S(2)}, u32[]{:S(2)}) collective-permute-start(bf16[1,272,128]{2,1,0:T(8,128)(2,1)S(1)} %get-tuple-element.70), channel_id=1, source_target_pairs={{0,10},{2,8},{4,14},{6,12},{8,2},{10,0},{12,6},{14,4},{1,11},{3,9}... | collective-permute-start | bytes 208904 | tf_op jit(solution)/shard_map/ppermute | solution.py:388
  44.5 7.5 %collective-permute-start.12 = (bf16[1,272,128]{2,1,0:T(8,128)(2,1)S(1)}, bf16[1,272,128]{2,1,0:T(8,128)(2,1)S(1)}, u32[]{:S(2)}, u32[]{:S(2)}) collective-permute-start(bf16[1,272,128]{2,1,0:T(8,128)(2,1)S(1)} %get-tuple-element.71), channel_id=1, source_target_pairs={{0,8},{2,10},{4,12},{6,14},{8,0},{10,2},{12,4},{14,6},{1,9},{3,11}... | collective-permute-start | bytes 208904 | tf_op jit(solution)/shard_map/ppermute | solution.py:388
  45.9 6.1 %collective-permute-start.13 = (bf16[1,272,128]{2,1,0:T(8,128)(2,1)S(1)}, bf16[1,272,128]{2,1,0:T(8,128)(2,1)S(1)}, u32[]{:S(2)}, u32[]{:S(2)}) collective-permute-start(bf16[1,272,128]{2,1,0:T(8,128)(2,1)S(1)} %get-tuple-element.72), channel_id=1, source_target_pairs={{0,6},{2,4},{4,2},{6,0},{8,14},{10,12},{12,10},{14,8},{1,7},{3,5},... | collective-permute-start | bytes 208904 | tf_op jit(solution)/shard_map/ppermute | solution.py:388
  47.4 5.7 %collective-permute-start.14 = (bf16[1,272,128]{2,1,0:T(8,128)(2,1)S(1)}, bf16[1,272,128]{2,1,0:T(8,128)(2,1)S(1)}, u32[]{:S(2)}, u32[]{:S(2)}) collective-permute-start(bf16[1,272,128]{2,1,0:T(8,128)(2,1)S(1)} %get-tuple-element.74), channel_id=1, source_target_pairs={{0,2},{2,0},{4,6},{6,4},{8,10},{10,8},{12,14},{14,12},{1,3},{3,1},... | collective-permute-start | bytes 208904 | tf_op jit(solution)/shard_map/ppermute | solution.py:388
  48.9 4.3 %collective-permute-start.15 = (bf16[1,272,128]{2,1,0:T(8,128)(2,1)S(1)}, bf16[1,272,128]{2,1,0:T(8,128)(2,1)S(1)}, u32[]{:S(2)}, u32[]{:S(2)}) collective-permute-start(bf16[1,272,128]{2,1,0:T(8,128)(2,1)S(1)} %get-tuple-element.75), channel_id=1, source_target_pairs={{0,4},{2,6},{4,0},{6,2},{8,12},{10,14},{12,8},{14,10},{1,5},{3,7},... | collective-permute-start | bytes 208904 | tf_op jit(solution)/shard_map/ppermute | solution.py:388
  53.2 1.2 %collective-permute-start.16 = (f32[1,128]{1,0:T(1,128)S(1)}, f32[1,128]{1,0:T(1,128)S(1)}, u32[]{:S(2)}, u32[]{:S(2)}) collective-permute-start(f32[1,128]{1,0:T(1,128)S(1)} %shard_map.102), channel_id=1, source_target_pairs={{0,1},{1,0},{2,3},{3,2},{4,5},{5,4},{6,7},{7,6},{8,9},{9,8},{10,11... | collective-permute-start | bytes 1544 | tf_op jit(solution)/shard_map/ppermute | solution.py:533

commit v3 on v2

--- a/solution.py
+++ b/solution.py
@@ -48,36 +48,11 @@
     return carried
 
 
-def pack_blocks(slots, firsts, pos, names, src_ref, outs):
-    count = pos.shape[1]
-    slot = lax.broadcasted_iota(I32, (max(slots, LANES), count), 0)
-    tail_row = lax.broadcasted_iota(I32, (TAIL, LANES), 0)
-
-    def one(ref, i, block, carried):
-        chosen = (slot == pos - block * slots).astype(F32).astype(BF16)
-        if slots < LANES:
-            chosen = jnp.where(slot < slots, chosen, jnp.zeros_like(chosen))
-        rows = jnp.dot(chosen[:slots], src_ref[...], preferred_element_type=F32)
-        cells = lax.dot_general(
-            names, chosen, (((1,), (1,)), ((), ())), preferred_element_type=F32
-        )
-        tail = cells[:, :LANES]
-        for half in range(1, halves_of(slots)):
-            tail = jnp.where(
-                tail_row < 2 * half, tail, cells[:, half * LANES : (half + 1) * LANES]
-            )
-        ref[i, :slots] = rows.astype(BF16)
-        ref[i, slots:] = tail.astype(BF16)
-        return carried
-
-    each(outs, firsts, one)
-
-
 def pack_kernel(
-    slots, groups, direct, firsts, own_hbm, layer_hbm, seg_hbm, src_hbm,
-    pos_ref, names_ref, src_ref, *rest,
+    slots, groups, direct, firsts, own_hbm, layer_hbm, seg_hbm, src_hbm, pos_ref, *rest
 ):
-    outs, (own_ref, layer_ref, seg_ref, sems) = rest[:-4], rest[-4:]
+    outs, (own_ref, layer_ref, seg_ref, wide_ref, sems) = rest[:-5], rest[-5:]
+    src_ref = wide_ref.at[:, pl.ds(0, LANES)]
     copies = [
         pltpu.make_async_copy(source, target, sems.at[i])
         for i, (source, target) in enumerate(
@@ -106,16 +81,42 @@
         carry = carry + jnp.sum(part, axis=1, keepdims=True)
     pos = own * slots + jnp.concatenate(ranks, axis=1).astype(I32)
     pos_ref[...] = pos
-    for copy in copies[1:]:
-        copy.wait()
-    even = lax.broadcasted_iota(I32, (TAIL, count), 0) % 2 == 0
-    names = jnp.where(even, layer_ref[...], seg_ref[...]).astype(F32).astype(BF16)
-    names_ref[...] = names
-    pack_blocks(slots, firsts, pos, names, src_ref, outs)
-
-
-def repack_kernel(slots, firsts, after_ref, pos_ref, names_ref, src_ref, *outs):
-    pack_blocks(slots, firsts, pos_ref[...], names_ref[...], src_ref, outs)
+    copies[1].wait()
+    copies[2].wait()
+    even = lax.broadcasted_iota(I32, (LANES, count), 0) % 2 == 0
+    names = jnp.where(even, layer_ref[...], seg_ref[...]).astype(F32)
+    wide_ref[:, LANES:] = jnp.transpose(names).astype(BF16)
+    copies[3].wait()
+    tall = max(slots, LANES)
+    slot = lax.broadcasted_iota(I32, (tall, count), 0)
+    lane_pair = lax.broadcasted_iota(I32, (tall, LANES), 1) // 2
+    tail_row = lax.broadcasted_iota(I32, (TAIL, LANES), 0)
+
+    def tail_of(named, row):
+        tail = jnp.zeros((TAIL, LANES), F32)
+        for half in range(halves_of(slots)):
+            pair = named[row : row + 2, half * LANES : (half + 1) * LANES]
+            for i in range(2):
+                tail = jnp.where(tail_row == 2 * half + i, pair[i : i + 1], tail)
+        return tail.astype(BF16)
+
+    def one(ref, i, block, named):
+        chosen = (slot == pos - block * slots).astype(F32).astype(BF16)
+        if slots < LANES:
+            chosen = jnp.where(slot < slots, chosen, jnp.zeros_like(chosen))
+        found = jnp.dot(chosen, wide_ref[...], preferred_element_type=F32)
+        ref[i, :slots] = found[:slots, :LANES].astype(BF16)
+        if few(groups):
+            return jnp.where(lane_pair == block, found[:, LANES:], named)
+        ref[i, slots:] = tail_of(jnp.transpose(found[:, LANES:]), 0)
+        return named
+
+    named = each(outs, firsts, one, jnp.zeros((tall, LANES), F32))
+    if few(groups):
+        named = jnp.transpose(named)
+        for ref, first in zip(outs, firsts):
+            for i in range(ref.shape[0]):
+                ref[i, slots:] = tail_of(named, 2 * (first + i))
 
 
 def cells_of(ref, i, slots, segs):
@@ -170,47 +171,57 @@
     copy.wait()
 
     def scatter(line, carried):
-        for slot in range(0, wide, 2):
+        for slot in range(0, wide, 4):
+            turns = []
             for step, plane in enumerate((resid_ref, extra_ref)):
-                place = pl.ds(cells[line, slot + step], 1)
-                plane[place, :] = plane[place, :] - blocks[
-                    pl.ds(line * wide + slot + step, 1), :
-                ]
+                one, two = cells[line, slot + step], cells[line, slot + step + 2]
+                first = blocks[pl.ds(line * wide + slot + step, 1), :]
+                second = blocks[pl.ds(line * wide + slot + step + 2, 1), :]
+                second = second + jnp.where(one == two, first, 0.0)
+                one, two = pl.ds(one, 1), pl.ds(two, 1)
+                turns.append((plane, one, two, plane[one, :] - first, plane[two, :] - second))
+            for plane, one, two, first, second in turns:
+                plane[one, :] = first
+                plane[two, :] = second
         return carried
 
     lax.fori_loop(0, cell_ref.shape[0], scatter, 0)
 
 
-def first_scatter_kernel(slots, segs, tdi_hbm, diag_hbm, off_hbm, *rest):
-    chunks, outs, (blocks, cells, sem, sems) = rest[:-12], rest[-12:-4], rest[-4:]
-    resid_ref, extra_ref, diag_ref, off_ref, low_ref, high_ref, last_ref, cell_ref = outs
+def first_scatter_kernel(slots, segs, tdi_hbm, off_hbm, *rest):
+    chunks, outs, (blocks, cells, sem, sems) = rest[:-10], rest[-10:-4], rest[-4:]
+    resid_ref, extra_ref, low_ref, high_ref, last_ref, cell_ref = outs
     size = resid_ref.shape[0]
+    copy = pltpu.make_async_copy(tdi_hbm, resid_ref, sems.at[0])
+    copy_last = pltpu.make_async_copy(off_hbm.at[pl.ds(size - segs, segs)], last_ref, sems.at[1])
+    copy_last.start()
+    copy.start()
+
+    def ready():
+        extra_ref[...] = jnp.zeros_like(extra_ref)
+        copy_last.wait()
+        copy.wait()
+        low_ref[...] = resid_ref[:segs]
+        high_ref[...] = resid_ref[size - segs :]
+
+    scatter_blocks(slots, segs, chunks, resid_ref, extra_ref, cell_ref, blocks, cells, sem, ready)
+
+
+def scatter_kernel(slots, segs, resid_in, extra_in, diag_hbm, off_hbm, *rest):
+    chunks, outs, (blocks, cells, sem, sems) = rest[:-9], rest[-9:-4], rest[-4:]
+    resid_ref, extra_ref, diag_ref, off_ref, cell_ref = outs
     copies = [
-        pltpu.make_async_copy(source, target, sems.at[i])
-        for i, (source, target) in enumerate(
-            ((tdi_hbm, resid_ref), (diag_hbm, diag_ref), (off_hbm, off_ref))
-        )
+        pltpu.make_async_copy(diag_hbm, diag_ref, sems.at[0]),
+        pltpu.make_async_copy(off_hbm, off_ref, sems.at[1]),
     ]
     for copy in copies:
         copy.start()
-
-    def ready():
-        extra_ref[...] = jnp.zeros_like(extra_ref)
-        copies[0].wait()
-        low_ref[...] = resid_ref[:segs]
-        high_ref[...] = resid_ref[size - segs :]
-
-    scatter_blocks(slots, segs, chunks, resid_ref, extra_ref, cell_ref, blocks, cells, sem, ready)
-    for copy in copies[1:]:
+    if chunks:
+        scatter_blocks(
+            slots, segs, chunks, resid_ref, extra_ref, cell_ref, blocks, cells, sem, lambda: None
+        )
+    for copy in copies:
         copy.wait()
-    last_ref[...] = off_ref[size - segs :]
-
-
-def scatter_kernel(slots, segs, resid_in, extra_in, *rest):
-    chunks, (resid_ref, extra_ref, cell_ref, blocks, cells, sem) = rest[:-6], rest[-6:]
-    scatter_blocks(
-        slots, segs, chunks, resid_ref, extra_ref, cell_ref, blocks, cells, sem, lambda: None
-    )
 
 
 def weigh_kernel(segs, layers, resid_ref, extra_ref, diag_ref, off_ref, plane_ref, part_ref):
@@ -271,27 +282,27 @@
     slots, chunks, plane_in, part_ref, lower_ref, upper_ref, off_ref, bottom_ref, prod_ref, *rest
 ):
     cell_refs = rest[:chunks]
-    plane_ref, sum_ref = rest[chunks : chunks + 2]
-    outs = rest[chunks + 2 :]
+    plane_ref, weighted_ref, sum_ref = rest[chunks : chunks + 3]
+    outs, sem = rest[chunks + 3 : -1], rest[-1]
     segs = lower_ref.shape[0]
     first, last = pl.ds(0, segs), pl.ds(plane_ref.shape[0] - segs, segs)
     plane_ref[first, :] = plane_ref[first, :] + lower_ref[...]
     plane_ref[last, :] = plane_ref[last, :] + off_ref[...] * upper_ref[...]
+    copy = pltpu.make_async_copy(plane_ref, weighted_ref, sem)
+    copy.start()
     rims = bottom_ref[...] * lower_ref[...] + prod_ref[...] * upper_ref[...]
     total = jnp.sum(part_ref[...] + jnp.sum(rims, axis=0, keepdims=True), axis=1, keepdims=True)
     total = jnp.broadcast_to(total, (1, LANES))
     sum_ref[...] = total
     put_sum(slots, total, outs)
     gather_blocks(slots, plane_ref, cell_refs, outs)
+    copy.wait()
 
 
 def repick_kernel(slots, chunks, plane_ref, sum_ref, *rest):
-    cell_refs, weighted_ref, outs, sem = rest[:chunks], rest[chunks], rest[chunks + 1 : -1], rest[-1]
-    copy = pltpu.make_async_copy(plane_ref, weighted_ref, sem)
-    copy.start()
+    cell_refs, outs = rest[:chunks], rest[chunks:]
     put_sum(slots, sum_ref[...], outs)
     gather_blocks(slots, plane_ref, cell_refs, outs)
-    copy.wait()
 
 
 def unpacked(slots, firsts, pos, chunks, total):
@@ -369,12 +380,12 @@
     cell_count = layers * segs
     direct = groups == 8
     if direct:
-        sizes, first_out, second_out = [1] * groups, [7, 6, 5, 4, 3, 2, 1, 0], []
+        sizes, first_out = [1] * groups, [7, 6, 5, 4, 3, 2, 1, 0]
         first_back, second_back = [7, 6, 5, 4, 3, 2, 1], [0]
         first_in, second_in = [0, 7, 6], [5, 4, 3, 2, 1]
-        early, late = [0, 7, 6, 5, 4, 3], [2, 1]
+        early, late = [0, 7, 6, 5], [4, 3, 2, 1]
     else:
-        sizes, first_out, second_out = [groups], [0], []
+        sizes, first_out = [groups], [0]
         first_back, second_back = [0], []
         first_in, second_in = [0], []
         early, late = [], [0]
@@ -396,7 +407,7 @@
     off = noise_off.reshape(cell_count, bins)
 
     arrived = [None] * total
-    pos, names, src, *packed = call(
+    pos, *packed = call(
         functools.partial(pack_kernel, slots, groups, direct, first_out),
         in_hbm(
             owner_dev.reshape(1, count),
@@ -405,28 +416,14 @@
             src_blocks.reshape(count, bins),
         ),
         [HBM] * 4,
-        [
-            pltpu.VMEM((1, count), I32),
-            pltpu.VMEM((TAIL, count), BF16),
-            pltpu.VMEM((count, bins), BF16),
-        ]
-        + [blocks[k] for k in first_out],
-        [VMEM] * (3 + len(first_out)),
-        [pltpu.VMEM((1, count), I32)] * 3 + [pltpu.SemaphoreType.DMA((4,))],
-        us=2.5,
+        [pltpu.VMEM((1, count), I32)] + [blocks[k] for k in first_out],
+        [VMEM] * (1 + len(first_out)),
+        [pltpu.VMEM((1, count), I32)] * 3
+        + [pltpu.VMEM((count, 2 * bins), BF16), pltpu.SemaphoreType.DMA((4,))],
+        us=3.0,
     )
     for k, block in zip(first_out, packed):
         arrived[k] = exchanged(k, block)
-    if second_out:
-        packed = call(
-            functools.partial(repack_kernel, slots, second_out),
-            (arrived[first_out[0]], pos, names, src),
-            [VMEM] * 4,
-            [blocks[k] for k in second_out],
-            [VMEM] * len(second_out),
-        )
-        for k, block in zip(second_out, packed):
-            arrived[k] = exchanged(k, block)
 
     cells = [None] * total
 
@@ -448,19 +445,19 @@
             cells[k] = joined[start:stop]
             start = stop
 
-    resid, extra, diag_in, off_in, low, high, off_last, joined = call(
+    resid, extra, low, high, off_last, joined = call(
         functools.partial(first_scatter_kernel, slots, segs),
-        in_hbm(tdi, diag, off) + [arrived[k] for k in first_in],
-        [HBM] * 3 + [VMEM] * len(first_in),
-        [plane] * 4 + [rim] * 3 + [lines_of(first_in)],
-        [VMEM] * 8,
-        scratch_of(first_in) + [pltpu.SemaphoreType.DMA((3,))],
-        us=5.0,
+        in_hbm(tdi, off) + [arrived[k] for k in first_in],
+        [HBM] * 2 + [VMEM] * len(first_in),
+        [plane] * 2 + [rim] * 3 + [lines_of(first_in)],
+        [VMEM] * 6,
+        scratch_of(first_in) + [pltpu.SemaphoreType.DMA((2,))],
+        us=3.0,
     )
     split_lines(first_in, joined)
     bottom, product = call(
         functools.partial(rim_kernel, slots, layers),
-        (low, high, off_last, *arrived),
+        [low, high, off_last, *arrived],
         [VMEM] * (3 + total),
         (rim, rim),
         (VMEM, VMEM),
@@ -468,17 +465,18 @@
     )
     lower_rim = passed_along(product, "band", 1)
     upper_rim = passed_along(bottom, "band", -1)
+    step = second_in or [0]
+    resid, extra, diag_in, off_in, joined = call(
+        functools.partial(scatter_kernel, slots, segs),
+        [resid, extra] + in_hbm(diag, off) + [arrived[k] for k in second_in],
+        [VMEM] * 2 + [HBM] * 2 + [VMEM] * len(second_in),
+        [plane] * 4 + [lines_of(step)],
+        [VMEM] * 5,
+        scratch_of(step) + [pltpu.SemaphoreType.DMA((2,))],
+        {0: 0, 1: 1},
+        us=3.5,
+    )
     if second_in:
-        resid, extra, joined = call(
-            functools.partial(scatter_kernel, slots, segs),
-            [resid, extra] + [arrived[k] for k in second_in],
-            [VMEM] * (2 + len(second_in)),
-            [plane] * 2 + [lines_of(second_in)],
-            [VMEM] * 3,
-            scratch_of(second_in),
-            {0: 0, 1: 1},
-            us=4.0,
-        )
         split_lines(second_in, joined)
     weighed, part = call(
         functools.partial(weigh_kernel, segs, layers),
@@ -489,30 +487,30 @@
         us=2.4,
     )
     returned = [None] * total
-    weighed, summed, *picked = call(
+    weighed, weighted, summed, *picked = call(
         functools.partial(pick_kernel, slots, len(first_back)),
         (weighed, part, lower_rim, upper_rim, off_last, bottom, product)
         + tuple(cells[k] for k in first_back),
         [VMEM] * 7 + [SMEM] * len(first_back),
-        [plane, line] + [blocks[k] for k in first_back],
-        [VMEM] * (2 + len(first_back)),
-        aliases={0: 0},
-        us=1.7,
+        [plane, shape_of((cell_count, bins), F32), line] + [blocks[k] for k in first_back],
+        [VMEM, HBM, VMEM] + [VMEM] * len(first_back),
+        [pltpu.SemaphoreType.DMA],
+        {0: 0},
+        us=2.5,
     )
     for k, block in zip(first_back, picked):
         returned[k] = exchanged(k, block)
-    weighted, *picked = call(
-        functools.partial(repick_kernel, slots, len(second_back)),
-        (weighed, summed)
-        + tuple(cells[k] for k in second_back),
-        [VMEM] * 2 + [SMEM] * len(second_back),
-        [shape_of((cell_count, bins), F32)] + [blocks[k] for k in second_back],
-        [HBM] + [VMEM] * len(second_back),
-        [pltpu.SemaphoreType.DMA],
-        us=2.0,
-    )
-    for k, block in zip(second_back, picked):
-        returned[k] = exchanged(k, block)
+    if second_back:
+        picked = call(
+            functools.partial(repick_kernel, slots, len(second_back)),
+            (weighed, summed) + tuple(cells[k] for k in second_back),
+            [VMEM] * 2 + [SMEM] * len(second_back),
+            [blocks[k] for k in second_back],
+            [VMEM] * len(second_back),
+            us=0.5,
+        )
+        for k, block in zip(second_back, picked):
+            returned[k] = exchanged(k, block)
 
     places, grads = call(
         functools.partial(unpack_kernel, slots, early),

time: 56.1 us -> 54.2 us (0.966)
  Pallas kernels: 21.1 us -> 17 us
  waiting for transfers between devices: 0.06 us -> 2.24 us
    pallas_call x10, Pallas kernels: 21.1 us -> 17 us  [call(): pl.pallas_call(kernel, out_shape=tuple(out_shape), in_specs=list(in_specs...]
    ppermute x14, waiting for transfers between devices: 0.06 us -> 2.23 us  [exchanged(): return lax.ppermute(block, AXES, [(i, i ^ number) for i in range(groups)])]
    ppermute x14, starting transfers between devices: 26.5 us -> 27.1 us  [exchanged(): return lax.ppermute(block, AXES, [(i, i ^ number) for i in range(groups)])]
  transfers between devices with their start and end apart: 17 -> 17, of which waited for: 0 -> 4; matrix products, arithmetic and copies ran while one was open for 0% -> 0% of each run, Pallas kernels for 27% -> 22%
where the time goes in v3:
time: 54.2 us; the launch traced here: 53.9 us
  starting transfers between devices  32.7 us (60%)
  Pallas kernels  17 us (31%)
  waiting for transfers between devices  2.24 us (4%)
  between operations  1.95 us (4%)
    ppermute x14, starting transfers between devices, exchanged(): return lax.ppermute(block, AXES, [(i, i ^ number) for i in range(groups)])  27.1 us
    pallas_call x10, Pallas kernels, call(): pl.pallas_call(kernel, out_shape=tuple(out_shape), in_specs=list(in_specs...  17 us
    ppermute x2, starting transfers between devices, passed_along(): lax.ppermute(value, axis, [(source, source + steps) for source in range(l...  5.47 us
    ppermute x14, waiting for transfers between devices, exchanged(): return lax.ppermute(block, AXES, [(i, i ^ number) for i in range(groups)])  2.23 us
  transfers between devices with their start and end apart: 17, of which 4 were waited for; matrix products, arithmetic and copies ran while one was open for 0% of the time, Pallas kernels for 22%

profile of v3, /device:TPU:0, one launch (start us, length us, event | category | flops | bytes accessed | tf_op | source)
XLA Modules:
  0.0 53.9 jit_solution(7156715909321439857)
XLA Ops:
  0.6 2.4 %shard_map.94 = (s32[1,1024]{1,0:T(1,128)S(1)}, bf16[1,272,128]{2,1,0:T(8,128)(2,1)S(1)}, bf16[1,272,128]{2,1,0:T(8,128)(2,1)S(1)}, bf16[1,272,128]{2,1,0:T(8,12...) custom-call(s32[1,1024]{1,0:T(1,128)} %bitcast.17, ...), custom_call_target="tpu_custom_call" | custom-call | bytes 9900000 | tf_op jit(solution)/shard_map/pallas_call | solution.py:360
  3.0 6.0 %collective-permute-start = (bf16[1,272,128]{2,1,0:T(8,128)(2,1)S(1)}, bf16[1,272,128]{2,1,0:T(8,128)(2,1)S(1)}, u32[]{:S(2)}, u32[]{:S(2)}) collective-permute-start(bf16[1,272,128]{2,1,0:T(8,128)(2,1)S(1)} %get-tuple-element.40), channel_id=1, source_target_pairs={{0,14},{2,12},{4,10},{6,8},{8,6},{10,4},{12,2},{14,0},{1,15},{3,13... | collective-permute-start | bytes 208904 | tf_op jit(solution)/shard_map/ppermute | solution.py:399
  9.0 0.2 collective-permute-start.1
  9.3 0.8 %collective-permute-start.2 = (bf16[1,272,128]{2,1,0:T(8,128)(2,1)S(1)}, bf16[1,272,128]{2,1,0:T(8,128)(2,1)S(1)}, u32[]{:S(2)}, u32[]{:S(2)}) collective-permute-start(bf16[1,272,128]{2,1,0:T(8,128)(2,1)S(1)} %get-tuple-element.44), channel_id=1, source_target_pairs={{0,10},{2,8},{4,14},{6,12},{8,2},{10,0},{12,6},{14,4},{1,11},{3,9}... | collective-permute-start | bytes 208904 | tf_op jit(solution)/shard_map/ppermute | solution.py:399
  10.0 2.0 %collective-permute-start.3 = (bf16[1,272,128]{2,1,0:T(8,128)(2,1)S(1)}, bf16[1,272,128]{2,1,0:T(8,128)(2,1)S(1)}, u32[]{:S(2)}, u32[]{:S(2)}) collective-permute-start(bf16[1,272,128]{2,1,0:T(8,128)(2,1)S(1)} %get-tuple-element.45), channel_id=1, source_target_pairs={{0,8},{2,10},{4,12},{6,14},{8,0},{10,2},{12,4},{14,6},{1,9},{3,11}... | collective-permute-start | bytes 208904 | tf_op jit(solution)/shard_map/ppermute | solution.py:399
  12.0 2.3 %collective-permute-start.4 = (bf16[1,272,128]{2,1,0:T(8,128)(2,1)S(1)}, bf16[1,272,128]{2,1,0:T(8,128)(2,1)S(1)}, u32[]{:S(2)}, u32[]{:S(2)}) collective-permute-start(bf16[1,272,128]{2,1,0:T(8,128)(2,1)S(1)} %get-tuple-element.46), channel_id=1, source_target_pairs={{0,6},{2,4},{4,2},{6,0},{8,14},{10,12},{12,10},{14,8},{1,7},{3,5},... | collective-permute-start | bytes 208904 | tf_op jit(solution)/shard_map/ppermute | solution.py:399
  14.3 0.0 collective-permute-done.rest_1_.rest_7_
  14.3 1.4 %collective-permute-start.5 = (bf16[1,272,128]{2,1,0:T(8,128)(2,1)S(1)}, bf16[1,272,128]{2,1,0:T(8,128)(2,1)S(1)}, u32[]{:S(2)}, u32[]{:S(2)}) collective-permute-start(bf16[1,272,128]{2,1,0:T(8,128)(2,1)S(1)} %get-tuple-element.47), channel_id=1, source_target_pairs={{0,4},{2,6},{4,0},{6,2},{8,12},{10,14},{12,8},{14,10},{1,5},{3,7},... | collective-permute-start | bytes 208904 | tf_op jit(solution)/shard_map/ppermute | solution.py:399
  15.8 0.0 collective-permute-done.1.rest_2_.rest_6_
  15.8 0.5 collective-permute-start.6
  16.3 3.7 %shard_map.95 = (f32[8192,128]{1,0:T(8,128)S(1)}, f32[8192,128]{1,0:T(8,128)S(1)}, f32[64,128]{1,0:T(8,128)S(1)}, f32[64,128]{1,0:T(8,128)S(1)}, f32[64,128]{1,0:T(8,128)S(1)}, /*index=5*/s32[6,128]{1,0:T(8,128)S(1)}) custom-call(f32[8192,128]{1,0:T(8,128)} %bitcast.13, f32[8192,128]{1,0:T(8,128)} %bitcast.11, ...), custom_call_target="tpu_custom_call" | custom-call | bytes 9900000 | tf_op jit(solution)/shard_map/pallas_call | solution.py:360
  20.1 0.0 collective-permute-done.2.rest_0_.rest_5_
  20.1 0.9 %collective-permute-done.3.rest_1_.rest_4_ = bf16[1,272,128]{2,1,0:T(8,128)(2,1)S(1)} collective-permute-done((bf16[1,272,128]{2,1,0:T(8,128)(2,1)S(1)}, bf16[1,272,128]{2,1,0:T(8,128)(2,1)S(1)}, u32[]{:S(2)}, u32[]{:S(2)}) %collective-permute-start.3) | collective-permute-done | bytes 69664 | tf_op jit(solution)/shard_map/ppermute | solution.py:399
  21.0 0.0 collective-permute-done.4.rest_2_.rest_3_
  21.0 0.1 collective-permute-done.5.rest_3_.rest_2_
  21.0 0.0 collective-permute-done.6.rest_4_.rest_1_
  21.0 0.3 shard_map.98
  21.3 4.2 %collective-permute-start.7 = (f32[64,128]{1,0:T(8,128)S(1)}, f32[64,128]{1,0:T(8,128)S(1)}, u32[]{:S(2)}, u32[]{:S(2)}) collective-permute-start(f32[64,128]{1,0:T(8,128)S(1)} %get-tuple-element.58.prod_ref), channel_id=1, source_target_pairs={{0,4},{4,8},{8,12},{1,5},{5,9},{9,13},{2,6},{6,10},{10,14},{3,7},{... | collective-permute-start | bytes 98312 | tf_op jit(solution)/shard_map/ppermute | solution.py:25
  25.5 1.3 %collective-permute-start.8 = (f32[64,128]{1,0:T(8,128)S(1)}, f32[64,128]{1,0:T(8,128)S(1)}, u32[]{:S(2)}, u32[]{:S(2)}) collective-permute-start(f32[64,128]{1,0:T(8,128)S(1)} %get-tuple-element.59.bottom_ref), channel_id=1, source_target_pairs={{4,0},{8,4},{12,8},{5,1},{9,5},{13,9},{6,2},{10,6},{14,10},{7,3},{... | collective-permute-start | bytes 98312 | tf_op jit(solution)/shard_map/ppermute | solution.py:25
  26.8 3.5 %shard_map.96 = (f32[8192,128]{1,0:T(8,128)S(1)}, f32[8192,128]{1,0:T(8,128)S(1)}, f32[8192,128]{1,0:T(8,128)S(1)}, f32[8192,128]{1,0:T(8,128)S(1)}, s32[10,128]{1,0:T(8,128)S(1)}) custom-call(f32[8192,128]{1,0:T(8,128)S(1)} %get-tuple-element.42.resid_in, f32[8192,128]{1,0:T(8,128)S(1)} %get-tuple-element.43.extra_in, ...), custom_call_target="tpu_custom_call", output_to_operand_aliasing={{0}: (0, {}), {1}: (1, {})} | custom-call | bytes 11550000 | tf_op jit(solution)/shard_map/pallas_call | solution.py:360
  30.3 1.4 %shard_map.97 = (f32[8192,128]{1,0:T(8,128)S(1)}, f32[1,128]{1,0:T(1,128)S(1)}) custom-call(f32[8192,128]{1,0:T(8,128)S(1)} %get-tuple-element.49.resid_ref, f32[8192,128]{1,0:T(8,128)S(1)} %get-tuple-element.50.extra_ref, f32[8192,128]{1,0:T(8,128)S(1)} %get-tuple-element.51.diag_ref, f32[8192,128]{1,0:T(8,128)S(1)} %get-tuple-element.52.off_ref), custom_call_target="tpu_custom_call" | custom-call | bytes 7920000 | tf_op jit(solution)/shard_map/pallas_call | solution.py:360
  31.8 0.0 collective-permute-done.7.lower_ref
  31.8 0.0 collective-permute-done.8.upper_ref
  31.8 2.7 %shard_map.99 = (f32[8192,128]{1,0:T(8,128)S(1)}, f32[8192,128]{1,0:T(8,128)}, f32[1,128]{1,0:T(1,128)S(1)}, bf16[1,272,128]{2,1,0:T(8,128)(2,1)S(1)}, bf16[1,27...) custom-call(f32[8192,128]{1,0:T(8,128)S(1)} %get-tuple-element.53.pl, ...), custom_call_target="tpu_custom_call", output_to_operand_aliasing={{0}: (0, {})} | custom-call | bytes 8250000 | tf_op jit(solution)/shard_map/pallas_call | solution.py:360
  34.5 4.8 %collective-permute-start.9 = (bf16[1,272,128]{2,1,0:T(8,128)(2,1)S(1)}, bf16[1,272,128]{2,1,0:T(8,128)(2,1)S(1)}, u32[]{:S(2)}, u32[]{:S(2)}) collective-permute-start(bf16[1,272,128]{2,1,0:T(8,128)(2,1)S(1)} %get-tuple-element.66), channel_id=1, source_target_pairs={{0,14},{2,12},{4,10},{6,8},{8,6},{10,4},{12,2},{14,0},{1,15},{3,13... | collective-permute-start | bytes 208904 | tf_op jit(solution)/shard_map/ppermute | solution.py:399
  39.3 0.0 collective-permute-start.10
  39.3 2.1 %collective-permute-start.11 = (bf16[1,272,128]{2,1,0:T(8,128)(2,1)S(1)}, bf16[1,272,128]{2,1,0:T(8,128)(2,1)S(1)}, u32[]{:S(2)}, u32[]{:S(2)}) collective-permute-start(bf16[1,272,128]{2,1,0:T(8,128)(2,1)S(1)} %get-tuple-element.68), channel_id=1, source_target_pairs={{0,10},{2,8},{4,14},{6,12},{8,2},{10,0},{12,6},{14,4},{1,11},{3,9}... | collective-permute-start | bytes 208904 | tf_op jit(solution)/shard_map/ppermute | solution.py:399
  41.5 1.2 %collective-permute-start.12 = (bf16[1,272,128]{2,1,0:T(8,128)(2,1)S(1)}, bf16[1,272,128]{2,1,0:T(8,128)(2,1)S(1)}, u32[]{:S(2)}, u32[]{:S(2)}) collective-permute-start(bf16[1,272,128]{2,1,0:T(8,128)(2,1)S(1)} %get-tuple-element.70), channel_id=1, source_target_pairs={{0,2},{2,0},{4,6},{6,4},{8,10},{10,8},{12,14},{14,12},{1,3},{3,1},... | collective-permute-start | bytes 208904 | tf_op jit(solution)/shard_map/ppermute | solution.py:399
  42.6 2.5 %collective-permute-start.13 = (bf16[1,272,128]{2,1,0:T(8,128)(2,1)S(1)}, bf16[1,272,128]{2,1,0:T(8,128)(2,1)S(1)}, u32[]{:S(2)}, u32[]{:S(2)}) collective-permute-start(bf16[1,272,128]{2,1,0:T(8,128)(2,1)S(1)} %get-tuple-element.71), channel_id=1, source_target_pairs={{0,4},{2,6},{4,0},{6,2},{8,12},{10,14},{12,8},{14,10},{1,5},{3,7},... | collective-permute-start | bytes 208904 | tf_op jit(solution)/shard_map/ppermute | solution.py:399
  45.2 0.0 collective-permute-done.9.rest_1_.rest_7_
  45.2 0.9 %collective-permute-start.14 = (bf16[1,272,128]{2,1,0:T(8,128)(2,1)S(1)}, bf16[1,272,128]{2,1,0:T(8,128)(2,1)S(1)}, u32[]{:S(2)}, u32[]{:S(2)}) collective-permute-start(bf16[1,272,128]{2,1,0:T(8,128)(2,1)S(1)} %get-tuple-element.72), channel_id=1, source_target_pairs={{0,6},{2,4},{4,2},{6,0},{8,14},{10,12},{12,10},{14,8},{1,7},{3,5},... | collective-permute-start | bytes 208904 | tf_op jit(solution)/shard_map/ppermute | solution.py:399
  46.0 0.0 collective-permute-done.10.rest_2_.rest_6_
  46.0 2.3 %collective-permute-start.15 = (bf16[1,272,128]{2,1,0:T(8,128)(2,1)S(1)}, bf16[1,272,128]{2,1,0:T(8,128)(2,1)S(1)}, u32[]{:S(2)}, u32[]{:S(2)}) collective-permute-start(bf16[1,272,128]{2,1,0:T(8,128)(2,1)S(1)} %get-tuple-element.73), channel_id=1, source_target_pairs={{0,8},{2,10},{4,12},{6,14},{8,0},{10,2},{12,4},{14,6},{1,9},{3,11}... | collective-permute-start | bytes 208904 | tf_op jit(solution)/shard_map/ppermute | solution.py:399
  48.3 0.8 %shard_map.100.rest_0_ = bf16[1,272,128]{2,1,0:T(8,128)(2,1)S(1)} custom-call(f32[8192,128]{1,0:T(8,128)S(1)} %get-tuple-element.64.plane_ref, f32[1,128]{1,0:T(1,128)S(1)} %get-tuple-element.65.sum_ref, s32[2,128]{1,0:T(2,128)S(1)} %get-tuple-element.85.rest_0_), custom_call_target="tpu_custom_call" | custom-call | bytes 1650000 | tf_op jit(solution)/shard_map/pallas_call | solution.py:360
  49.1 0.0 collective-permute-done.11.rest_3_.rest_5_
  49.2 0.8 %shard_map.101 = (f32[1024,128]{1,0:T(8,128)S(1)}, f32[1024,128]{1,0:T(8,128)S(1)}) custom-call(s32[1,1024]{1,0:T(1,128)S(1)} %get-tuple-element.63.pos_ref, bf16[1,272,128]{2,1,0:T(8,128)(2,1)S(1)} %shard_map.100.rest_0_, bf16[1,272,128]{2,1,0:T(8,128)(2,1)S(1)} %collective-permute-done.9.rest_1_.rest_7_, ...), custom_call_target="tpu_custom_call" | custom-call | bytes 3300000 | tf_op jit(solution)/shard_map/pallas_call | solution.py:360
  49.9 0.0 collective-permute-done.12.rest_1_.rest_3_
  50.0 0.0 collective-permute-done.13.rest_2_
  50.0 0.4 collective-permute-done.14.rest_3_.rest_1_
  50.4 0.9 %collective-permute-done.15.rest_4_.rest_0_ = bf16[1,272,128]{2,1,0:T(8,128)(2,1)S(1)} collective-permute-done((bf16[1,272,128]{2,1,0:T(8,128)(2,1)S(1)}, bf16[1,272,128]{2,1,0:T(8,128)(2,1)S(1)}, u32[]{:S(2)}, u32[]{:S(2)}) %collective-permute-start.15) | collective-permute-done | bytes 69664 | tf_op jit(solution)/shard_map/ppermute | solution.py:399
  51.3 0.1 collective-permute-start.16
  51.3 1.4 %shard_map.103 = bf16[1024,128]{1,0:T(8,128)(2,1)} custom-call(f32[1024,128]{1,0:T(8,128)S(1)} %get-tuple-element.69.after_ref.places_ref, f32[1024,128]{1,0:T(8,128)S(1)} %get-tuple-element.74.total_ref, bf16[1,272,128]{2,1,0:T(8,128)(2,1)S(1)} %collective-permute-done.15.rest_4_.rest_0_, bf16[1,272,128]{2,1,0:T(8,128)(2,1)S(1)} %collective-permute-done.14.rest_3_.rest_1_, ...), custom_call_target="tpu_custom_call" | custom-call | bytes 3300000 | tf_op jit(solution)/shard_map/pallas_call | solution.py:360
  52.7 0.0 collective-permute-done.16
  (3 shorter events, 0.0 us)
Async XLA Ops:
  3.0 11.3 %collective-permute-start = (bf16[1,272,128]{2,1,0:T(8,128)(2,1)S(1)}, bf16[1,272,128]{2,1,0:T(8,128)(2,1)S(1)}, u32[]{:S(2)}, u32[]{:S(2)}) collective-permute-start(bf16[1,272,128]{2,1,0:T(8,128)(2,1)S(1)} %get-tuple-element.40), channel_id=1, source_target_pairs={{0,14},{2,12},{4,10},{6,8},{8,6},{10,4},{12,2},{14,0},{1,15},{3,13... | collective-permute-start | bytes 208904 | tf_op jit(solution)/shard_map/ppermute | solution.py:399
  9.0 6.7 %collective-permute-start.1 = (bf16[1,272,128]{2,1,0:T(8,128)(2,1)S(1)}, bf16[1,272,128]{2,1,0:T(8,128)(2,1)S(1)}, u32[]{:S(2)}, u32[]{:S(2)}) collective-permute-start(bf16[1,272,128]{2,1,0:T(8,128)(2,1)S(1)} %get-tuple-element.41), channel_id=1, source_target_pairs={{0,12},{2,14},{4,8},{6,10},{8,4},{10,6},{12,0},{14,2},{1,13},{3,15... | collective-permute-start | bytes 208904 | tf_op jit(solution)/shard_map/ppermute | solution.py:399
  9.3 10.8 %collective-permute-start.2 = (bf16[1,272,128]{2,1,0:T(8,128)(2,1)S(1)}, bf16[1,272,128]{2,1,0:T(8,128)(2,1)S(1)}, u32[]{:S(2)}, u32[]{:S(2)}) collective-permute-start(bf16[1,272,128]{2,1,0:T(8,128)(2,1)S(1)} %get-tuple-element.44), channel_id=1, source_target_pairs={{0,10},{2,8},{4,14},{6,12},{8,2},{10,0},{12,6},{14,4},{1,11},{3,9}... | collective-permute-start | bytes 208904 | tf_op jit(solution)/shard_map/ppermute | solution.py:399
  10.0 10.9 %collective-permute-start.3 = (bf16[1,272,128]{2,1,0:T(8,128)(2,1)S(1)}, bf16[1,272,128]{2,1,0:T(8,128)(2,1)S(1)}, u32[]{:S(2)}, u32[]{:S(2)}) collective-permute-start(bf16[1,272,128]{2,1,0:T(8,128)(2,1)S(1)} %get-tuple-element.45), channel_id=1, source_target_pairs={{0,8},{2,10},{4,12},{6,14},{8,0},{10,2},{12,4},{14,6},{1,9},{3,11}... | collective-permute-start | bytes 208904 | tf_op jit(solution)/shard_map/ppermute | solution.py:399
  12.0 8.9 %collective-permute-start.4 = (bf16[1,272,128]{2,1,0:T(8,128)(2,1)S(1)}, bf16[1,272,128]{2,1,0:T(8,128)(2,1)S(1)}, u32[]{:S(2)}, u32[]{:S(2)}) collective-permute-start(bf16[1,272,128]{2,1,0:T(8,128)(2,1)S(1)} %get-tuple-element.46), channel_id=1, source_target_pairs={{0,6},{2,4},{4,2},{6,0},{8,14},{10,12},{12,10},{14,8},{1,7},{3,5},... | collective-permute-start | bytes 208904 | tf_op jit(solution)/shard_map/ppermute | solution.py:399
  14.3 6.7 %collective-permute-start.5 = (bf16[1,272,128]{2,1,0:T(8,128)(2,1)S(1)}, bf16[1,272,128]{2,1,0:T(8,128)(2,1)S(1)}, u32[]{:S(2)}, u32[]{:S(2)}) collective-permute-start(bf16[1,272,128]{2,1,0:T(8,128)(2,1)S(1)} %get-tuple-element.47), channel_id=1, source_target_pairs={{0,4},{2,6},{4,0},{6,2},{8,12},{10,14},{12,8},{14,10},{1,5},{3,7},... | collective-permute-start | bytes 208904 | tf_op jit(solution)/shard_map/ppermute | solution.py:399
  15.8 5.2 %collective-permute-start.6 = (bf16[1,272,128]{2,1,0:T(8,128)(2,1)S(1)}, bf16[1,272,128]{2,1,0:T(8,128)(2,1)S(1)}, u32[]{:S(2)}, u32[]{:S(2)}) collective-permute-start(bf16[1,272,128]{2,1,0:T(8,128)(2,1)S(1)} %get-tuple-element.48), channel_id=1, source_target_pairs={{0,2},{2,0},{4,6},{6,4},{8,10},{10,8},{12,14},{14,12},{1,3},{3,1},... | collective-permute-start | bytes 208904 | tf_op jit(solution)/shard_map/ppermute | solution.py:399
  21.3 10.4 %collective-permute-start.7 = (f32[64,128]{1,0:T(8,128)S(1)}, f32[64,128]{1,0:T(8,128)S(1)}, u32[]{:S(2)}, u32[]{:S(2)}) collective-permute-start(f32[64,128]{1,0:T(8,128)S(1)} %get-tuple-element.58.prod_ref), channel_id=1, source_target_pairs={{0,4},{4,8},{8,12},{1,5},{5,9},{9,13},{2,6},{6,10},{10,14},{3,7},{... | collective-permute-start | bytes 98312 | tf_op jit(solution)/shard_map/ppermute | solution.py:25
  25.5 6.3 %collective-permute-start.8 = (f32[64,128]{1,0:T(8,128)S(1)}, f32[64,128]{1,0:T(8,128)S(1)}, u32[]{:S(2)}, u32[]{:S(2)}) collective-permute-start(f32[64,128]{1,0:T(8,128)S(1)} %get-tuple-element.59.bottom_ref), channel_id=1, source_target_pairs={{4,0},{8,4},{12,8},{5,1},{9,5},{13,9},{6,2},{10,6},{14,10},{7,3},{... | collective-permute-start | bytes 98312 | tf_op jit(solution)/shard_map/ppermute | solution.py:25
  34.5 10.7 %collective-permute-start.9 = (bf16[1,272,128]{2,1,0:T(8,128)(2,1)S(1)}, bf16[1,272,128]{2,1,0:T(8,128)(2,1)S(1)}, u32[]{:S(2)}, u32[]{:S(2)}) collective-permute-start(bf16[1,272,128]{2,1,0:T(8,128)(2,1)S(1)} %get-tuple-element.66), channel_id=1, source_target_pairs={{0,14},{2,12},{4,10},{6,8},{8,6},{10,4},{12,2},{14,0},{1,15},{3,13... | collective-permute-start | bytes 208904 | tf_op jit(solution)/shard_map/ppermute | solution.py:399
  39.3 6.7 %collective-permute-start.10 = (bf16[1,272,128]{2,1,0:T(8,128)(2,1)S(1)}, bf16[1,272,128]{2,1,0:T(8,128)(2,1)S(1)}, u32[]{:S(2)}, u32[]{:S(2)}) collective-permute-start(bf16[1,272,128]{2,1,0:T(8,128)(2,1)S(1)} %get-tuple-element.67), channel_id=1, source_target_pairs={{0,12},{2,14},{4,8},{6,10},{8,4},{10,6},{12,0},{14,2},{1,13},{3,15... | collective-permute-start | bytes 208904 | tf_op jit(solution)/shard_map/ppermute | solution.py:399
  39.3 9.8 %collective-permute-start.11 = (bf16[1,272,128]{2,1,0:T(8,128)(2,1)S(1)}, bf16[1,272,128]{2,1,0:T(8,128)(2,1)S(1)}, u32[]{:S(2)}, u32[]{:S(2)}) collective-permute-start(bf16[1,272,128]{2,1,0:T(8,128)(2,1)S(1)} %get-tuple-element.68), channel_id=1, source_target_pairs={{0,10},{2,8},{4,14},{6,12},{8,2},{10,0},{12,6},{14,4},{1,11},{3,9}... | collective-permute-start | bytes 208904 | tf_op jit(solution)/shard_map/ppermute | solution.py:399
  41.5 8.5 %collective-permute-start.12 = (bf16[1,272,128]{2,1,0:T(8,128)(2,1)S(1)}, bf16[1,272,128]{2,1,0:T(8,128)(2,1)S(1)}, u32[]{:S(2)}, u32[]{:S(2)}) collective-permute-start(bf16[1,272,128]{2,1,0:T(8,128)(2,1)S(1)} %get-tuple-element.70), channel_id=1, source_target_pairs={{0,2},{2,0},{4,6},{6,4},{8,10},{10,8},{12,14},{14,12},{1,3},{3,1},... | collective-permute-start | bytes 208904 | tf_op jit(solution)/shard_map/ppermute | solution.py:399
  42.6 7.3 %collective-permute-start.13 = (bf16[1,272,128]{2,1,0:T(8,128)(2,1)S(1)}, bf16[1,272,128]{2,1,0:T(8,128)(2,1)S(1)}, u32[]{:S(2)}, u32[]{:S(2)}) collective-permute-start(bf16[1,272,128]{2,1,0:T(8,128)(2,1)S(1)} %get-tuple-element.71), channel_id=1, source_target_pairs={{0,4},{2,6},{4,0},{6,2},{8,12},{10,14},{12,8},{14,10},{1,5},{3,7},... | collective-permute-start | bytes 208904 | tf_op jit(solution)/shard_map/ppermute | solution.py:399
  45.2 5.2 %collective-permute-start.14 = (bf16[1,272,128]{2,1,0:T(8,128)(2,1)S(1)}, bf16[1,272,128]{2,1,0:T(8,128)(2,1)S(1)}, u32[]{:S(2)}, u32[]{:S(2)}) collective-permute-start(bf16[1,272,128]{2,1,0:T(8,128)(2,1)S(1)} %get-tuple-element.72), channel_id=1, source_target_pairs={{0,6},{2,4},{4,2},{6,0},{8,14},{10,12},{12,10},{14,8},{1,7},{3,5},... | collective-permute-start | bytes 208904 | tf_op jit(solution)/shard_map/ppermute | solution.py:399
  46.0 5.2 %collective-permute-start.15 = (bf16[1,272,128]{2,1,0:T(8,128)(2,1)S(1)}, bf16[1,272,128]{2,1,0:T(8,128)(2,1)S(1)}, u32[]{:S(2)}, u32[]{:S(2)}) collective-permute-start(bf16[1,272,128]{2,1,0:T(8,128)(2,1)S(1)} %get-tuple-element.73), channel_id=1, source_target_pairs={{0,8},{2,10},{4,12},{6,14},{8,0},{10,2},{12,4},{14,6},{1,9},{3,11}... | collective-permute-start | bytes 208904 | tf_op jit(solution)/shard_map/ppermute | solution.py:399
  51.3 1.5 %collective-permute-start.16 = (f32[1,128]{1,0:T(1,128)S(1)}, f32[1,128]{1,0:T(1,128)S(1)}, u32[]{:S(2)}, u32[]{:S(2)}) collective-permute-start(f32[1,128]{1,0:T(1,128)S(1)} %shard_map.102), channel_id=1, source_target_pairs={{0,1},{1,0},{2,3},{3,2},{4,5},{5,4},{6,7},{7,6},{8,9},{9,8},{10,11... | collective-permute-start | bytes 1544 | tf_op jit(solution)/shard_map/ppermute | solution.py:531

commit v4 on v3

--- a/solution.py
+++ b/solution.py
@@ -49,14 +49,21 @@
 
 
 def pack_kernel(
-    slots, groups, direct, firsts, own_hbm, layer_hbm, seg_hbm, src_hbm, pos_ref, *rest
+    slots, groups, direct, firsts, own_hbm, layer_hbm, seg_hbm, src_hbm, tdi_hbm,
+    resid_ref, pos_ref, *rest
 ):
     outs, (own_ref, layer_ref, seg_ref, wide_ref, sems) = rest[:-5], rest[-5:]
     src_ref = wide_ref.at[:, pl.ds(0, LANES)]
     copies = [
         pltpu.make_async_copy(source, target, sems.at[i])
         for i, (source, target) in enumerate(
-            ((own_hbm, own_ref), (layer_hbm, layer_ref), (seg_hbm, seg_ref), (src_hbm, src_ref))
+            (
+                (own_hbm, own_ref),
+                (layer_hbm, layer_ref),
+                (seg_hbm, seg_ref),
+                (src_hbm, src_ref),
+                (tdi_hbm, resid_ref),
+            )
         )
     ]
     for copy in copies:
@@ -117,6 +124,7 @@
         for ref, first in zip(outs, firsts):
             for i in range(ref.shape[0]):
                 ref[i, slots:] = tail_of(named, 2 * (first + i))
+    copies[4].wait()
 
 
 def cells_of(ref, i, slots, segs):
@@ -127,7 +135,7 @@
     ]
 
 
-def rim_kernel(slots, layers, low_ref, high_ref, off_ref, *rest):
+def rim_kernel(slots, layers, after_ref, low_ref, high_ref, off_ref, *rest):
     chunks, (bottom_ref, prod_ref) = rest[:-2], rest[-2:]
     segs = low_ref.shape[0]
     line = lax.broadcasted_iota(I32, (2 * segs, LANES), 0)
@@ -188,40 +196,44 @@
     lax.fori_loop(0, cell_ref.shape[0], scatter, 0)
 
 
-def first_scatter_kernel(slots, segs, tdi_hbm, off_hbm, *rest):
-    chunks, outs, (blocks, cells, sem, sems) = rest[:-10], rest[-10:-4], rest[-4:]
-    resid_ref, extra_ref, low_ref, high_ref, last_ref, cell_ref = outs
+def first_scatter_kernel(slots, segs, resid_in, diag_hbm, off_hbm, *rest):
+    chunks, outs, (blocks, cells, sem, sems) = rest[:-11], rest[-11:-4], rest[-4:]
+    resid_ref, extra_ref, diag_ref, low_ref, high_ref, last_ref, cell_ref = outs
     size = resid_ref.shape[0]
-    copy = pltpu.make_async_copy(tdi_hbm, resid_ref, sems.at[0])
-    copy_last = pltpu.make_async_copy(off_hbm.at[pl.ds(size - segs, segs)], last_ref, sems.at[1])
-    copy_last.start()
-    copy.start()
-
-    def ready():
-        extra_ref[...] = jnp.zeros_like(extra_ref)
-        copy_last.wait()
-        copy.wait()
-        low_ref[...] = resid_ref[:segs]
-        high_ref[...] = resid_ref[size - segs :]
-
-    scatter_blocks(slots, segs, chunks, resid_ref, extra_ref, cell_ref, blocks, cells, sem, ready)
-
-
-def scatter_kernel(slots, segs, resid_in, extra_in, diag_hbm, off_hbm, *rest):
-    chunks, outs, (blocks, cells, sem, sems) = rest[:-9], rest[-9:-4], rest[-4:]
-    resid_ref, extra_ref, diag_ref, off_ref, cell_ref = outs
     copies = [
-        pltpu.make_async_copy(diag_hbm, diag_ref, sems.at[0]),
-        pltpu.make_async_copy(off_hbm, off_ref, sems.at[1]),
+        pltpu.make_async_copy(off_hbm.at[pl.ds(size - segs, segs)], last_ref, sems.at[0]),
+        pltpu.make_async_copy(diag_hbm, diag_ref, sems.at[1]),
     ]
     for copy in copies:
         copy.start()
+
+    def ready():
+        extra_ref[...] = jnp.zeros_like(extra_ref)
+        low_ref[...] = resid_ref[:segs]
+        high_ref[...] = resid_ref[size - segs :]
+
+    scatter_blocks(slots, segs, chunks, resid_ref, extra_ref, cell_ref, blocks, cells, sem, ready)
+    for copy in copies:
+        copy.wait()
+
+
+def scatter_kernel(slots, segs, resid_in, extra_in, *rest):
+    chunks, (resid_ref, extra_ref, cell_ref, blocks, cells, sem) = rest[:-6], rest[-6:]
+    scatter_blocks(
+        slots, segs, chunks, resid_ref, extra_ref, cell_ref, blocks, cells, sem, lambda: None
+    )
+
+
+def last_scatter_kernel(slots, segs, resid_in, extra_in, off_hbm, *rest):
+    chunks, outs, (blocks, cells, sem, off_sem) = rest[:-8], rest[-8:-4], rest[-4:]
+    resid_ref, extra_ref, off_ref, cell_ref = outs
+    copy = pltpu.make_async_copy(off_hbm, off_ref, off_sem)
+    copy.start()
     if chunks:
         scatter_blocks(
             slots, segs, chunks, resid_ref, extra_ref, cell_ref, blocks, cells, sem, lambda: None
         )
-    for copy in copies:
-        copy.wait()
+    copy.wait()
 
 
 def weigh_kernel(segs, layers, resid_ref, extra_ref, diag_ref, off_ref, plane_ref, part_ref):
@@ -380,14 +392,15 @@
     cell_count = layers * segs
     direct = groups == 8
     if direct:
-        sizes, first_out = [1] * groups, [7, 6, 5, 4, 3, 2, 1, 0]
-        first_back, second_back = [7, 6, 5, 4, 3, 2, 1], [0]
-        first_in, second_in = [0, 7, 6], [5, 4, 3, 2, 1]
-        early, late = [0, 7, 6, 5], [4, 3, 2, 1]
+        order = [7, 6, 5, 4, 3, 2, 1]
+        sizes, first_out = [1] * groups, order + [0]
+        first_back, second_back = order, [0]
+        first_in, second_in, last_in = [0] + order[:2], order[2:3], order[3:]
+        early, late = [0] + order[:3], order[3:]
     else:
         sizes, first_out = [groups], [0]
         first_back, second_back = [0], []
-        first_in, second_in = [0], []
+        first_in, second_in, last_in = [0], [], []
         early, late = [], [0]
     total = len(sizes)
 
@@ -407,19 +420,20 @@
     off = noise_off.reshape(cell_count, bins)
 
     arrived = [None] * total
-    pos, *packed = call(
+    resid, pos, *packed = call(
         functools.partial(pack_kernel, slots, groups, direct, first_out),
         in_hbm(
             owner_dev.reshape(1, count),
             layer_in.reshape(1, count),
             seg_in.reshape(1, count),
             src_blocks.reshape(count, bins),
+            tdi,
         ),
-        [HBM] * 4,
-        [pltpu.VMEM((1, count), I32)] + [blocks[k] for k in first_out],
-        [VMEM] * (1 + len(first_out)),
+        [HBM] * 5,
+        [plane, pltpu.VMEM((1, count), I32)] + [blocks[k] for k in first_out],
+        [VMEM] * (2 + len(first_out)),
         [pltpu.VMEM((1, count), I32)] * 3
-        + [pltpu.VMEM((count, 2 * bins), BF16), pltpu.SemaphoreType.DMA((4,))],
+        + [pltpu.VMEM((count, 2 * bins), BF16), pltpu.SemaphoreType.DMA((5,))],
         us=3.0,
     )
     for k, block in zip(first_out, packed):
@@ -445,39 +459,52 @@
             cells[k] = joined[start:stop]
             start = stop
 
-    resid, extra, low, high, off_last, joined = call(
+    resid, extra, diag_in, low, high, off_last, joined = call(
         functools.partial(first_scatter_kernel, slots, segs),
-        in_hbm(tdi, off) + [arrived[k] for k in first_in],
-        [HBM] * 2 + [VMEM] * len(first_in),
-        [plane] * 2 + [rim] * 3 + [lines_of(first_in)],
-        [VMEM] * 6,
+        [resid] + in_hbm(diag, off) + [arrived[k] for k in first_in],
+        [VMEM] + [HBM] * 2 + [VMEM] * len(first_in),
+        [plane] * 3 + [rim] * 3 + [lines_of(first_in)],
+        [VMEM] * 7,
         scratch_of(first_in) + [pltpu.SemaphoreType.DMA((2,))],
-        us=3.0,
+        {0: 0},
+        us=2.5,
     )
     split_lines(first_in, joined)
+    if second_in:
+        resid, extra, joined = call(
+            functools.partial(scatter_kernel, slots, segs),
+            [resid, extra] + [arrived[k] for k in second_in],
+            [VMEM] * (2 + len(second_in)),
+            [plane] * 2 + [lines_of(second_in)],
+            [VMEM] * 3,
+            scratch_of(second_in),
+            {0: 0, 1: 1},
+            us=0.9,
+        )
+        split_lines(second_in, joined)
     bottom, product = call(
         functools.partial(rim_kernel, slots, layers),
-        [low, high, off_last, *arrived],
-        [VMEM] * (3 + total),
+        [joined, low, high, off_last, *arrived],
+        [VMEM] * (4 + total),
         (rim, rim),
         (VMEM, VMEM),
         us=0.3,
     )
     lower_rim = passed_along(product, "band", 1)
     upper_rim = passed_along(bottom, "band", -1)
-    step = second_in or [0]
-    resid, extra, diag_in, off_in, joined = call(
-        functools.partial(scatter_kernel, slots, segs),
-        [resid, extra] + in_hbm(diag, off) + [arrived[k] for k in second_in],
-        [VMEM] * 2 + [HBM] * 2 + [VMEM] * len(second_in),
-        [plane] * 4 + [lines_of(step)],
-        [VMEM] * 5,
-        scratch_of(step) + [pltpu.SemaphoreType.DMA((2,))],
+    step = last_in or [0]
+    resid, extra, off_in, joined = call(
+        functools.partial(last_scatter_kernel, slots, segs),
+        [resid, extra] + in_hbm(off) + [arrived[k] for k in last_in],
+        [VMEM] * 2 + [HBM] + [VMEM] * len(last_in),
+        [plane] * 3 + [lines_of(step)],
+        [VMEM] * 4,
+        scratch_of(step) + [pltpu.SemaphoreType.DMA],
         {0: 0, 1: 1},
-        us=3.5,
-    )
-    if second_in:
-        split_lines(second_in, joined)
+        us=2.5,
+    )
+    if last_in:
+        split_lines(last_in, joined)
     weighed, part = call(
         functools.partial(weigh_kernel, segs, layers),
         (resid, extra, diag_in, off_in),

time: 54.2 us -> 52.8 us (0.974)
  Pallas kernels: 17 us -> 15.9 us
  starting transfers between devices: 32.7 us -> 31.8 us
  waiting for transfers between devices: 2.24 us -> 3.05 us
    pallas_call x10 -> x11, Pallas kernels: 17 us -> 15.9 us  [call(): pl.pallas_call(kernel, out_shape=tuple(out_shape), in_specs=list(in_specs...]
    ppermute x14, starting transfers between devices: 27.1 us -> 26.3 us  [exchanged(): return lax.ppermute(block, AXES, [(i, i ^ number) for i in range(groups)])]
  transfers between devices with their start and end apart: 17 -> 17, of which waited for: 4 -> 4; matrix products, arithmetic and copies ran while one was open for 0% -> 0% of each run, Pallas kernels for 22% -> 20%
where the time goes in v4:
time: 52.8 us
  starting transfers between devices  31.8 us (60%)
  Pallas kernels  15.9 us (30%)
  waiting for transfers between devices  3.05 us (6%)
  between operations  1.97 us (4%)
    ppermute x14, starting transfers between devices, exchanged(): return lax.ppermute(block, AXES, [(i, i ^ number) for i in range(groups)])  26.3 us
    pallas_call x11, Pallas kernels, call(): pl.pallas_call(kernel, out_shape=tuple(out_shape), in_specs=list(in_specs...  15.9 us
    ppermute x2, starting transfers between devices, passed_along(): lax.ppermute(value, axis, [(source, source + steps) for source in range(l...  5.42 us
    ppermute x14, waiting for transfers between devices, exchanged(): return lax.ppermute(block, AXES, [(i, i ^ number) for i in range(groups)])  2.66 us
  transfers between devices with their start and end apart: 17, of which 4 were waited for; matrix products, arithmetic and copies ran while one was open for 0% of the time, Pallas kernels for 20%

profile of v4, /device:TPU:0, one launch (start us, length us, event | category | flops | bytes accessed | tf_op | source)
XLA Modules:
  0.0 52.8 jit_solution(4911120095718887764)
XLA Ops:
  0.6 2.4 %shard_map.94 = (f32[8192,128]{1,0:T(8,128)S(1)}, s32[1,1024]{1,0:T(1,128)S(1)}, bf16[1,272,128]{2,1,0:T(8,128)(2,1)S(1)}, bf16[1,272,128]{2,1,0:T(8,128)(2,1)S(...) custom-call(s32[1,1024]{1,0:T(1,128)} %bitcast.17, ...), custom_call_target="tpu_custom_call" | custom-call | bytes 9900000 | tf_op jit(solution)/shard_map/pallas_call | solution.py:372
  3.0 6.0 %collective-permute-start = (bf16[1,272,128]{2,1,0:T(8,128)(2,1)S(1)}, bf16[1,272,128]{2,1,0:T(8,128)(2,1)S(1)}, u32[]{:S(2)}, u32[]{:S(2)}) collective-permute-start(bf16[1,272,128]{2,1,0:T(8,128)(2,1)S(1)} %get-tuple-element.45), channel_id=1, source_target_pairs={{0,14},{2,12},{4,10},{6,8},{8,6},{10,4},{12,2},{14,0},{1,15},{3,13... | collective-permute-start | bytes 208904 | tf_op jit(solution)/shard_map/ppermute | solution.py:412
  9.1 0.2 collective-permute-start.1
  9.3 0.8 %collective-permute-start.2 = (bf16[1,272,128]{2,1,0:T(8,128)(2,1)S(1)}, bf16[1,272,128]{2,1,0:T(8,128)(2,1)S(1)}, u32[]{:S(2)}, u32[]{:S(2)}) collective-permute-start(bf16[1,272,128]{2,1,0:T(8,128)(2,1)S(1)} %get-tuple-element.49), channel_id=1, source_target_pairs={{0,10},{2,8},{4,14},{6,12},{8,2},{10,0},{12,6},{14,4},{1,11},{3,9}... | collective-permute-start | bytes 208904 | tf_op jit(solution)/shard_map/ppermute | solution.py:412
  10.0 2.0 %collective-permute-start.3 = (bf16[1,272,128]{2,1,0:T(8,128)(2,1)S(1)}, bf16[1,272,128]{2,1,0:T(8,128)(2,1)S(1)}, u32[]{:S(2)}, u32[]{:S(2)}) collective-permute-start(bf16[1,272,128]{2,1,0:T(8,128)(2,1)S(1)} %get-tuple-element.52), channel_id=1, source_target_pairs={{0,8},{2,10},{4,12},{6,14},{8,0},{10,2},{12,4},{14,6},{1,9},{3,11}... | collective-permute-start | bytes 208904 | tf_op jit(solution)/shard_map/ppermute | solution.py:412
  12.1 2.3 %collective-permute-start.4 = (bf16[1,272,128]{2,1,0:T(8,128)(2,1)S(1)}, bf16[1,272,128]{2,1,0:T(8,128)(2,1)S(1)}, u32[]{:S(2)}, u32[]{:S(2)}) collective-permute-start(bf16[1,272,128]{2,1,0:T(8,128)(2,1)S(1)} %get-tuple-element.53), channel_id=1, source_target_pairs={{0,6},{2,4},{4,2},{6,0},{8,14},{10,12},{12,10},{14,8},{1,7},{3,5},... | collective-permute-start | bytes 208904 | tf_op jit(solution)/shard_map/ppermute | solution.py:412
  14.3 0.0 collective-permute-done.rest_1_.rest_7_
  14.3 1.4 %collective-permute-start.5 = (bf16[1,272,128]{2,1,0:T(8,128)(2,1)S(1)}, bf16[1,272,128]{2,1,0:T(8,128)(2,1)S(1)}, u32[]{:S(2)}, u32[]{:S(2)}) collective-permute-start(bf16[1,272,128]{2,1,0:T(8,128)(2,1)S(1)} %get-tuple-element.54), channel_id=1, source_target_pairs={{0,4},{2,6},{4,0},{6,2},{8,12},{10,14},{12,8},{14,10},{1,5},{3,7},... | collective-permute-start | bytes 208904 | tf_op jit(solution)/shard_map/ppermute | solution.py:412
  15.8 0.0 collective-permute-done.1.rest_2_.rest_6_
  15.8 0.5 %collective-permute-start.6 = (bf16[1,272,128]{2,1,0:T(8,128)(2,1)S(1)}, bf16[1,272,128]{2,1,0:T(8,128)(2,1)S(1)}, u32[]{:S(2)}, u32[]{:S(2)}) collective-permute-start(bf16[1,272,128]{2,1,0:T(8,128)(2,1)S(1)} %get-tuple-element.55), channel_id=1, source_target_pairs={{0,2},{2,0},{4,6},{6,4},{8,10},{10,8},{12,14},{14,12},{1,3},{3,1},... | collective-permute-start | bytes 208904 | tf_op jit(solution)/shard_map/ppermute | solution.py:412
  16.3 2.4 %shard_map.95 = (f32[8192,128]{1,0:T(8,128)S(1)}, f32[8192,128]{1,0:T(8,128)S(1)}, f32[8192,128]{1,0:T(8,128)S(1)}, f32[64,128]{1,0:T(8,128)S(1)}, f32[64,128]{1...) custom-call(f32[8192,128]{1,0:T(8,128)S(1)} %get-tuple-element.43.resid_in, ...), custom_call_target="tpu_custom_call", output_to_operand_aliasing={{0}: (0, {})} | custom-call | bytes 8250000 | tf_op jit(solution)/shard_map/pallas_call | solution.py:372
  18.7 1.2 %collective-permute-done.2.rest_0_.rest_5_ = bf16[1,272,128]{2,1,0:T(8,128)(2,1)S(1)} collective-permute-done((bf16[1,272,128]{2,1,0:T(8,128)(2,1)S(1)}, bf16[1,272,128]{2,1,0:T(8,128)(2,1)S(1)}, u32[]{:S(2)}, u32[]{:S(2)}) %collective-permute-start.2) | collective-permute-done | bytes 69664 | tf_op jit(solution)/shard_map/ppermute | solution.py:412
  19.9 1.1 %shard_map.96 = (f32[8192,128]{1,0:T(8,128)S(1)}, f32[8192,128]{1,0:T(8,128)S(1)}, s32[2,128]{1,0:T(2,128)S(1)}) custom-call(f32[8192,128]{1,0:T(8,128)S(1)} %get-tuple-element.47.resid_in, f32[8192,128]{1,0:T(8,128)S(1)} %get-tuple-element.48.extra_in, ...), custom_call_target="tpu_custom_call", output_to_operand_aliasing={{0}: (0, {}), {1}: (1, {})} | custom-call | bytes 2970000 | tf_op jit(solution)/shard_map/pallas_call | solution.py:372
  21.0 0.0 collective-permute-done.3.rest_0_.rest_4_
  21.0 0.0 collective-permute-done.4.rest_1_.rest_3_
  21.1 0.0 collective-permute-done.5.rest_2_
  21.1 0.0 collective-permute-done.6.rest_3_.rest_1_
  21.1 0.3 shard_map.99
  21.4 4.1 %collective-permute-start.7 = (f32[64,128]{1,0:T(8,128)S(1)}, f32[64,128]{1,0:T(8,128)S(1)}, u32[]{:S(2)}, u32[]{:S(2)}) collective-permute-start(f32[64,128]{1,0:T(8,128)S(1)} %get-tuple-element.66.prod_ref), channel_id=1, source_target_pairs={{0,4},{4,8},{8,12},{1,5},{5,9},{9,13},{2,6},{6,10},{10,14},{3,7},{... | collective-permute-start | bytes 98312 | tf_op jit(solution)/shard_map/ppermute | solution.py:25
  25.5 1.3 %collective-permute-start.8 = (f32[64,128]{1,0:T(8,128)S(1)}, f32[64,128]{1,0:T(8,128)S(1)}, u32[]{:S(2)}, u32[]{:S(2)}) collective-permute-start(f32[64,128]{1,0:T(8,128)S(1)} %get-tuple-element.67.bottom_ref), channel_id=1, source_target_pairs={{4,0},{8,4},{12,8},{5,1},{9,5},{13,9},{6,2},{10,6},{14,10},{7,3},{... | collective-permute-start | bytes 98312 | tf_op jit(solution)/shard_map/ppermute | solution.py:25
  26.8 2.7 %shard_map.97 = (f32[8192,128]{1,0:T(8,128)S(1)}, f32[8192,128]{1,0:T(8,128)S(1)}, f32[8192,128]{1,0:T(8,128)S(1)}, s32[8,128]{1,0:T(8,128)S(1)}) custom-call(f32[8192,128]{1,0:T(8,128)S(1)} %get-tuple-element.50.resid_in, f32[8192,128]{1,0:T(8,128)S(1)} %get-tuple-element.51.extra_in, ...), custom_call_target="tpu_custom_call", output_to_operand_aliasing={{0}: (0, {}), {1}: (1, {})} | custom-call | bytes 8250000 | tf_op jit(solution)/shard_map/pallas_call | solution.py:372
  29.5 1.4 %shard_map.98 = (f32[8192,128]{1,0:T(8,128)S(1)}, f32[1,128]{1,0:T(1,128)S(1)}) custom-call(f32[8192,128]{1,0:T(8,128)S(1)} %get-tuple-element.56.resid_ref, f32[8192,128]{1,0:T(8,128)S(1)} %get-tuple-element.57.extra_ref, f32[8192,128]{1,0:T(8,128)S(1)} %get-tuple-element.58.diag_ref, f32[8192,128]{1,0:T(8,128)S(1)} %get-tuple-element.59.off_ref), custom_call_target="tpu_custom_call" | custom-call | bytes 7920000 | tf_op jit(solution)/shard_map/pallas_call | solution.py:372
  30.9 0.0 collective-permute-done.7.lower_ref
  30.9 0.4 collective-permute-done.8.upper_ref
  31.3 2.7 %shard_map.100 = (f32[8192,128]{1,0:T(8,128)S(1)}, f32[8192,128]{1,0:T(8,128)}, f32[1,128]{1,0:T(1,128)S(1)}, bf16[1,272,128]{2,1,0:T(8,128)(2,1)S(1)}, bf16[1,2...) custom-call(f32[8192,128]{1,0:T(8,128)S(1)} %get-tuple-element.60.pl, ...), custom_call_target="tpu_custom_call", output_to_operand_aliasing={{0}: (0, {})} | custom-call | bytes 8250000 | tf_op jit(solution)/shard_map/pallas_call | solution.py:372
  34.0 4.0 %collective-permute-start.9 = (bf16[1,272,128]{2,1,0:T(8,128)(2,1)S(1)}, bf16[1,272,128]{2,1,0:T(8,128)(2,1)S(1)}, u32[]{:S(2)}, u32[]{:S(2)}) collective-permute-start(bf16[1,272,128]{2,1,0:T(8,128)(2,1)S(1)} %get-tuple-element.74), channel_id=1, source_target_pairs={{0,14},{2,12},{4,10},{6,8},{8,6},{10,4},{12,2},{14,0},{1,15},{3,13... | collective-permute-start | bytes 208904 | tf_op jit(solution)/shard_map/ppermute | solution.py:412
  38.0 0.5 %collective-permute-start.10 = (bf16[1,272,128]{2,1,0:T(8,128)(2,1)S(1)}, bf16[1,272,128]{2,1,0:T(8,128)(2,1)S(1)}, u32[]{:S(2)}, u32[]{:S(2)}) collective-permute-start(bf16[1,272,128]{2,1,0:T(8,128)(2,1)S(1)} %get-tuple-element.75), channel_id=1, source_target_pairs={{0,12},{2,14},{4,8},{6,10},{8,4},{10,6},{12,0},{14,2},{1,13},{3,15... | collective-permute-start | bytes 208904 | tf_op jit(solution)/shard_map/ppermute | solution.py:412
  38.6 2.0 %collective-permute-start.11 = (bf16[1,272,128]{2,1,0:T(8,128)(2,1)S(1)}, bf16[1,272,128]{2,1,0:T(8,128)(2,1)S(1)}, u32[]{:S(2)}, u32[]{:S(2)}) collective-permute-start(bf16[1,272,128]{2,1,0:T(8,128)(2,1)S(1)} %get-tuple-element.76), channel_id=1, source_target_pairs={{0,10},{2,8},{4,14},{6,12},{8,2},{10,0},{12,6},{14,4},{1,11},{3,9}... | collective-permute-start | bytes 208904 | tf_op jit(solution)/shard_map/ppermute | solution.py:412
  40.5 0.8 %collective-permute-start.12 = (bf16[1,272,128]{2,1,0:T(8,128)(2,1)S(1)}, bf16[1,272,128]{2,1,0:T(8,128)(2,1)S(1)}, u32[]{:S(2)}, u32[]{:S(2)}) collective-permute-start(bf16[1,272,128]{2,1,0:T(8,128)(2,1)S(1)} %get-tuple-element.78), channel_id=1, source_target_pairs={{0,2},{2,0},{4,6},{6,4},{8,10},{10,8},{12,14},{14,12},{1,3},{3,1},... | collective-permute-start | bytes 208904 | tf_op jit(solution)/shard_map/ppermute | solution.py:412
  41.4 2.5 %collective-permute-start.13 = (bf16[1,272,128]{2,1,0:T(8,128)(2,1)S(1)}, bf16[1,272,128]{2,1,0:T(8,128)(2,1)S(1)}, u32[]{:S(2)}, u32[]{:S(2)}) collective-permute-start(bf16[1,272,128]{2,1,0:T(8,128)(2,1)S(1)} %get-tuple-element.79), channel_id=1, source_target_pairs={{0,4},{2,6},{4,0},{6,2},{8,12},{10,14},{12,8},{14,10},{1,5},{3,7},... | collective-permute-start | bytes 208904 | tf_op jit(solution)/shard_map/ppermute | solution.py:412
  43.9 0.0 collective-permute-done.9.rest_1_.rest_7_
  43.9 1.0 %collective-permute-start.14 = (bf16[1,272,128]{2,1,0:T(8,128)(2,1)S(1)}, bf16[1,272,128]{2,1,0:T(8,128)(2,1)S(1)}, u32[]{:S(2)}, u32[]{:S(2)}) collective-permute-start(bf16[1,272,128]{2,1,0:T(8,128)(2,1)S(1)} %get-tuple-element.80), channel_id=1, source_target_pairs={{0,6},{2,4},{4,2},{6,0},{8,14},{10,12},{12,10},{14,8},{1,7},{3,5},... | collective-permute-start | bytes 208904 | tf_op jit(solution)/shard_map/ppermute | solution.py:412
  44.9 0.0 collective-permute-done.10.rest_2_.rest_6_
  44.9 2.2 %collective-permute-start.15 = (bf16[1,272,128]{2,1,0:T(8,128)(2,1)S(1)}, bf16[1,272,128]{2,1,0:T(8,128)(2,1)S(1)}, u32[]{:S(2)}, u32[]{:S(2)}) collective-permute-start(bf16[1,272,128]{2,1,0:T(8,128)(2,1)S(1)} %get-tuple-element.81), channel_id=1, source_target_pairs={{0,8},{2,10},{4,12},{6,14},{8,0},{10,2},{12,4},{14,6},{1,9},{3,11}... | collective-permute-start | bytes 208904 | tf_op jit(solution)/shard_map/ppermute | solution.py:412
  47.0 0.8 %shard_map.101.rest_0_ = bf16[1,272,128]{2,1,0:T(8,128)(2,1)S(1)} custom-call(f32[8192,128]{1,0:T(8,128)S(1)} %get-tuple-element.72.plane_ref, f32[1,128]{1,0:T(1,128)S(1)} %get-tuple-element.73.sum_ref, s32[2,128]{1,0:T(2,128)S(1)} %get-tuple-element.83.rest_0_), custom_call_target="tpu_custom_call" | custom-call | bytes 1650000 | tf_op jit(solution)/shard_map/pallas_call | solution.py:372
  47.8 0.0 collective-permute-done.11.rest_3_.rest_5_
  47.9 0.8 %shard_map.102 = (f32[1024,128]{1,0:T(8,128)S(1)}, f32[1024,128]{1,0:T(8,128)S(1)}) custom-call(s32[1,1024]{1,0:T(1,128)S(1)} %get-tuple-element.71.pos_ref, bf16[1,272,128]{2,1,0:T(8,128)(2,1)S(1)} %shard_map.101.rest_0_, bf16[1,272,128]{2,1,0:T(8,128)(2,1)S(1)} %collective-permute-done.9.rest_1_.rest_7_, ...), custom_call_target="tpu_custom_call" | custom-call | bytes 3300000 | tf_op jit(solution)/shard_map/pallas_call | solution.py:372
  48.6 0.0 collective-permute-done.12.rest_1_.rest_3_
  48.7 0.0 collective-permute-done.13.rest_2_
  48.7 0.4 collective-permute-done.14.rest_3_.rest_1_
  49.1 1.0 %collective-permute-done.15.rest_4_.rest_0_ = bf16[1,272,128]{2,1,0:T(8,128)(2,1)S(1)} collective-permute-done((bf16[1,272,128]{2,1,0:T(8,128)(2,1)S(1)}, bf16[1,272,128]{2,1,0:T(8,128)(2,1)S(1)}, u32[]{:S(2)}, u32[]{:S(2)}) %collective-permute-start.15) | collective-permute-done | bytes 69664 | tf_op jit(solution)/shard_map/ppermute | solution.py:412
  50.1 0.1 collective-permute-start.16
  50.2 1.4 %shard_map.104 = bf16[1024,128]{1,0:T(8,128)(2,1)} custom-call(f32[1024,128]{1,0:T(8,128)S(1)} %get-tuple-element.77.after_ref.places_ref, f32[1024,128]{1,0:T(8,128)S(1)} %get-tuple-element.82.total_ref, bf16[1,272,128]{2,1,0:T(8,128)(2,1)S(1)} %collective-permute-done.15.rest_4_.rest_0_, bf16[1,272,128]{2,1,0:T(8,128)(2,1)S(1)} %collective-permute-done.14.rest_3_.rest_1_, ...), custom_call_target="tpu_custom_call" | custom-call | bytes 3300000 | tf_op jit(solution)/shard_map/pallas_call | solution.py:372
  51.6 0.0 collective-permute-done.16
  (3 shorter events, 0.0 us)
Async XLA Ops:
  3.0 11.3 %collective-permute-start = (bf16[1,272,128]{2,1,0:T(8,128)(2,1)S(1)}, bf16[1,272,128]{2,1,0:T(8,128)(2,1)S(1)}, u32[]{:S(2)}, u32[]{:S(2)}) collective-permute-start(bf16[1,272,128]{2,1,0:T(8,128)(2,1)S(1)} %get-tuple-element.45), channel_id=1, source_target_pairs={{0,14},{2,12},{4,10},{6,8},{8,6},{10,4},{12,2},{14,0},{1,15},{3,13... | collective-permute-start | bytes 208904 | tf_op jit(solution)/shard_map/ppermute | solution.py:412
  9.1 6.7 %collective-permute-start.1 = (bf16[1,272,128]{2,1,0:T(8,128)(2,1)S(1)}, bf16[1,272,128]{2,1,0:T(8,128)(2,1)S(1)}, u32[]{:S(2)}, u32[]{:S(2)}) collective-permute-start(bf16[1,272,128]{2,1,0:T(8,128)(2,1)S(1)} %get-tuple-element.46), channel_id=1, source_target_pairs={{0,12},{2,14},{4,8},{6,10},{8,4},{10,6},{12,0},{14,2},{1,13},{3,15... | collective-permute-start | bytes 208904 | tf_op jit(solution)/shard_map/ppermute | solution.py:412
  9.3 10.7 %collective-permute-start.2 = (bf16[1,272,128]{2,1,0:T(8,128)(2,1)S(1)}, bf16[1,272,128]{2,1,0:T(8,128)(2,1)S(1)}, u32[]{:S(2)}, u32[]{:S(2)}) collective-permute-start(bf16[1,272,128]{2,1,0:T(8,128)(2,1)S(1)} %get-tuple-element.49), channel_id=1, source_target_pairs={{0,10},{2,8},{4,14},{6,12},{8,2},{10,0},{12,6},{14,4},{1,11},{3,9}... | collective-permute-start | bytes 208904 | tf_op jit(solution)/shard_map/ppermute | solution.py:412
  10.0 11.0 %collective-permute-start.3 = (bf16[1,272,128]{2,1,0:T(8,128)(2,1)S(1)}, bf16[1,272,128]{2,1,0:T(8,128)(2,1)S(1)}, u32[]{:S(2)}, u32[]{:S(2)}) collective-permute-start(bf16[1,272,128]{2,1,0:T(8,128)(2,1)S(1)} %get-tuple-element.52), channel_id=1, source_target_pairs={{0,8},{2,10},{4,12},{6,14},{8,0},{10,2},{12,4},{14,6},{1,9},{3,11}... | collective-permute-start | bytes 208904 | tf_op jit(solution)/shard_map/ppermute | solution.py:412
  12.1 9.0 %collective-permute-start.4 = (bf16[1,272,128]{2,1,0:T(8,128)(2,1)S(1)}, bf16[1,272,128]{2,1,0:T(8,128)(2,1)S(1)}, u32[]{:S(2)}, u32[]{:S(2)}) collective-permute-start(bf16[1,272,128]{2,1,0:T(8,128)(2,1)S(1)} %get-tuple-element.53), channel_id=1, source_target_pairs={{0,6},{2,4},{4,2},{6,0},{8,14},{10,12},{12,10},{14,8},{1,7},{3,5},... | collective-permute-start | bytes 208904 | tf_op jit(solution)/shard_map/ppermute | solution.py:412
  14.3 6.7 %collective-permute-start.5 = (bf16[1,272,128]{2,1,0:T(8,128)(2,1)S(1)}, bf16[1,272,128]{2,1,0:T(8,128)(2,1)S(1)}, u32[]{:S(2)}, u32[]{:S(2)}) collective-permute-start(bf16[1,272,128]{2,1,0:T(8,128)(2,1)S(1)} %get-tuple-element.54), channel_id=1, source_target_pairs={{0,4},{2,6},{4,0},{6,2},{8,12},{10,14},{12,8},{14,10},{1,5},{3,7},... | collective-permute-start | bytes 208904 | tf_op jit(solution)/shard_map/ppermute | solution.py:412
  15.8 5.3 %collective-permute-start.6 = (bf16[1,272,128]{2,1,0:T(8,128)(2,1)S(1)}, bf16[1,272,128]{2,1,0:T(8,128)(2,1)S(1)}, u32[]{:S(2)}, u32[]{:S(2)}) collective-permute-start(bf16[1,272,128]{2,1,0:T(8,128)(2,1)S(1)} %get-tuple-element.55), channel_id=1, source_target_pairs={{0,2},{2,0},{4,6},{6,4},{8,10},{10,8},{12,14},{14,12},{1,3},{3,1},... | collective-permute-start | bytes 208904 | tf_op jit(solution)/shard_map/ppermute | solution.py:412
  21.4 9.6 %collective-permute-start.7 = (f32[64,128]{1,0:T(8,128)S(1)}, f32[64,128]{1,0:T(8,128)S(1)}, u32[]{:S(2)}, u32[]{:S(2)}) collective-permute-start(f32[64,128]{1,0:T(8,128)S(1)} %get-tuple-element.66.prod_ref), channel_id=1, source_target_pairs={{0,4},{4,8},{8,12},{1,5},{5,9},{9,13},{2,6},{6,10},{10,14},{3,7},{... | collective-permute-start | bytes 98312 | tf_op jit(solution)/shard_map/ppermute | solution.py:25
  25.5 5.8 %collective-permute-start.8 = (f32[64,128]{1,0:T(8,128)S(1)}, f32[64,128]{1,0:T(8,128)S(1)}, u32[]{:S(2)}, u32[]{:S(2)}) collective-permute-start(f32[64,128]{1,0:T(8,128)S(1)} %get-tuple-element.67.bottom_ref), channel_id=1, source_target_pairs={{4,0},{8,4},{12,8},{5,1},{9,5},{13,9},{6,2},{10,6},{14,10},{7,3},{... | collective-permute-start | bytes 98312 | tf_op jit(solution)/shard_map/ppermute | solution.py:25
  34.0 9.9 %collective-permute-start.9 = (bf16[1,272,128]{2,1,0:T(8,128)(2,1)S(1)}, bf16[1,272,128]{2,1,0:T(8,128)(2,1)S(1)}, u32[]{:S(2)}, u32[]{:S(2)}) collective-permute-start(bf16[1,272,128]{2,1,0:T(8,128)(2,1)S(1)} %get-tuple-element.74), channel_id=1, source_target_pairs={{0,14},{2,12},{4,10},{6,8},{8,6},{10,4},{12,2},{14,0},{1,15},{3,13... | collective-permute-start | bytes 208904 | tf_op jit(solution)/shard_map/ppermute | solution.py:412
  38.0 6.8 %collective-permute-start.10 = (bf16[1,272,128]{2,1,0:T(8,128)(2,1)S(1)}, bf16[1,272,128]{2,1,0:T(8,128)(2,1)S(1)}, u32[]{:S(2)}, u32[]{:S(2)}) collective-permute-start(bf16[1,272,128]{2,1,0:T(8,128)(2,1)S(1)} %get-tuple-element.75), channel_id=1, source_target_pairs={{0,12},{2,14},{4,8},{6,10},{8,4},{10,6},{12,0},{14,2},{1,13},{3,15... | collective-permute-start | bytes 208904 | tf_op jit(solution)/shard_map/ppermute | solution.py:412
  38.6 9.3 %collective-permute-start.11 = (bf16[1,272,128]{2,1,0:T(8,128)(2,1)S(1)}, bf16[1,272,128]{2,1,0:T(8,128)(2,1)S(1)}, u32[]{:S(2)}, u32[]{:S(2)}) collective-permute-start(bf16[1,272,128]{2,1,0:T(8,128)(2,1)S(1)} %get-tuple-element.76), channel_id=1, source_target_pairs={{0,10},{2,8},{4,14},{6,12},{8,2},{10,0},{12,6},{14,4},{1,11},{3,9}... | collective-permute-start | bytes 208904 | tf_op jit(solution)/shard_map/ppermute | solution.py:412
  40.5 8.1 %collective-permute-start.12 = (bf16[1,272,128]{2,1,0:T(8,128)(2,1)S(1)}, bf16[1,272,128]{2,1,0:T(8,128)(2,1)S(1)}, u32[]{:S(2)}, u32[]{:S(2)}) collective-permute-start(bf16[1,272,128]{2,1,0:T(8,128)(2,1)S(1)} %get-tuple-element.78), channel_id=1, source_target_pairs={{0,2},{2,0},{4,6},{6,4},{8,10},{10,8},{12,14},{14,12},{1,3},{3,1},... | collective-permute-start | bytes 208904 | tf_op jit(solution)/shard_map/ppermute | solution.py:412
  41.4 7.3 %collective-permute-start.13 = (bf16[1,272,128]{2,1,0:T(8,128)(2,1)S(1)}, bf16[1,272,128]{2,1,0:T(8,128)(2,1)S(1)}, u32[]{:S(2)}, u32[]{:S(2)}) collective-permute-start(bf16[1,272,128]{2,1,0:T(8,128)(2,1)S(1)} %get-tuple-element.79), channel_id=1, source_target_pairs={{0,4},{2,6},{4,0},{6,2},{8,12},{10,14},{12,8},{14,10},{1,5},{3,7},... | collective-permute-start | bytes 208904 | tf_op jit(solution)/shard_map/ppermute | solution.py:412
  43.9 5.2 %collective-permute-start.14 = (bf16[1,272,128]{2,1,0:T(8,128)(2,1)S(1)}, bf16[1,272,128]{2,1,0:T(8,128)(2,1)S(1)}, u32[]{:S(2)}, u32[]{:S(2)}) collective-permute-start(bf16[1,272,128]{2,1,0:T(8,128)(2,1)S(1)} %get-tuple-element.80), channel_id=1, source_target_pairs={{0,6},{2,4},{4,2},{6,0},{8,14},{10,12},{12,10},{14,8},{1,7},{3,5},... | collective-permute-start | bytes 208904 | tf_op jit(solution)/shard_map/ppermute | solution.py:412
  44.9 5.2 %collective-permute-start.15 = (bf16[1,272,128]{2,1,0:T(8,128)(2,1)S(1)}, bf16[1,272,128]{2,1,0:T(8,128)(2,1)S(1)}, u32[]{:S(2)}, u32[]{:S(2)}) collective-permute-start(bf16[1,272,128]{2,1,0:T(8,128)(2,1)S(1)} %get-tuple-element.81), channel_id=1, source_target_pairs={{0,8},{2,10},{4,12},{6,14},{8,0},{10,2},{12,4},{14,6},{1,9},{3,11}... | collective-permute-start | bytes 208904 | tf_op jit(solution)/shard_map/ppermute | solution.py:412
  50.1 1.5 %collective-permute-start.16 = (f32[1,128]{1,0:T(1,128)S(1)}, f32[1,128]{1,0:T(1,128)S(1)}, u32[]{:S(2)}, u32[]{:S(2)}) collective-permute-start(f32[1,128]{1,0:T(1,128)S(1)} %shard_map.103), channel_id=1, source_target_pairs={{0,1},{1,0},{2,3},{3,2},{4,5},{5,4},{6,7},{7,6},{8,9},{9,8},{10,11... | collective-permute-start | bytes 1544 | tf_op jit(solution)/shard_map/ppermute | solution.py:558

commit v5 on v4

--- a/solution.py
+++ b/solution.py
@@ -392,11 +392,11 @@
     cell_count = layers * segs
     direct = groups == 8
     if direct:
-        order = [7, 6, 5, 4, 3, 2, 1]
+        order = [7, 6, 5, 2, 3, 4, 1]
         sizes, first_out = [1] * groups, order + [0]
         first_back, second_back = order, [0]
-        first_in, second_in, last_in = [0] + order[:2], order[2:3], order[3:]
-        early, late = [0] + order[:3], order[3:]
+        first_in, second_in, last_in = [0] + order[:2], order[2:4], order[4:]
+        early, late = [0] + order[:5], order[5:]
     else:
         sizes, first_out = [groups], [0]
         first_back, second_back = [0], []

time: 52.8 us -> 51.2 us (0.970)
  starting transfers between devices: 31.8 us -> 29.2 us
  waiting for transfers between devices: 3.05 us -> 3.73 us
    ppermute x2, starting transfers between devices: 5.42 us -> 2.62 us  [passed_along(): lax.ppermute(value, axis, [(source, source + steps) for source in range(l...]
    ppermute x2, waiting for transfers between devices: 0.39 us -> 1.71 us  [passed_along(): lax.ppermute(value, axis, [(source, source + steps) for source in range(l...]
    ppermute x14, waiting for transfers between devices: 2.66 us -> 2.02 us  [exchanged(): return lax.ppermute(block, AXES, [(i, i ^ number) for i in range(groups)])]
  transfers between devices with their start and end apart: 17 -> 17, of which waited for: 4 -> 3; matrix products, arithmetic and copies ran while one was open for 0% -> 0% of each run, Pallas kernels for 20% -> 21%
where the time goes in v5:
time: 51.2 us; the launch traced here: 50.8 us
  starting transfers between devices  29.2 us (57%)
  Pallas kernels  15.9 us (31%)
  waiting for transfers between devices  3.73 us (7%)
  between operations  1.97 us (4%)
    ppermute x14, starting transfers between devices, exchanged(): return lax.ppermute(block, AXES, [(i, i ^ number) for i in range(groups)])  26.5 us
    pallas_call x11, Pallas kernels, call(): pl.pallas_call(kernel, out_shape=tuple(out_shape), in_specs=list(in_specs...  15.9 us
    ppermute x2, starting transfers between devices, passed_along(): lax.ppermute(value, axis, [(source, source + steps) for source in range(l...  2.62 us
    ppermute x14, waiting for transfers between devices, exchanged(): return lax.ppermute(block, AXES, [(i, i ^ number) for i in range(groups)])  2.02 us
    ppermute x2, waiting for transfers between devices, passed_along(): lax.ppermute(value, axis, [(source, source + steps) for source in range(l...  1.71 us
  transfers between devices with their start and end apart: 17, of which 3 were waited for; matrix products, arithmetic and copies ran while one was open for 0% of the time, Pallas kernels for 21%

profile of v5, /device:TPU:0, one launch (start us, length us, event | category | flops | bytes accessed | tf_op | source)
XLA Modules:
  0.0 50.8 jit_solution(4607358662068023703)
XLA Ops:
  0.6 2.4 %shard_map.94 = (f32[8192,128]{1,0:T(8,128)S(1)}, s32[1,1024]{1,0:T(1,128)S(1)}, bf16[1,272,128]{2,1,0:T(8,128)(2,1)S(1)}, bf16[1,272,128]{2,1,0:T(8,128)(2,1)S(...) custom-call(s32[1,1024]{1,0:T(1,128)} %bitcast.17, ...), custom_call_target="tpu_custom_call" | custom-call | bytes 9900000 | tf_op jit(solution)/shard_map/pallas_call | solution.py:372
  3.0 6.0 %collective-permute-start = (bf16[1,272,128]{2,1,0:T(8,128)(2,1)S(1)}, bf16[1,272,128]{2,1,0:T(8,128)(2,1)S(1)}, u32[]{:S(2)}, u32[]{:S(2)}) collective-permute-start(bf16[1,272,128]{2,1,0:T(8,128)(2,1)S(1)} %get-tuple-element.45), channel_id=1, source_target_pairs={{0,14},{2,12},{4,10},{6,8},{8,6},{10,4},{12,2},{14,0},{1,15},{3,13... | collective-permute-start | bytes 208904 | tf_op jit(solution)/shard_map/ppermute | solution.py:412
  9.1 0.2 collective-permute-start.1
  9.3 0.8 %collective-permute-start.2 = (bf16[1,272,128]{2,1,0:T(8,128)(2,1)S(1)}, bf16[1,272,128]{2,1,0:T(8,128)(2,1)S(1)}, u32[]{:S(2)}, u32[]{:S(2)}) collective-permute-start(bf16[1,272,128]{2,1,0:T(8,128)(2,1)S(1)} %get-tuple-element.49), channel_id=1, source_target_pairs={{0,10},{2,8},{4,14},{6,12},{8,2},{10,0},{12,6},{14,4},{1,11},{3,9}... | collective-permute-start | bytes 208904 | tf_op jit(solution)/shard_map/ppermute | solution.py:412
  10.0 3.4 %collective-permute-start.3 = (bf16[1,272,128]{2,1,0:T(8,128)(2,1)S(1)}, bf16[1,272,128]{2,1,0:T(8,128)(2,1)S(1)}, u32[]{:S(2)}, u32[]{:S(2)}) collective-permute-start(bf16[1,272,128]{2,1,0:T(8,128)(2,1)S(1)} %get-tuple-element.50), channel_id=1, source_target_pairs={{0,4},{2,6},{4,0},{6,2},{8,12},{10,14},{12,8},{14,10},{1,5},{3,7},... | collective-permute-start | bytes 208904 | tf_op jit(solution)/shard_map/ppermute | solution.py:412
  13.4 0.9 %collective-permute-start.4 = (bf16[1,272,128]{2,1,0:T(8,128)(2,1)S(1)}, bf16[1,272,128]{2,1,0:T(8,128)(2,1)S(1)}, u32[]{:S(2)}, u32[]{:S(2)}) collective-permute-start(bf16[1,272,128]{2,1,0:T(8,128)(2,1)S(1)} %get-tuple-element.53), channel_id=1, source_target_pairs={{0,6},{2,4},{4,2},{6,0},{8,14},{10,12},{12,10},{14,8},{1,7},{3,5},... | collective-permute-start | bytes 208904 | tf_op jit(solution)/shard_map/ppermute | solution.py:412
  14.3 0.0 collective-permute-done.rest_1_.rest_7_
  14.3 3.1 %collective-permute-start.5 = (bf16[1,272,128]{2,1,0:T(8,128)(2,1)S(1)}, bf16[1,272,128]{2,1,0:T(8,128)(2,1)S(1)}, u32[]{:S(2)}, u32[]{:S(2)}) collective-permute-start(bf16[1,272,128]{2,1,0:T(8,128)(2,1)S(1)} %get-tuple-element.54), channel_id=1, source_target_pairs={{0,8},{2,10},{4,12},{6,14},{8,0},{10,2},{12,4},{14,6},{1,9},{3,11}... | collective-permute-start | bytes 208904 | tf_op jit(solution)/shard_map/ppermute | solution.py:412
  17.5 0.0 collective-permute-done.1.rest_2_.rest_6_
  17.5 0.9 %collective-permute-start.6 = (bf16[1,272,128]{2,1,0:T(8,128)(2,1)S(1)}, bf16[1,272,128]{2,1,0:T(8,128)(2,1)S(1)}, u32[]{:S(2)}, u32[]{:S(2)}) collective-permute-start(bf16[1,272,128]{2,1,0:T(8,128)(2,1)S(1)} %get-tuple-element.55), channel_id=1, source_target_pairs={{0,2},{2,0},{4,6},{6,4},{8,10},{10,8},{12,14},{14,12},{1,3},{3,1},... | collective-permute-start | bytes 208904 | tf_op jit(solution)/shard_map/ppermute | solution.py:412
  18.4 2.3 %shard_map.95 = (f32[8192,128]{1,0:T(8,128)S(1)}, f32[8192,128]{1,0:T(8,128)S(1)}, f32[8192,128]{1,0:T(8,128)S(1)}, f32[64,128]{1,0:T(8,128)S(1)}, f32[64,128]{1...) custom-call(f32[8192,128]{1,0:T(8,128)S(1)} %get-tuple-element.43.resid_in, ...), custom_call_target="tpu_custom_call", output_to_operand_aliasing={{0}: (0, {})} | custom-call | bytes 8250000 | tf_op jit(solution)/shard_map/pallas_call | solution.py:372
  20.7 0.0 collective-permute-done.2.rest_0_.rest_5_
  20.7 0.0 collective-permute-done.3.rest_1_.rest_2_
  20.7 1.6 %shard_map.96 = (f32[8192,128]{1,0:T(8,128)S(1)}, f32[8192,128]{1,0:T(8,128)S(1)}, s32[4,128]{1,0:T(4,128)S(1)}) custom-call(f32[8192,128]{1,0:T(8,128)S(1)} %get-tuple-element.47.resid_in, f32[8192,128]{1,0:T(8,128)S(1)} %get-tuple-element.48.extra_in, ...), custom_call_target="tpu_custom_call", output_to_operand_aliasing={{0}: (0, {}), {1}: (1, {})} | custom-call | bytes 2970000 | tf_op jit(solution)/shard_map/pallas_call | solution.py:372
  22.3 0.0 collective-permute-done.4.rest_0_.rest_3_
  22.3 0.0 collective-permute-done.5.rest_1_.rest_4_
  22.3 0.0 collective-permute-done.6.rest_2_.rest_1_
  22.3 0.3 shard_map.99
  22.6 1.3 %collective-permute-start.7 = (f32[64,128]{1,0:T(8,128)S(1)}, f32[64,128]{1,0:T(8,128)S(1)}, u32[]{:S(2)}, u32[]{:S(2)}) collective-permute-start(f32[64,128]{1,0:T(8,128)S(1)} %get-tuple-element.66.prod_ref), channel_id=1, source_target_pairs={{0,4},{4,8},{8,12},{1,5},{5,9},{9,13},{2,6},{6,10},{10,14},{3,7},{... | collective-permute-start | bytes 98312 | tf_op jit(solution)/shard_map/ppermute | solution.py:25
  24.0 1.3 %collective-permute-start.8 = (f32[64,128]{1,0:T(8,128)S(1)}, f32[64,128]{1,0:T(8,128)S(1)}, u32[]{:S(2)}, u32[]{:S(2)}) collective-permute-start(f32[64,128]{1,0:T(8,128)S(1)} %get-tuple-element.67.bottom_ref), channel_id=1, source_target_pairs={{4,0},{8,4},{12,8},{5,1},{9,5},{13,9},{6,2},{10,6},{14,10},{7,3},{... | collective-permute-start | bytes 98312 | tf_op jit(solution)/shard_map/ppermute | solution.py:25
  25.3 2.2 %shard_map.97 = (f32[8192,128]{1,0:T(8,128)S(1)}, f32[8192,128]{1,0:T(8,128)S(1)}, f32[8192,128]{1,0:T(8,128)S(1)}, s32[6,128]{1,0:T(8,128)S(1)}) custom-call(f32[8192,128]{1,0:T(8,128)S(1)} %get-tuple-element.51.resid_in, f32[8192,128]{1,0:T(8,128)S(1)} %get-tuple-element.52.extra_in, ...), custom_call_target="tpu_custom_call", output_to_operand_aliasing={{0}: (0, {}), {1}: (1, {})} | custom-call | bytes 8250000 | tf_op jit(solution)/shard_map/pallas_call | solution.py:372
  27.5 1.4 %shard_map.98 = (f32[8192,128]{1,0:T(8,128)S(1)}, f32[1,128]{1,0:T(1,128)S(1)}) custom-call(f32[8192,128]{1,0:T(8,128)S(1)} %get-tuple-element.56.resid_ref, f32[8192,128]{1,0:T(8,128)S(1)} %get-tuple-element.57.extra_ref, f32[8192,128]{1,0:T(8,128)S(1)} %get-tuple-element.58.diag_ref, f32[8192,128]{1,0:T(8,128)S(1)} %get-tuple-element.59.off_ref), custom_call_target="tpu_custom_call" | custom-call | bytes 7920000 | tf_op jit(solution)/shard_map/pallas_call | solution.py:372
  29.0 0.0 collective-permute-done.7.lower_ref
  29.0 1.7 %collective-permute-done.8.upper_ref = f32[64,128]{1,0:T(8,128)S(1)} collective-permute-done((f32[64,128]{1,0:T(8,128)S(1)}, f32[64,128]{1,0:T(8,128)S(1)}, u32[]{:S(2)}, u32[]{:S(2)}) %collective-permute-start.8) | collective-permute-done | bytes 32800 | tf_op jit(solution)/shard_map/ppermute | solution.py:25
  30.7 2.7 %shard_map.100 = (f32[8192,128]{1,0:T(8,128)S(1)}, f32[8192,128]{1,0:T(8,128)}, f32[1,128]{1,0:T(1,128)S(1)}, bf16[1,272,128]{2,1,0:T(8,128)(2,1)S(1)}, bf16[1,2...) custom-call(f32[8192,128]{1,0:T(8,128)S(1)} %get-tuple-element.60.pl, ...), custom_call_target="tpu_custom_call", output_to_operand_aliasing={{0}: (0, {})} | custom-call | bytes 8250000 | tf_op jit(solution)/shard_map/pallas_call | solution.py:372
  33.4 3.6 %collective-permute-start.9 = (bf16[1,272,128]{2,1,0:T(8,128)(2,1)S(1)}, bf16[1,272,128]{2,1,0:T(8,128)(2,1)S(1)}, u32[]{:S(2)}, u32[]{:S(2)}) collective-permute-start(bf16[1,272,128]{2,1,0:T(8,128)(2,1)S(1)} %get-tuple-element.74), channel_id=1, source_target_pairs={{0,14},{2,12},{4,10},{6,8},{8,6},{10,4},{12,2},{14,0},{1,15},{3,13... | collective-permute-start | bytes 208904 | tf_op jit(solution)/shard_map/ppermute | solution.py:412
  37.0 0.3 collective-permute-start.10
  37.3 2.4 %collective-permute-start.11 = (bf16[1,272,128]{2,1,0:T(8,128)(2,1)S(1)}, bf16[1,272,128]{2,1,0:T(8,128)(2,1)S(1)}, u32[]{:S(2)}, u32[]{:S(2)}) collective-permute-start(bf16[1,272,128]{2,1,0:T(8,128)(2,1)S(1)} %get-tuple-element.76), channel_id=1, source_target_pairs={{0,10},{2,8},{4,14},{6,12},{8,2},{10,0},{12,6},{14,4},{1,11},{3,9}... | collective-permute-start | bytes 208904 | tf_op jit(solution)/shard_map/ppermute | solution.py:412
  39.7 1.8 %collective-permute-start.12 = (bf16[1,272,128]{2,1,0:T(8,128)(2,1)S(1)}, bf16[1,272,128]{2,1,0:T(8,128)(2,1)S(1)}, u32[]{:S(2)}, u32[]{:S(2)}) collective-permute-start(bf16[1,272,128]{2,1,0:T(8,128)(2,1)S(1)} %get-tuple-element.77), channel_id=1, source_target_pairs={{0,4},{2,6},{4,0},{6,2},{8,12},{10,14},{12,8},{14,10},{1,5},{3,7},... | collective-permute-start | bytes 208904 | tf_op jit(solution)/shard_map/ppermute | solution.py:412
  41.5 0.8 %collective-permute-start.13 = (bf16[1,272,128]{2,1,0:T(8,128)(2,1)S(1)}, bf16[1,272,128]{2,1,0:T(8,128)(2,1)S(1)}, u32[]{:S(2)}, u32[]{:S(2)}) collective-permute-start(bf16[1,272,128]{2,1,0:T(8,128)(2,1)S(1)} %get-tuple-element.78), channel_id=1, source_target_pairs={{0,6},{2,4},{4,2},{6,0},{8,14},{10,12},{12,10},{14,8},{1,7},{3,5},... | collective-permute-start | bytes 208904 | tf_op jit(solution)/shard_map/ppermute | solution.py:412
  42.3 0.0 collective-permute-done.9.rest_1_.rest_7_
  42.3 0.9 %collective-permute-start.14 = (bf16[1,272,128]{2,1,0:T(8,128)(2,1)S(1)}, bf16[1,272,128]{2,1,0:T(8,128)(2,1)S(1)}, u32[]{:S(2)}, u32[]{:S(2)}) collective-permute-start(bf16[1,272,128]{2,1,0:T(8,128)(2,1)S(1)} %get-tuple-element.80), channel_id=1, source_target_pairs={{0,2},{2,0},{4,6},{6,4},{8,10},{10,8},{12,14},{14,12},{1,3},{3,1},... | collective-permute-start | bytes 208904 | tf_op jit(solution)/shard_map/ppermute | solution.py:412
  43.2 0.0 collective-permute-done.10.rest_2_.rest_6_
  43.2 1.4 %collective-permute-start.15 = (bf16[1,272,128]{2,1,0:T(8,128)(2,1)S(1)}, bf16[1,272,128]{2,1,0:T(8,128)(2,1)S(1)}, u32[]{:S(2)}, u32[]{:S(2)}) collective-permute-start(bf16[1,272,128]{2,1,0:T(8,128)(2,1)S(1)} %get-tuple-element.81), channel_id=1, source_target_pairs={{0,8},{2,10},{4,12},{6,14},{8,0},{10,2},{12,4},{14,6},{1,9},{3,11}... | collective-permute-start | bytes 208904 | tf_op jit(solution)/shard_map/ppermute | solution.py:412
  44.6 0.8 %shard_map.101.rest_0_ = bf16[1,272,128]{2,1,0:T(8,128)(2,1)S(1)} custom-call(f32[8192,128]{1,0:T(8,128)S(1)} %get-tuple-element.72.plane_ref, f32[1,128]{1,0:T(1,128)S(1)} %get-tuple-element.73.sum_ref, s32[2,128]{1,0:T(2,128)S(1)} %get-tuple-element.83.rest_0_), custom_call_target="tpu_custom_call" | custom-call | bytes 1650000 | tf_op jit(solution)/shard_map/pallas_call | solution.py:372
  45.4 1.0 %collective-permute-done.11.rest_3_.rest_5_ = bf16[1,272,128]{2,1,0:T(8,128)(2,1)S(1)} collective-permute-done((bf16[1,272,128]{2,1,0:T(8,128)(2,1)S(1)}, bf16[1,272,128]{2,1,0:T(8,128)(2,1)S(1)}, u32[]{:S(2)}, u32[]{:S(2)}) %collective-permute-start.11) | collective-permute-done | bytes 69664 | tf_op jit(solution)/shard_map/ppermute | solution.py:412
  46.4 0.0 collective-permute-done.12.rest_4_.rest_2_
  46.4 0.9 %collective-permute-done.13.rest_5_.rest_3_ = bf16[1,272,128]{2,1,0:T(8,128)(2,1)S(1)} collective-permute-done((bf16[1,272,128]{2,1,0:T(8,128)(2,1)S(1)}, bf16[1,272,128]{2,1,0:T(8,128)(2,1)S(1)}, u32[]{:S(2)}, u32[]{:S(2)}) %collective-permute-start.13) | collective-permute-done | bytes 69664 | tf_op jit(solution)/shard_map/ppermute | solution.py:412
  47.3 1.0 %shard_map.102 = (f32[1024,128]{1,0:T(8,128)S(1)}, f32[1024,128]{1,0:T(8,128)S(1)}) custom-call(s32[1,1024]{1,0:T(1,128)S(1)} %get-tuple-element.71.pos_ref, bf16[1,272,128]{2,1,0:T(8,128)(2,1)S(1)} %shard_map.101.rest_0_, bf16[1,272,128]{2,1,0:T(8,128)(2,1)S(1)} %collective-permute-done.9.rest_1_.rest_7_, ...), custom_call_target="tpu_custom_call" | custom-call | bytes 3300000 | tf_op jit(solution)/shard_map/pallas_call | solution.py:372
  48.4 0.0 collective-permute-done.14.rest_1_
  48.4 0.0 collective-permute-done.15.rest_4_.rest_0_
  48.4 0.1 collective-permute-start.16
  48.5 1.1 %shard_map.104 = bf16[1024,128]{1,0:T(8,128)(2,1)} custom-call(f32[1024,128]{1,0:T(8,128)S(1)} %get-tuple-element.79.after_ref.places_ref, f32[1024,128]{1,0:T(8,128)S(1)} %get-tuple-element.82.total_ref, bf16[1,272,128]{2,1,0:T(8,128)(2,1)S(1)} %collective-permute-done.15.rest_4_.rest_0_, bf16[1,272,128]{2,1,0:T(8,128)(2,1)S(1)} %collective-permute-done.14.rest_1_), custom_call_target="tpu_custom_call" | custom-call | bytes 3300000 | tf_op jit(solution)/shard_map/pallas_call | solution.py:372
  49.6 0.0 collective-permute-done.16
  (4 shorter events, 0.0 us)
Async XLA Ops:
  3.0 11.3 %collective-permute-start = (bf16[1,272,128]{2,1,0:T(8,128)(2,1)S(1)}, bf16[1,272,128]{2,1,0:T(8,128)(2,1)S(1)}, u32[]{:S(2)}, u32[]{:S(2)}) collective-permute-start(bf16[1,272,128]{2,1,0:T(8,128)(2,1)S(1)} %get-tuple-element.45), channel_id=1, source_target_pairs={{0,14},{2,12},{4,10},{6,8},{8,6},{10,4},{12,2},{14,0},{1,15},{3,13... | collective-permute-start | bytes 208904 | tf_op jit(solution)/shard_map/ppermute | solution.py:412
  9.1 8.4 %collective-permute-start.1 = (bf16[1,272,128]{2,1,0:T(8,128)(2,1)S(1)}, bf16[1,272,128]{2,1,0:T(8,128)(2,1)S(1)}, u32[]{:S(2)}, u32[]{:S(2)}) collective-permute-start(bf16[1,272,128]{2,1,0:T(8,128)(2,1)S(1)} %get-tuple-element.46), channel_id=1, source_target_pairs={{0,12},{2,14},{4,8},{6,10},{8,4},{10,6},{12,0},{14,2},{1,13},{3,15... | collective-permute-start | bytes 208904 | tf_op jit(solution)/shard_map/ppermute | solution.py:412
  9.3 11.4 %collective-permute-start.2 = (bf16[1,272,128]{2,1,0:T(8,128)(2,1)S(1)}, bf16[1,272,128]{2,1,0:T(8,128)(2,1)S(1)}, u32[]{:S(2)}, u32[]{:S(2)}) collective-permute-start(bf16[1,272,128]{2,1,0:T(8,128)(2,1)S(1)} %get-tuple-element.49), channel_id=1, source_target_pairs={{0,10},{2,8},{4,14},{6,12},{8,2},{10,0},{12,6},{14,4},{1,11},{3,9}... | collective-permute-start | bytes 208904 | tf_op jit(solution)/shard_map/ppermute | solution.py:412
  10.0 10.7 %collective-permute-start.3 = (bf16[1,272,128]{2,1,0:T(8,128)(2,1)S(1)}, bf16[1,272,128]{2,1,0:T(8,128)(2,1)S(1)}, u32[]{:S(2)}, u32[]{:S(2)}) collective-permute-start(bf16[1,272,128]{2,1,0:T(8,128)(2,1)S(1)} %get-tuple-element.50), channel_id=1, source_target_pairs={{0,4},{2,6},{4,0},{6,2},{8,12},{10,14},{12,8},{14,10},{1,5},{3,7},... | collective-permute-start | bytes 208904 | tf_op jit(solution)/shard_map/ppermute | solution.py:412
  13.4 8.9 %collective-permute-start.4 = (bf16[1,272,128]{2,1,0:T(8,128)(2,1)S(1)}, bf16[1,272,128]{2,1,0:T(8,128)(2,1)S(1)}, u32[]{:S(2)}, u32[]{:S(2)}) collective-permute-start(bf16[1,272,128]{2,1,0:T(8,128)(2,1)S(1)} %get-tuple-element.53), channel_id=1, source_target_pairs={{0,6},{2,4},{4,2},{6,0},{8,14},{10,12},{12,10},{14,8},{1,7},{3,5},... | collective-permute-start | bytes 208904 | tf_op jit(solution)/shard_map/ppermute | solution.py:412
  14.3 8.0 %collective-permute-start.5 = (bf16[1,272,128]{2,1,0:T(8,128)(2,1)S(1)}, bf16[1,272,128]{2,1,0:T(8,128)(2,1)S(1)}, u32[]{:S(2)}, u32[]{:S(2)}) collective-permute-start(bf16[1,272,128]{2,1,0:T(8,128)(2,1)S(1)} %get-tuple-element.54), channel_id=1, source_target_pairs={{0,8},{2,10},{4,12},{6,14},{8,0},{10,2},{12,4},{14,6},{1,9},{3,11}... | collective-permute-start | bytes 208904 | tf_op jit(solution)/shard_map/ppermute | solution.py:412
  17.5 4.8 %collective-permute-start.6 = (bf16[1,272,128]{2,1,0:T(8,128)(2,1)S(1)}, bf16[1,272,128]{2,1,0:T(8,128)(2,1)S(1)}, u32[]{:S(2)}, u32[]{:S(2)}) collective-permute-start(bf16[1,272,128]{2,1,0:T(8,128)(2,1)S(1)} %get-tuple-element.55), channel_id=1, source_target_pairs={{0,2},{2,0},{4,6},{6,4},{8,10},{10,8},{12,14},{14,12},{1,3},{3,1},... | collective-permute-start | bytes 208904 | tf_op jit(solution)/shard_map/ppermute | solution.py:412
  22.6 6.3 %collective-permute-start.7 = (f32[64,128]{1,0:T(8,128)S(1)}, f32[64,128]{1,0:T(8,128)S(1)}, u32[]{:S(2)}, u32[]{:S(2)}) collective-permute-start(f32[64,128]{1,0:T(8,128)S(1)} %get-tuple-element.66.prod_ref), channel_id=1, source_target_pairs={{0,4},{4,8},{8,12},{1,5},{5,9},{9,13},{2,6},{6,10},{10,14},{3,7},{... | collective-permute-start | bytes 98312 | tf_op jit(solution)/shard_map/ppermute | solution.py:25
  24.0 6.7 %collective-permute-start.8 = (f32[64,128]{1,0:T(8,128)S(1)}, f32[64,128]{1,0:T(8,128)S(1)}, u32[]{:S(2)}, u32[]{:S(2)}) collective-permute-start(f32[64,128]{1,0:T(8,128)S(1)} %get-tuple-element.67.bottom_ref), channel_id=1, source_target_pairs={{4,0},{8,4},{12,8},{5,1},{9,5},{13,9},{6,2},{10,6},{14,10},{7,3},{... | collective-permute-start | bytes 98312 | tf_op jit(solution)/shard_map/ppermute | solution.py:25
  33.4 8.9 %collective-permute-start.9 = (bf16[1,272,128]{2,1,0:T(8,128)(2,1)S(1)}, bf16[1,272,128]{2,1,0:T(8,128)(2,1)S(1)}, u32[]{:S(2)}, u32[]{:S(2)}) collective-permute-start(bf16[1,272,128]{2,1,0:T(8,128)(2,1)S(1)} %get-tuple-element.74), channel_id=1, source_target_pairs={{0,14},{2,12},{4,10},{6,8},{8,6},{10,4},{12,2},{14,0},{1,15},{3,13... | collective-permute-start | bytes 208904 | tf_op jit(solution)/shard_map/ppermute | solution.py:412
  37.0 6.2 %collective-permute-start.10 = (bf16[1,272,128]{2,1,0:T(8,128)(2,1)S(1)}, bf16[1,272,128]{2,1,0:T(8,128)(2,1)S(1)}, u32[]{:S(2)}, u32[]{:S(2)}) collective-permute-start(bf16[1,272,128]{2,1,0:T(8,128)(2,1)S(1)} %get-tuple-element.75), channel_id=1, source_target_pairs={{0,12},{2,14},{4,8},{6,10},{8,4},{10,6},{12,0},{14,2},{1,13},{3,15... | collective-permute-start | bytes 208904 | tf_op jit(solution)/shard_map/ppermute | solution.py:412
  37.3 9.1 %collective-permute-start.11 = (bf16[1,272,128]{2,1,0:T(8,128)(2,1)S(1)}, bf16[1,272,128]{2,1,0:T(8,128)(2,1)S(1)}, u32[]{:S(2)}, u32[]{:S(2)}) collective-permute-start(bf16[1,272,128]{2,1,0:T(8,128)(2,1)S(1)} %get-tuple-element.76), channel_id=1, source_target_pairs={{0,10},{2,8},{4,14},{6,12},{8,2},{10,0},{12,6},{14,4},{1,11},{3,9}... | collective-permute-start | bytes 208904 | tf_op jit(solution)/shard_map/ppermute | solution.py:412
  39.7 6.7 %collective-permute-start.12 = (bf16[1,272,128]{2,1,0:T(8,128)(2,1)S(1)}, bf16[1,272,128]{2,1,0:T(8,128)(2,1)S(1)}, u32[]{:S(2)}, u32[]{:S(2)}) collective-permute-start(bf16[1,272,128]{2,1,0:T(8,128)(2,1)S(1)} %get-tuple-element.77), channel_id=1, source_target_pairs={{0,4},{2,6},{4,0},{6,2},{8,12},{10,14},{12,8},{14,10},{1,5},{3,7},... | collective-permute-start | bytes 208904 | tf_op jit(solution)/shard_map/ppermute | solution.py:412
  41.5 5.8 %collective-permute-start.13 = (bf16[1,272,128]{2,1,0:T(8,128)(2,1)S(1)}, bf16[1,272,128]{2,1,0:T(8,128)(2,1)S(1)}, u32[]{:S(2)}, u32[]{:S(2)}) collective-permute-start(bf16[1,272,128]{2,1,0:T(8,128)(2,1)S(1)} %get-tuple-element.78), channel_id=1, source_target_pairs={{0,6},{2,4},{4,2},{6,0},{8,14},{10,12},{12,10},{14,8},{1,7},{3,5},... | collective-permute-start | bytes 208904 | tf_op jit(solution)/shard_map/ppermute | solution.py:412
  42.3 6.1 %collective-permute-start.14 = (bf16[1,272,128]{2,1,0:T(8,128)(2,1)S(1)}, bf16[1,272,128]{2,1,0:T(8,128)(2,1)S(1)}, u32[]{:S(2)}, u32[]{:S(2)}) collective-permute-start(bf16[1,272,128]{2,1,0:T(8,128)(2,1)S(1)} %get-tuple-element.80), channel_id=1, source_target_pairs={{0,2},{2,0},{4,6},{6,4},{8,10},{10,8},{12,14},{14,12},{1,3},{3,1},... | collective-permute-start | bytes 208904 | tf_op jit(solution)/shard_map/ppermute | solution.py:412
  43.2 5.2 %collective-permute-start.15 = (bf16[1,272,128]{2,1,0:T(8,128)(2,1)S(1)}, bf16[1,272,128]{2,1,0:T(8,128)(2,1)S(1)}, u32[]{:S(2)}, u32[]{:S(2)}) collective-permute-start(bf16[1,272,128]{2,1,0:T(8,128)(2,1)S(1)} %get-tuple-element.81), channel_id=1, source_target_pairs={{0,8},{2,10},{4,12},{6,14},{8,0},{10,2},{12,4},{14,6},{1,9},{3,11}... | collective-permute-start | bytes 208904 | tf_op jit(solution)/shard_map/ppermute | solution.py:412
  48.4 1.2 %collective-permute-start.16 = (f32[1,128]{1,0:T(1,128)S(1)}, f32[1,128]{1,0:T(1,128)S(1)}, u32[]{:S(2)}, u32[]{:S(2)}) collective-permute-start(f32[1,128]{1,0:T(1,128)S(1)} %shard_map.103), channel_id=1, source_target_pairs={{0,1},{1,0},{2,3},{3,2},{4,5},{5,4},{6,7},{7,6},{8,9},{9,8},{10,11... | collective-permute-start | bytes 1544 | tf_op jit(solution)/shard_map/ppermute | solution.py:558
